TPU v7x, 32 devices: a whole 2x2x4 slice. The times are simulated.
32 devices in a mesh: tp: 8 (over z, y), ep: 4 (over x, core).
Axes of the slice: x: 2, y: 2, z: 4, core: 2. Of those that a mesh axis runs over, the one named last changes fastest.
Arguments:
- attn_out: bfloat16 [4096, 8192], P('ep', 'tp'), may hold values from -6 to 6
- residual: bfloat16 [4096, 7168], P(('ep', 'tp')), may hold values from -6 to 6
- w_out: bfloat16 [8192, 7168], P('tp'), may hold values from -0.0625 to 0.0625
- norm_gain: bfloat16 [7168], replicated, may hold values from 0.5 to 1.5
- router: bfloat16 [7168, 256], P(None, 'tp'), may hold values from -0.0625 to 0.0625
- router_bias: float32 [256], replicated, may hold values from -3 to 3
- choices: int32 [4096, 8], P(('ep', 'tp')), may hold values from 0 to 255, as said below
- w_gate: bfloat16 [8, 7168, 2048], P('tp', None, 'ep'), may hold values from -0.0625 to 0.0625
- w_up: bfloat16 [8, 7168, 2048], P('tp', None, 'ep'), may hold values from -0.0625 to 0.0625
- w_down: bfloat16 [8, 2048, 7168], P('tp', 'ep'), may hold values from -0.125 to 0.125
Outputs:
- hidden_out: bfloat16 [4096, 7168], P(('ep', 'tp'))
- moe_out: bfloat16 [4096, 7168], P(('ep', 'tp'))
- load: float32 [256], replicated
- bias_next: float32 [256], replicated
Inputs may be any that keep to these rules, and one draw needn't show every extreme that they name: `choices`: each row names 8 different experts. Among the rows of one device no expert below 8 is named by more than 2 rows; one such expert is named by exactly 2 rows of every device.
All inputs are finite; a program needn't handle non-finite values.
Results may differ from a plain program's by a relative error of at most 0.034.
Values may be sent and summed in bfloat16 or wider, within the bound.
No kernel may reach another device: no remote copies, remote signals or barrier semaphores. Data moves between devices by JAX's collectives and lax.ppermute only.
A program may use at most 128 MiB of HBM per device.

v0:
```python
import jax
import jax.numpy as jnp
from jax import lax
from jax.sharding import PartitionSpec as P

TOP = 8
CAP = 2


norm_eps = 1e-06
route_scale = 2.5
bias_rate = 0.001


def on_device(
    attn_out, residual, w_out, norm_gain, router, router_bias, choices, w_gate, w_up, w_down
):
    tp_count = lax.axis_size("tp")
    ep_count = lax.axis_size("ep")
    tok_rows = residual.shape[0]
    width = residual.shape[1]
    routed = router_bias.shape[0]
    projected = lax.psum_scatter(
        jnp.dot(attn_out, w_out, preferred_element_type=jnp.float32).astype(jnp.bfloat16),
        "tp",
        scatter_dimension=0,
        tiled=True,
    ).astype(jnp.float32)
    hidden_out = (residual.astype(jnp.float32) + projected).astype(jnp.bfloat16)
    stream = hidden_out.astype(jnp.float32)
    scaled = stream * lax.rsqrt(jnp.mean(stream * stream, axis=-1, keepdims=True) + norm_eps)
    normed = (scaled * norm_gain.astype(jnp.float32)).astype(jnp.bfloat16)
    logits = jnp.dot(
        normed, lax.all_gather(router, "tp", axis=1, tiled=True), preferred_element_type=jnp.float32
    )
    scores = jax.nn.sigmoid(logits)
    onehot = choices[:, :, None] == jnp.arange(routed, dtype=jnp.int32)[None, None, :]
    chosen = jnp.sum(jnp.where(onehot, scores[:, None, :], 0.0), axis=-1)
    weights = route_scale * chosen / jnp.sum(chosen, axis=-1, keepdims=True)
    window = onehot[:, :, :tp_count]
    expert_weight = jnp.sum(jnp.where(window, weights[:, :, None], 0.0), axis=1)
    member = jnp.any(window, axis=1).astype(jnp.int32)
    slot_rank = jnp.cumsum(member, axis=0) - member
    slot_ids = jnp.arange(CAP, dtype=jnp.int32)[None, :, None]
    slot_pick = (member.T[:, None, :] == 1) & (slot_rank.T[:, None, :] == slot_ids)
    outgoing = jnp.einsum(
        "wcr,rd->wcd", slot_pick.astype(jnp.bfloat16), normed, preferred_element_type=jnp.float32
    ).astype(jnp.bfloat16)
    landed = lax.all_to_all(outgoing, "tp", split_axis=0, concat_axis=0, tiled=True)
    arrived = lax.all_gather(landed[:, None], "ep", axis=1, tiled=True)
    group_rows = tp_count * CAP
    picked = arrived
    picked = jnp.swapaxes(picked, 0, 1).reshape(lax.axis_size("ep") * group_rows, width)
    gate_val = jnp.dot(picked, w_gate[0], preferred_element_type=jnp.float32)
    up_val = jnp.dot(picked, w_up[0], preferred_element_type=jnp.float32)
    active = (jax.nn.silu(gate_val) * up_val).astype(jnp.bfloat16)
    summed = lax.psum_scatter(
        jnp.dot(active, w_down[0], preferred_element_type=jnp.float32).astype(jnp.bfloat16),
        "ep",
        scatter_dimension=0,
        tiled=True,
    )
    outbound = summed.reshape(tp_count, CAP, width)
    returned = lax.all_to_all(outbound, "tp", split_axis=0, concat_axis=0, tiled=True)
    coeff = jnp.where(slot_pick, expert_weight.T[:, None, :], 0.0)
    mixed = jnp.einsum(
        "wcr,wcd->rd", coeff, returned.astype(jnp.float32), precision=lax.Precision.HIGHEST
    )
    moe_out = mixed.astype(jnp.bfloat16)
    local_counts = jnp.sum(onehot.astype(jnp.int32), axis=(0, 1))
    counts = lax.psum(local_counts, ("tp", "ep"))
    all_slots = tok_rows * tp_count * ep_count * TOP
    load = counts.astype(jnp.float32) * routed / all_slots
    bias_next = router_bias + bias_rate * jnp.sign(all_slots - counts * routed).astype(jnp.float32)
    return (hidden_out, moe_out, load, bias_next)


def solution(mesh):
    placed = (
        P("ep", "tp"),
        P(("ep", "tp"), None),
        P("tp", None),
        P(),
        P(None, "tp"),
        P(),
        P(("ep", "tp"), None),
        P("tp", None, "ep"),
        P("tp", None, "ep"),
        P("tp", "ep", None),
    )
    return jax.shard_map(
        on_device,
        mesh=mesh,
        in_specs=placed,
        out_specs=(P(("ep", "tp"), None), P(("ep", "tp"), None), P(), P()),
        check_vma=False,
    )
```

profile of v0, /device:TPU:0, one launch (start us, length us, event | category | flops | bytes accessed | tf_op | source)
XLA Modules:
  0.0 393.3 jit_solution(16185060088893172466)
XLA Ops:
  7.2 0.0 copy-start
  7.2 0.0 reduce-scatter.3.cloned.1.call-start
  7.2 1.5 copy-done
  8.8 23.0 %convolution_convert_fusion = bf16[1024,7168]{1,0:T(8,128)(2,1)} fusion(bf16[1024,1024]{1,0:T(8,128)(2,1)S(1)} %copy-done, bf16[1024,7168]{1,0:T(8,128)(2,1)} %param.12), kind=kOutput, calls=%fused_computation | convolution fusion | flops 15039725568 | bytes 31457280 | tf_op jit(solution)/shard_map/dot_general | solution.py:24
  31.7 0.0 copy-start.5
  31.7 0.0 copy-start.4
  31.7 0.0 copy-start.2
  31.7 0.0 reduce-scatter.3.cloned.1.call-update
  31.8 0.0 all-gather.3.cloned.1.call-start
  31.8 0.7 all-gather.3.cloned.1.call-update
  32.5 0.0 reduce-scatter.5.cloned.1.call-start
  32.6 0.0 copy-done.5
  32.6 0.0 copy-done.4
  32.6 0.2 iota_compare_fusion
  32.8 0.1 copy.42
  32.9 0.2 reduce_window_sum.11
  33.2 0.1 copy.43
  33.2 238.0 %reduce-scatter.3.cloned.1.call-done = bf16[128,7168]{1,0:T(8,128)(2,1)} async-done(((bf16[1024,7168]{1,0:T(8,128)(2,1)}), bf16[128,7168]{1,0:T(8,128)(2,1)}) %reduce-scatter.3.cloned.1.call-update) | async-done | bytes 1835024 | tf_op jit(solution)/shard_map/reduce_scatter | solution.py:23
  271.2 0.0 copy-done.2
  271.2 2.2 fusion.6
  273.4 0.0 copy-start.3
  273.5 0.6 convolution_convert_fusion.2
  274.1 0.2 copy.49
  274.3 14.9 %all_to_all.10 = bf16[8,2,7168]{2,1,0:T(2,128)(2,1)S(1)} all-to-all(bf16[8,2,7168]{2,1,0:T(2,128)(2,1)S(1)} %copy.49), channel_id=1, replica_groups=mesh['tp'=8,'ep'=4] {'tp'}, dimensions={0} | all-to-all | bytes 458752 | tf_op jit(solution)/shard_map/all_to_all | solution.py:49
  289.2 9.3 %all-gather = bf16[8,8,7168]{2,0,1:T(8,128)(2,1)S(1)} all-gather(bf16[8,2,7168]{2,0,1:T(8,128)(2,1)S(1)} %copy.50), channel_id=2, replica_groups=mesh['tp'=8,'ep'=4] {'ep'}, dimensions={1}, use_global_device_ids=true | all-gather | bytes 1146880 | tf_op jit(solution)/shard_map/all_gather | solution.py:50
  298.5 0.9 copy.60
  299.5 0.0 copy-done.3
  299.5 0.3 reshape.48
  299.8 4.5 %fusion.4 = f32[64,512]{1,0:T(8,128)S(1)} fusion(bf16[64,7168]{1,0:T(8,128)(2,1)S(1)} %reshape.48, bf16[1,7168,512]{2,1,0:T(8,128)(2,1)} %param.17), kind=kOutput, calls=%fused_computation.8 | convolution fusion | flops 469762048 | bytes 8388608 | tf_op jit(solution)/shard_map/dot_general | solution.py:54
  304.3 0.0 copy-start.6
  304.3 9.3 %convolution_convert_fusion.1 = bf16[64,7168]{1,0:T(8,128)(2,1)} fusion(bf16[1,512,7168]{2,1,0:T(8,128)(2,1)} %param.19, bf16[64,7168]{1,0:T(8,128)(2,1)S(1)} %reshape.48, bf16[1,7168,512]{2,1,0:T(8,128)(2,1)} %param.18, f32[64,512]{1,0:T(8,128)S(1)} %fusion.4), kind=kOutput, calls=%fused_computation.3 | convolution fusion | flops 940179456 | bytes 16646144 | tf_op jit(solution)/shard_map/dot_general | solution.py:58
  313.6 0.0 reduce-scatter.5.cloned.1.call-update
  313.6 0.2 convert_reduce_fusion
  313.8 39.4 %psum.7 = s32[256]{0:T(256)S(1)} all-reduce(s32[256]{0:T(256)S(1)} %convert_reduce_fusion), channel_id=1, replica_groups=mesh['tp'=8,'ep'=4] {'tp','ep'}, use_global_device_ids=true, to_apply=%region_9.10 | all-reduce | flops 256 | bytes 2048 | tf_op jit(solution)/shard_map/psum | solution.py:71
  353.2 0.0 copy-done.6
  353.2 0.6 multiply_add_fusion
  353.8 0.0 all-gather.3.cloned.1.call-done
  353.8 4.0 %fusion.12 = f32[128,256]{1,0:T(8,128)S(1)} fusion(bf16[7168,256]{0,1:T(8,128)(2,1)} %all-gather.3.cloned.1.call-done, bf16[128,7168]{1,0:T(8,128)(2,1)} %copy-done.3, f32[7168]{0:T(1024)S(1)} %convert_element_type.56, f32[128]{0:T(128)S(1)} %add_rsqrt_fusion), kind=kOutput, calls=%fused_computation.22 | convolution fusion | flops 473530368 | bytes 5665280 | tf_op jit(solution)/shard_map/dot_general | solution.py:33
  357.9 0.1 copy.45
  357.9 10.3 %reduce-scatter.5.cloned.1.call-done = bf16[16,7168]{1,0:T(8,128)(2,1)} async-done(((bf16[64,7168]{1,0:T(8,128)(2,1)}), bf16[16,7168]{1,0:T(8,128)(2,1)}) %reduce-scatter.5.cloned.1.call-update) | async-done | bytes 229392 | tf_op jit(solution)/shard_map/reduce_scatter | solution.py:57
  368.2 1.7 reshape.49
  369.9 5.5 %all-to-all-start.1 = ((bf16[8,2,7168]{2,1,0:T(2,128)(2,1)}), bf16[8,2,7168]{2,1,0:T(2,128)(2,1)S(1)}, u32[]{:S(2)}, u32[]{:S(2)}) async-start(bf16[8,2,7168]{2,1,0:T(2,128)(2,1)} %reshape.49), calls=%async_computation.3 | async-start | bytes 458752 | tf_op jit(solution)/shard_map/all_to_all | solution.py:64
  375.4 0.3 select_reduce_fusion.1
  375.7 0.1 copy.54
  375.8 0.1 multiply_divide_fusion
  376.0 7.9 %all-to-all-done.1 = bf16[8,2,7168]{2,1,0:T(2,128)(2,1)S(1)} async-done(((bf16[8,2,7168]{2,1,0:T(2,128)(2,1)}), bf16[8,2,7168]{2,1,0:T(2,128)(2,1)S(1)}, u32[]{:S(2)}, u32[]{:S(2)}) %all-to-all-start.1) | async-done | bytes 229408 | tf_op jit(solution)/shard_map/all_to_all | solution.py:64
  383.9 2.9 fusion
  386.7 0.0 copy-done.1
  (10 shorter events, 0.2 us)
Async XLA Ops:
  7.2 1.6 copy-start
  7.2 264.0 %reduce-scatter.3.cloned.1.call-start = ((), (), s32[]{:S(2)}) async-start(), calls=%async_computation.4 | async-start | bytes 16515072 | tf_op jit(solution)/shard_map/reduce_scatter | solution.py:23
  31.7 0.8 copy-start.5
  31.7 0.9 copy-start.4
  31.7 239.4 %copy-start.2 = (bf16[128,7168]{1,0:T(8,128)(2,1)S(1)}, bf16[128,7168]{1,0:T(8,128)(2,1)}, u32[]{:S(2)}) copy-start(bf16[128,7168]{1,0:T(8,128)(2,1)} %param.11) | copy-start | bytes 5505028
  31.8 322.1 %all-gather.3.cloned.1.call-start = ((), (), s32[]{:S(2)}) async-start(), calls=%async_computation.5 | async-start | bytes 4128768 | tf_op jit(solution)/shard_map/all_gather | solution.py:34
  32.5 335.7 %reduce-scatter.5.cloned.1.call-start = ((), (), s32[]{:S(2)}) async-start(), calls=%async_computation.6 | async-start | bytes 1146880 | tf_op jit(solution)/shard_map/reduce_scatter | solution.py:57
  273.4 26.0 %copy-start.3 = (bf16[128,7168]{1,0:T(8,128)(2,1)}, bf16[128,7168]{1,0:T(8,128)(2,1)S(1)}, u32[]{:S(2)}) copy-start(bf16[128,7168]{1,0:T(8,128)(2,1)S(1)} %get-tuple-element.7) | copy-start | bytes 5505028
  304.3 48.9 %copy-start.6 = (f32[256]{0:T(256)S(1)}, f32[256]{0:T(256)}, u32[]{:S(2)}) copy-start(f32[256]{0:T(256)} %param.15) | copy-start | bytes 3076
  353.2 33.5 %copy-start.1 = (bf16[1024,1024]{1,0:T(8,128)(2,1)S(1)}, bf16[1024,1024]{1,0:T(8,128)(2,1)}, u32[]{:S(2)}) copy-start(bf16[1024,1024]{1,0:T(8,128)(2,1)} %param.10) | copy-start | bytes 6291460
  369.9 13.9 %all-to-all-start.1 = ((bf16[8,2,7168]{2,1,0:T(2,128)(2,1)}), bf16[8,2,7168]{2,1,0:T(2,128)(2,1)S(1)}, u32[]{:S(2)}, u32[]{:S(2)}) async-start(bf16[8,2,7168]{2,1,0:T(2,128)(2,1)} %reshape.49), calls=%async_computation.3 | async-start | bytes 458752 | tf_op jit(solution)/shard_map/all_to_all | solution.py:64
Sparse Core Ops, SparseCore 0:
  31.9 239.2 reduce-scatter.2
  273.4 68.9 all-gather.2
  345.6 22.5 reduce-scatter.4
where the time goes:
time: 394 us; the launch traced here: 393 us
  waiting for transfers between devices  257 us (65%)
  blocking collectives  63.6 us (16%)
  matrix products  44.2 us (11%)
  between operations  13.9 us (4%)
  starting transfers between devices  5.63 us (1%)
  local copies, waits for them, and re-layouts  5.35 us (1%)
    reduce_scatter x1, waiting for transfers between devices, on_device(): lax.psum_scatter(jnp.dot(attn_out, w_out, preferred_element_type=jnp.floa...  238 us
    psum x1, blocking collectives, on_device(): counts = lax.psum(local_counts, ('tp', 'ep'))  39.4 us
    dot_general x1, matrix products, on_device(): jnp.dot(attn_out, w_out, preferred_element_type=jnp.float32)  23 us
    all_to_all x1, blocking collectives, on_device(): lax.all_to_all(outgoing, 'tp', split_axis=0, concat_axis=0, tiled=True)  14.9 us
    reduce_scatter x1, waiting for transfers between devices, on_device(): lax.psum_scatter(jnp.dot(active, w_down[0], preferred_element_type=jnp.fl...  10.3 us
    all_gather x1, blocking collectives, on_device(): arrived = lax.all_gather(landed[:, None], 'ep', axis=1, tiled=True)  9.31 us
    dot_general x1, matrix products, on_device(): jnp.dot(active, w_down[0], preferred_element_type=jnp.float32)  9.3 us
  transfers between devices with their start and end apart: 4, of which 3 were waited for; matrix products, arithmetic and copies ran while one was open for 6% of the time, Pallas kernels for 0%

commit v1 on v0

v1 whole, which is shorter than its diff:
```python
import jax
import jax.numpy as jnp
from jax import lax
from jax.experimental import pallas as pl
from jax.experimental.pallas import tpu as pltpu
from jax.sharding import PartitionSpec as P

TOP = 8
CAP = 2


norm_eps = 1e-06
route_scale = 2.5
bias_rate = 0.001
f32 = jnp.float32
bf16 = jnp.bfloat16


def swap(value, axis, bit):
    size = lax.axis_size(axis)
    return lax.ppermute(value, axis, [(i, i ^ bit) for i in range(size)])


def bits_of(size):
    return [1 << k for k in range(size.bit_length() - 1)]


def halving_order(stages):
    order = [0]
    for bit in reversed(stages):
        order = order + [j | bit for j in order]
    return order


ANY = pl.BlockSpec(memory_space=pl.ANY)


def run(body, grid, ins, outs, marks, aliases=None, scratch=(), mib=16):
    count, skip = len(ins), len(marks)

    def inner(*refs):
        body(*refs[:count], *refs[count + skip :])

    return pl.pallas_call(
        inner,
        grid=grid,
        in_specs=[spec for _, spec in ins] + [ANY] * skip,
        out_specs=[spec for _, spec in outs],
        out_shape=[jax.ShapeDtypeStruct(shape, kind) for (shape, kind), _ in outs],
        input_output_aliases=aliases or {},
        scratch_shapes=list(scratch),
        compiler_params=pltpu.CompilerParams(vmem_limit_bytes=mib * 1024 * 1024),
        cost_estimate=pl.CostEstimate(flops=1, bytes_accessed=1, transcendentals=0),
    )(*[a for a, _ in ins], *marks)


def whole(shape):
    return pl.BlockSpec(shape, lambda i: (0,) * len(shape))


def kept_block(shape):
    return pl.BlockSpec(shape, lambda i: (0,) * len(shape), pipeline_mode=pl.Buffered(1))


def block_of(span, most):
    size = span.stop - span.start
    best = 128
    for n in range(128, most + 1, 128):
        if size % n == 0 and span.start % n == 0:
            best = n
    return best


def gated(value, marks):
    return run(lambda *refs: None, (1,), [(value, ANY)], [((value.shape, value.dtype), ANY)], marks, {0: 0})[0]


def adds(groups, marks):
    rows = groups[0][0][0].shape[0]
    cut = rows // 2
    plain = all(len(group) == 1 for group in groups)
    sizes = {kept.shape[1] for group in groups for kept, _ in group}
    wide = block_of(slice(0, min(sizes)), 640) if plain and len(sizes) == 1 and cut >= 128 else None
    ins, outs = [], []
    for group in groups:
        cols = sum(kept.shape[1] for kept, _ in group)
        for pair in group:
            for value in pair:
                ins.append((value, pl.BlockSpec((rows, wide), lambda i: (0, i)) if wide else whole(value.shape)))
        for kind in (bf16, f32):
            spec = pl.BlockSpec((cut, wide), lambda i: (0, i)) if wide else whole((cut, cols))
            outs.append((((cut, cols), kind), spec))
    counts = [len(group) for group in groups]

    def body(*refs):
        place, out_place = 0, 2 * sum(counts)
        for count in counts:
            out, rest = refs[out_place], refs[out_place + 1]
            low = 0
            for _ in range(count):
                kept, got = refs[place], refs[place + 1]
                size = kept.shape[1]
                out[:, low : low + size] = (kept[cut:].astype(f32) + got[cut:].astype(f32)).astype(bf16)
                rest[:, low : low + size] = kept[:cut].astype(f32) + got[:cut].astype(f32)
                low += size
                place += 2
            out_place += 2

    got = run(body, (min(sizes) // wide if wide else 1,), ins, outs, marks)
    return [(got[2 * n], got[2 * n + 1]) for n in range(len(groups))]


def mm(a, b):
    return jnp.dot(a, b, preferred_element_type=f32)


def mm_t(a, b):
    return lax.dot_general(a, b, (((1,), (1,)), ((), ())), preferred_element_type=f32)


def mm_rows(a, b):
    return lax.dot_general(a, b, (((0,), (0,)), ((), ())), preferred_element_type=f32)


def on_device(
    attn_out, residual, w_out, norm_gain, router, router_bias, choices, w_gate, w_up, w_down
):
    tp_count = lax.axis_size("tp")
    ep_count = lax.axis_size("ep")
    tok_rows = residual.shape[0]
    width = residual.shape[1]
    routed = router_bias.shape[0]
    top = choices.shape[1]
    all_rows = tp_count * tok_rows
    first = CAP * tp_count
    me = lax.axis_index("tp")
    ep_me = lax.axis_index("ep")
    tp_bits, ep_bits = bits_of(tp_count), bits_of(ep_count)
    y_first = list(tp_bits)
    z_first = [tp_bits[1], tp_bits[0]] + tp_bits[2:]
    far = tp_bits[2:]
    stages = {"y": y_first, "z": z_first}
    order = {"y": halving_order(y_first), "z": halving_order(z_first)}
    half = all_rows // 2
    flying, values, hidden = {}, {}, []

    onehot = choices[:, :, None] == jnp.arange(routed, dtype=jnp.int32)
    counts = jnp.sum(onehot.astype(jnp.int32), axis=(0, 1))
    count_hops = list(ep_bits)
    rel = [0]
    for bit in tp_bits[::-1]:
        rel = rel + [j | bit for j in rel]
    per_device = routed // tp_count
    per_part = per_device // ep_count
    part_rows = -(-(per_part + 2) // 16) * 16
    base_digit = 64

    def count_hop():
        nonlocal counts
        counts = counts + swap(counts, "ep", count_hops.pop(0))
        return [counts]

    def router_gather(marks):
        part = lax.dynamic_slice_in_dim(router.T, ep_me * per_part, per_part, axis=0)
        digits = jnp.stack([counts // base_digit, counts % base_digit]).astype(bf16)
        digits = jnp.pad(digits, ((0, part_rows - per_part - 2), (0, width - routed)))
        part = gated(jnp.concatenate([part, digits], axis=0), marks)
        for bit in tp_bits[::-1]:
            part = jnp.concatenate([part, swap(part, "tp", bit)], axis=0)
        return part

    blocks = [
        lax.dynamic_slice_in_dim(attn_out, (me ^ j) * tok_rows, tok_rows, axis=0)
        for j in range(tp_count)
    ]
    halves = []
    for kind in ("y", "z"):
        for part in (slice(0, tp_count // 2), slice(tp_count // 2, tp_count)):
            halves.append(jnp.concatenate([blocks[j] for j in order[kind][part]], axis=0))
    tiles = {"y0": 2, "z0": 2, "y1": 4, "y2": 4, "y3": 5, "z1": 3, "y4": 4, "y5": 2, "z2": 2}
    unit = width // sum(tiles.values())
    spans, lo = {}, 0
    for name, count in tiles.items():
        spans[name] = slice(lo, lo + count * unit)
        lo += count * unit
    partial = {}

    def bulk(names, marks):
        base = spans[names[0]].start // unit
        starts = [spans[name].start // unit - base for name in names]
        outs = []
        for name, low in zip(names, starts):
            top_block = tiles[name] - 1
            spec = pl.BlockSpec(
                (half, unit), lambda i, low=low, top_block=top_block: (0, jnp.clip(i - low, 0, top_block))
            )
            outs += [(((half, tiles[name] * unit), bf16), spec)] * 2

        def body(*refs):
            step = pl.program_id(0)
            w, refs_out = refs[4], refs[5:]
            for n, (name, low) in enumerate(zip(names, starts)):

                @pl.when((step >= low) & (step < low + tiles[name]))
                def _(n=n, name=name):
                    at = 0 if name[0] == "y" else 2
                    refs_out[2 * n][...] = mm(refs[at][...], w[...]).astype(bf16)
                    refs_out[2 * n + 1][...] = mm(refs[at + 1][...], w[...]).astype(bf16)

        got = run(
            body,
            (sum(tiles[name] for name in names),),
            [(rows, kept_block(rows.shape)) for rows in halves]
            + [(w_out, pl.BlockSpec((w_out.shape[0], unit), lambda i: (0, base + i)))],
            outs,
            marks,
            mib=50,
        )
        for n, name in enumerate(names):
            partial[name] = (got[2 * n], got[2 * n + 1])
        return [got[-2]]

    def begin(name, marks=None):
        kept, out = partial.pop(name)
        if marks:
            out = gated(out, marks)
        flying[name] = swap(out, "tp", stages[name[0]][0])
        values[name] = kept

    def second(names, marks):
        parts = adds([[(values.pop(name), flying.pop(name))] for name in names], marks)
        for name, (out, kept) in zip(names, parts):
            flying[name] = swap(out, "tp", stages[name[0]][1])
            values[name] = kept
        return [parts[0][0]]

    def third(names, marks):
        ((out, kept),) = adds([[(values.pop(name), flying.pop(name)) for name in names]], marks)
        flying[names] = swap(out, "tp", far[0])
        values[names] = kept
        return [out]

    def finish(names, marks):
        kept, got = values.pop(names), flying.pop(names)
        for bit in far[1:]:
            ((out, kept),) = adds([[(kept, got)]], marks)
            got = swap(out, "tp", bit)
        span = slice(spans[names[0]].start, spans[names[-1]].stop)
        wide = block_of(span, 1280)
        low = span.start // wide
        here = pl.BlockSpec((tok_rows, wide), lambda i: (0, low + i))
        part = pl.BlockSpec((tok_rows, wide), lambda i: (0, i))

        def body(kept, got, residual, *refs):
            refs[-2][...] = (residual[...].astype(f32) + (kept[...] + got[...].astype(f32))).astype(bf16)
            refs[-1][...] = jnp.zeros((8, 128), f32)

        before = [(hidden.pop(), ANY)] if hidden else []
        out, mark = run(
            body,
            ((span.stop - span.start) // wide,),
            [(kept, part), (got, part), (residual, here)] + before,
            [(((tok_rows, width), bf16), here), (((8, 128), f32), whole((8, 128)))],
            marks,
            {3: 0} if before else None,
        )
        hidden.append(out)
        return [mark]

    marks = bulk(("y0", "z0"), [])
    begin("y0")
    begin("z0")
    marks = bulk(("y1",), marks)
    marks = second(("y0", "z0"), marks)
    begin("y1", marks)
    marks = bulk(("y2",), marks)
    marks = second(("y1",), marks + count_hop())
    begin("y2", marks)
    marks = third(("y0", "z0"), marks)
    marks = bulk(("y3", "z1"), marks)
    begin("y3")
    marks = third(("y1",), marks)
    begin("z1", marks)
    marks = finish(("y0", "z0"), marks + count_hop())
    marks = second(("y2",), marks)
    marks = bulk(("y4",), marks)
    begin("y4")
    marks = finish(("y1",), marks)
    marks = second(("z1",), marks)
    marks = third(("y2",), marks)
    marks = second(("y3",), marks)
    marks = bulk(("y5", "z2"), marks)
    begin("y5")
    begin("z2")
    marks = finish(("y2",), marks)
    marks = third(("y3",), marks)
    marks = second(("y4",), marks)
    marks = third(("z1",), marks)
    marks = finish(("y3",), marks)
    marks = second(("z2",), marks)
    marks = third(("y4",), marks)
    marks = second(("y5",), marks)
    marks = finish(("z1",), marks)
    router_all = router_gather(marks)
    marks = finish(("y4",), marks)
    marks = third(("y5", "z2"), marks)
    finish(("y5", "z2"), marks)
    (hidden_out,) = hidden

    window = onehot[:, :, :tp_count]
    member = jnp.any(window, axis=1).astype(jnp.int32)
    slot_rank = jnp.cumsum(member, axis=0) - member
    slot_ids = jnp.arange(CAP, dtype=jnp.int32)[None, :, None]
    slot_pick = (member.T[:, None, :] == 1) & (slot_rank.T[:, None, :] == slot_ids)
    pick = slot_pick.reshape(first, tok_rows).astype(bf16)

    lanes = 128
    choice_cols = jnp.pad(choices.astype(bf16), ((0, 0), (0, lanes - top)))

    def norm_body(pick, rows, gain, choice, out):
        stream = mm(pick[...], rows[...])
        scaled = stream * lax.rsqrt(jnp.mean(stream * stream, axis=-1, keepdims=True) + norm_eps)
        out[:, :width] = (scaled * gain[...].astype(f32)).astype(bf16)
        out[:, width:] = mm(pick[...], choice[...]).astype(bf16)

    (normed,) = run(
        norm_body,
        (1,),
        [
            (pick, whole(pick.shape)),
            (hidden_out, whole(hidden_out.shape)),
            (norm_gain[None], whole((1, width))),
            (choice_cols, whole(choice_cols.shape)),
        ],
        [(((first, width + lanes), bf16), whole((first, width + lanes)))],
        [],
    )
    landed = lax.all_to_all(
        normed.reshape(tp_count, CAP, width + lanes), "tp", split_axis=0, concat_axis=0, tiled=True
    ).reshape(first, width + lanes)
    picked = [landed]
    for bit in ep_bits[::-1]:
        picked = picked + [swap(rows, "ep", bit) for rows in picked]
    rows_all = first * ep_count
    hid = w_gate.shape[2]
    deep = block_of(slice(0, width), 1024)
    last_step = width // deep - 1

    def up_body(*refs):
        rows, (gate_w, up_w, out, gate_sum, up_sum) = refs[:ep_count], refs[ep_count:]
        step = pl.program_id(0)

        @pl.when(step == 0)
        def _():
            gate_sum[...] = jnp.zeros_like(gate_sum)
            up_sum[...] = jnp.zeros_like(up_sum)

        x = jnp.concatenate([r[...] for r in rows], axis=0)
        gate_sum[...] += mm(x, gate_w[0])
        up_sum[...] += mm(x, up_w[0])

        @pl.when(step == last_step)
        def _():
            gate = gate_sum[...]
            out[...] = (gate / (1.0 + jnp.exp(-gate)) * up_sum[...]).astype(bf16)

    deep_rows = pl.BlockSpec((first, deep), lambda i: (0, i))
    deep_w = pl.BlockSpec((1, deep, hid), lambda i: (0, i, 0))
    (active,) = run(
        up_body,
        (last_step + 1,),
        [(rows, deep_rows) for rows in picked] + [(w_gate, deep_w), (w_up, deep_w)],
        [(((rows_all, hid), bf16), whole((rows_all, hid)))],
        [],
        scratch=[pltpu.VMEM((rows_all, hid), f32)] * 2,
    )
    cut = rows_all // 2

    def down_body(x, w, out, kept):
        value = mm(x[...], w[0])
        kept[...] = value[:cut]
        out[...] = value[cut:].astype(bf16)

    wide_half = pl.BlockSpec((cut, deep), lambda i: (0, i))
    out, kept = run(
        down_body,
        (last_step + 1,),
        [(active, whole(active.shape)), (w_down, pl.BlockSpec((1, hid, deep), lambda i: (0, 0, i)))],
        [(((cut, width), bf16), wide_half), (((cut, width), f32), wide_half)],
        [],
    )
    got = swap(out, "ep", ep_bits[0])

    row_of = jnp.arange(part_rows, dtype=jnp.int32)
    column_ids = (jnp.array(rel, jnp.int32) ^ me)[:, None] * per_device + ep_me * per_part + row_of
    column_ids = jnp.where(row_of < per_part, column_ids, -1).reshape(1, -1)

    def score_body(*refs):
        rows, (table, columns, expert, out) = refs[:ep_count], refs[ep_count:]
        x = jnp.concatenate([r[:, :width] for r in rows], axis=0)
        ids = jnp.concatenate([r[:, width:] for r in rows], axis=0).astype(f32).astype(jnp.int32)
        scores = 1.0 / (1.0 + jnp.exp(-mm_t(x, table[...])))
        here = columns[...]
        chosen = jnp.where(here == expert[...], scores, 0.0)
        total = jnp.zeros_like(scores)
        for k in range(top):
            total += jnp.where(here == ids[:, k : k + 1], scores, 0.0)
        lane = lax.broadcasted_iota(jnp.int32, out.shape, 1)
        chosen = jnp.sum(chosen, axis=-1, keepdims=True)
        total = jnp.sum(total, axis=-1, keepdims=True)
        out[...] = jnp.where(lane == 0, chosen, jnp.where(lane == 1, total, 0.0))

    expert_id = jnp.full((1, 1), me, jnp.int32)
    (parts,) = run(
        score_body,
        (1,),
        [(rows, whole(rows.shape)) for rows in picked]
        + [
            (router_all, whole(router_all.shape)),
            (column_ids, whole(column_ids.shape)),
            (expert_id, whole((1, 1))),
        ],
        [(((rows_all, lanes), f32), whole((rows_all, lanes)))],
        [],
    )
    for bit in ep_bits:
        low = parts.shape[0] // 2
        parts = parts[:low] + swap(parts[low:], "ep", bit)
    for bit in ep_bits[1:]:
        ((out, kept),) = adds([[(kept, got)]], [])
        got = swap(out, "ep", bit)

    def weigh_body(kept, got, part, out):
        value = (kept[...] + got[...].astype(f32)).astype(bf16).astype(f32)
        out[...] = (value * (route_scale * part[:, 0:1] / part[:, 1:2])).astype(bf16)

    (summed,) = run(
        weigh_body,
        (1,),
        [(kept, whole(kept.shape)), (got, whole(kept.shape)), (parts, whole(parts.shape))],
        [((kept.shape, bf16), whole(kept.shape))],
        [],
    )
    returned = lax.all_to_all(
        summed.reshape(tp_count, CAP, width), "tp", split_axis=0, concat_axis=0, tiled=True
    ).reshape(first, width)
    moe_out = mm_rows(pick, returned).astype(bf16)

    digits = router_all.reshape(tp_count, part_rows, width)[:, per_part : per_part + 2, :routed]
    digits = jnp.sum(digits.astype(jnp.int32), axis=0)
    counts = digits[0] * base_digit + digits[1]
    all_slots = all_rows * ep_count * top
    load = counts.astype(f32) * routed / all_slots
    bias_next = router_bias + bias_rate * jnp.sign(all_slots - counts * routed).astype(f32)
    return (hidden_out, moe_out, load, bias_next)


def solution(mesh):
    placed = (
        P("ep", "tp"),
        P(("ep", "tp"), None),
        P("tp", None),
        P(),
        P(None, "tp"),
        P(),
        P(("ep", "tp"), None),
        P("tp", None, "ep"),
        P("tp", None, "ep"),
        P("tp", "ep", None),
    )
    return jax.shard_map(
        on_device,
        mesh=mesh,
        in_specs=placed,
        out_specs=(P(("ep", "tp"), None), P(("ep", "tp"), None), P(), P()),
        check_vma=False,
    )
```

time: 394 us -> 310 us (0.79)
  waiting for transfers between devices: 257 us -> 159 us
  Pallas kernels: 0 us -> 68.5 us
  blocking collectives: 63.6 us -> 0 us
  matrix products: 44.2 us -> 1.91 us
  starting transfers between devices: 5.63 us -> 47.1 us
  local copies, waits for them, and re-layouts: 5.35 us -> 23.6 us
  between operations: 13.9 us -> 1.21 us
  other arithmetic: 3.77 us -> 7.88 us
    reduce_scatter x2 -> x0, waiting for transfers between devices: 248 us -> none  [the longest x1 238 us: on_device(): lax.psum_scatter(jnp.dot(attn_out, w_out, preferred_element_type=jnp.floa...]
    ppermute x0 -> x37, waiting for transfers between devices: none -> 146 us  [swap(): return lax.ppermute(value, axis, [(i, i ^ bit) for i in range(size)])]
    pallas_call x0 -> x38, Pallas kernels: none -> 68.5 us  [run(): pl.pallas_call(inner, grid=grid, in_specs=[spec for _, spec in ins] + [AN...]
    dot_general x6 -> x1, matrix products: 44.2 us -> 1.91 us  [mm_rows(): lax.dot_general(a, b, (((0,), (0,)), ((), ())), preferred_element_type=f32)]
    psum x1 -> x0, blocking collectives: 39.4 us -> none  [on_device(): counts = lax.psum(local_counts, ('tp', 'ep'))]
    ppermute x0 -> x37, starting transfers between devices: none -> 38.9 us  [swap(): return lax.ppermute(value, axis, [(i, i ^ bit) for i in range(size)])]
    unnamed x15 -> x58, local copies, waits for them, and re-layouts: 1.67 us -> 19.5 us
    all_to_all x1 -> x0, blocking collectives: 14.9 us -> none  [on_device(): lax.all_to_all(outgoing, 'tp', split_axis=0, concat_axis=0, tiled=True)]
  transfers between devices with their start and end apart: 4 -> 39, of which waited for: 3 -> 24; matrix products, arithmetic and copies ran while one was open for 6% -> 2% of each run, Pallas kernels for 0% -> 20%
where the time goes in v1:
time: 310 us; the launch traced here: 309 us
  waiting for transfers between devices  159 us (51%)
  Pallas kernels  68.5 us (22%)
  starting transfers between devices  47.1 us (15%)
  local copies, waits for them, and re-layouts  23.6 us (8%)
  other arithmetic  7.88 us (3%)
    ppermute x37, waiting for transfers between devices, swap(): return lax.ppermute(value, axis, [(i, i ^ bit) for i in range(size)])  146 us
    pallas_call x38, Pallas kernels, run(): pl.pallas_call(inner, grid=grid, in_specs=[spec for _, spec in ins] + [AN...  68.5 us
    ppermute x37, starting transfers between devices, swap(): return lax.ppermute(value, axis, [(i, i ^ bit) for i in range(size)])  38.9 us
    unnamed x58, local copies, waits for them, and re-layouts  19.5 us
    all_to_all x1, waiting for transfers between devices, on_device(): lax.all_to_all(summed.reshape(tp_count, CAP, width), 'tp', split_axis=0,...  6.86 us
  transfers between devices with their start and end apart: 39, of which 24 were waited for; matrix products, arithmetic and copies ran while one was open for 2% of the time, Pallas kernels for 20%

profile of v1, /device:TPU:0, one launch (start us, length us, event | category | flops | bytes accessed | tf_op | source)
XLA Modules:
  0.0 308.8 jit_solution(9255834078085137180)
XLA Ops:
  0.7 1.8 constant_dynamic-slice_fusion.3
  2.5 1.8 pad_maximum_fusion.1
  4.3 5.5 %shard_map.138 = (bf16[512,512]{1,0:T(8,128)(2,1)S(1)}, bf16[512,512]{1,0:T(8,128)(2,1)S(1)}, bf16[512,512]{1,0:T(8,128)(2,1)S(1)}, bf16[512,512]{1,0:T(8,128)(2,1)S(1)}) custom-call(bf16[512,1024]{1,0:T(8,128)(2,1)S(1)} %get-tuple-element.151.refs_0_, bf16[512,1024]{1,0:T(8,128)(2,1)} %get-tuple-element.153.refs_1_, ...), custom_call_target="tpu_custom_call" | custom-call | flops 1 | bytes 1 | tf_op jit(solution)/shard_map/pallas_call | solution.py:44
  9.9 3.0 collective-permute-start
  14.5 5.5 %shard_map.139 = (bf16[512,1024]{1,0:T(8,128)(2,1)S(1)}, bf16[512,1024]{1,0:T(8,128)(2,1)S(1)}) custom-call(bf16[512,1024]{1,0:T(8,128)(2,1)S(1)} %get-tuple-element.151.refs_0_, bf16[512,1024]{1,0:T(8,128)(2,1)} %get-tuple-element.153.refs_1_, bf16[512,1024]{1,0:T(8,128)(2,1)} %get-tuple-element.152.refs_2_, bf16[512,1024]{1,0:T(8,128)(2,1)} %get-tuple-element.150.refs_3_, ...), custom_call_target="tpu_custom_call" | custom-call | flops 1 | bytes 1 | tf_op jit(solution)/shard_map/pallas_call | solution.py:44
  20.0 4.8 %collective-permute-done.refs_1_ = bf16[512,512]{1,0:T(8,128)(2,1)S(1)} collective-permute-done((bf16[512,512]{1,0:T(8,128)(2,1)S(1)}, bf16[512,512]{1,0:T(8,128)(2,1)S(1)}, u32[]{:S(2)}, u32[]{:S(2)}) %collective-permute-start) | collective-permute-done | bytes 524320 | tf_op jit(solution)/shard_map/ppermute | solution.py:21
  28.4 6.2 %shard_map.142 = (bf16[512,1024]{1,0:T(8,128)(2,1)S(1)}, bf16[512,1024]{1,0:T(8,128)(2,1)}) custom-call(bf16[512,1024]{1,0:T(8,128)(2,1)S(1)} %get-tuple-element.151.refs_0_, bf16[512,1024]{1,0:T(8,128)(2,1)} %get-tuple-element.153.refs_1_, bf16[512,1024]{1,0:T(8,128)(2,1)} %get-tuple-element.152.refs_2_, bf16[512,1024]{1,0:T(8,128)(2,1)} %get-tuple-element.150.refs_3_, ...), custom_call_target="tpu_custom_call" | custom-call | flops 1 | bytes 1 | tf_op jit(solution)/shard_map/pallas_call | solution.py:44
  34.6 15.7 %collective-permute-done.4.refs_1_ = bf16[512,1024]{1,0:T(8,128)(2,1)S(1)} collective-permute-done((bf16[512,1024]{1,0:T(8,128)(2,1)S(1)}, bf16[512,1024]{1,0:T(8,128)(2,1)S(1)}, u32[]{:S(2)}, u32[]{:S(2)}) %collective-permute-start.4) | collective-permute-done | bytes 1048608 | tf_op jit(solution)/shard_map/ppermute | solution.py:21
  55.9 5.9 %collective-permute-done.2.refs_1_ = bf16[256,512]{1,0:T(8,128)(2,1)S(1)} collective-permute-done((bf16[256,512]{1,0:T(8,128)(2,1)S(1)}, bf16[256,512]{1,0:T(8,128)(2,1)S(1)}, u32[]{:S(2)}, u32[]{:S(2)}) %collective-permute-start.2) | collective-permute-done | bytes 262176 | tf_op jit(solution)/shard_map/ppermute | solution.py:21
  61.7 18.7 %collective-permute-done.3.refs_3_ = bf16[256,512]{1,0:T(8,128)(2,1)S(1)} collective-permute-done((bf16[256,512]{1,0:T(8,128)(2,1)S(1)}, bf16[256,512]{1,0:T(8,128)(2,1)S(1)}, u32[]{:S(2)}, u32[]{:S(2)}) %collective-permute-start.3) | collective-permute-done | bytes 262176 | tf_op jit(solution)/shard_map/ppermute | solution.py:21
  82.0 10.0 %shard_map.145 = (bf16[512,1280]{1,0:T(8,128)(2,1)}, bf16[512,1280]{1,0:T(8,128)(2,1)}, bf16[512,768]{1,0:T(8,128)(2,1)S(1)}, bf16[512,768]{1,0:T(8,128)(2,1)}) custom-call(bf16[512,1024]{1,0:T(8,128)(2,1)S(1)} %get-tuple-element.151.refs_0_, bf16[512,1024]{1,0:T(8,128)(2,1)S(1)} %copy-done.4, bf16[512,1024]{1,0:T(8,128)(2,1)} %get-tuple-element.152.refs_2_, ...), custom_call_target="tpu_custom_call" | custom-call | flops 1 | bytes 1 | tf_op jit(solution)/shard_map/pallas_call | solution.py:44
  93.9 2.3 collective-permute-start.8
  97.7 2.1 collective-permute-done.10
  105.5 5.5 %collective-permute-done.8.refs_1_ = bf16[128,1024]{1,0:T(8,128)(2,1)} collective-permute-done((bf16[128,1024]{1,0:T(8,128)(2,1)}, bf16[128,1024]{1,0:T(8,128)(2,1)}, u32[]{:S(2)}, u32[]{:S(2)}) %collective-permute-start.8) | collective-permute-done | bytes 262176 | tf_op jit(solution)/shard_map/ppermute | solution.py:21
  111.0 1.7 shard_map.148
  114.2 2.4 collective-permute-start.11
  116.6 6.2 %shard_map.151 = (bf16[512,1024]{1,0:T(8,128)(2,1)S(1)}, bf16[512,1024]{1,0:T(8,128)(2,1)}) custom-call(bf16[512,1024]{1,0:T(8,128)(2,1)S(1)} %get-tuple-element.151.refs_0_, bf16[512,1024]{1,0:T(8,128)(2,1)} %get-tuple-element.153.refs_1_, bf16[512,1024]{1,0:T(8,128)(2,1)} %get-tuple-element.152.refs_2_, bf16[512,1024]{1,0:T(8,128)(2,1)} %get-tuple-element.150.refs_3_, ...), custom_call_target="tpu_custom_call" | custom-call | flops 1 | bytes 1 | tf_op jit(solution)/shard_map/pallas_call | solution.py:44
  125.1 6.3 %collective-permute-done.12.refs_1_ = bf16[512,768]{1,0:T(8,128)(2,1)S(1)} collective-permute-done((bf16[512,768]{1,0:T(8,128)(2,1)}, bf16[512,768]{1,0:T(8,128)(2,1)S(1)}, u32[]{:S(2)}, u32[]{:S(2)}) %collective-permute-start.12) | collective-permute-done | bytes 786464 | tf_op jit(solution)/shard_map/ppermute | solution.py:21
  132.6 6.9 %collective-permute-done.11.refs_1_ = bf16[256,1024]{1,0:T(8,128)(2,1)S(1)} collective-permute-done((bf16[256,1024]{1,0:T(8,128)(2,1)S(1)}, bf16[256,1024]{1,0:T(8,128)(2,1)S(1)}, u32[]{:S(2)}, u32[]{:S(2)}) %collective-permute-start.11) | collective-permute-done | bytes 524320 | tf_op jit(solution)/shard_map/ppermute | solution.py:21
  139.8 1.8 collective-permute-start.17
  143.2 2.5 collective-permute-start.16
  145.8 6.2 %shard_map.156 = (bf16[512,512]{1,0:T(8,128)(2,1)S(1)}, bf16[512,512]{1,0:T(8,128)(2,1)S(1)}, bf16[512,512]{1,0:T(8,128)(2,1)S(1)}, bf16[512,512]{1,0:T(8,128)(2,1)}) custom-call(bf16[512,1024]{1,0:T(8,128)(2,1)S(1)} %get-tuple-element.151.refs_0_, bf16[512,1024]{1,0:T(8,128)(2,1)} %get-tuple-element.153.refs_1_, ...), custom_call_target="tpu_custom_call" | custom-call | flops 1 | bytes 1 | tf_op jit(solution)/shard_map/pallas_call | solution.py:44
  153.9 14.7 %collective-permute-done.16.refs_1_ = bf16[256,1280]{1,0:T(8,128)(2,1)S(1)} collective-permute-done((bf16[256,1280]{1,0:T(8,128)(2,1)S(1)}, bf16[256,1280]{1,0:T(8,128)(2,1)S(1)}, u32[]{:S(2)}, u32[]{:S(2)}) %collective-permute-start.16) | collective-permute-done | bytes 655392 | tf_op jit(solution)/shard_map/ppermute | solution.py:21
  170.1 3.0 collective-permute-start.25
  173.1 7.6 %collective-permute-done.20.refs_1_ = bf16[128,1280]{1,0:T(8,128)(2,1)S(1)} collective-permute-done((bf16[128,1280]{1,0:T(8,128)(2,1)S(1)}, bf16[128,1280]{1,0:T(8,128)(2,1)S(1)}, u32[]{:S(2)}, u32[]{:S(2)}) %collective-permute-start.20) | collective-permute-done | bytes 327712 | tf_op jit(solution)/shard_map/ppermute | solution.py:21
  180.6 2.1 shard_map.161
  182.7 3.9 %collective-permute-done.19.refs_1_ = bf16[512,512]{1,0:T(8,128)(2,1)S(1)} collective-permute-done((bf16[512,512]{1,0:T(8,128)(2,1)}, bf16[512,512]{1,0:T(8,128)(2,1)S(1)}, u32[]{:S(2)}, u32[]{:S(2)}) %collective-permute-start.19) | collective-permute-done | bytes 524320 | tf_op jit(solution)/shard_map/ppermute | solution.py:21
  186.7 9.0 %collective-permute-done.18.refs_1_ = bf16[256,1024]{1,0:T(8,128)(2,1)S(1)} collective-permute-done((bf16[256,1024]{1,0:T(8,128)(2,1)S(1)}, bf16[256,1024]{1,0:T(8,128)(2,1)S(1)}, u32[]{:S(2)}, u32[]{:S(2)}) %collective-permute-start.18) | collective-permute-done | bytes 524320 | tf_op jit(solution)/shard_map/ppermute | solution.py:21
  200.2 2.5 collective-permute-start.22
  202.7 10.0 %collective-permute-done.32 = bf16[16,7168]{1,0:T(8,128)(2,1)} collective-permute-done((bf16[16,7168]{1,0:T(8,128)(2,1)S(1)}, bf16[16,7168]{1,0:T(8,128)(2,1)}, u32[]{:S(2)}, u32[]{:S(2)}) %collective-permute-start.32) | collective-permute-done | bytes 229408 | tf_op jit(solution)/shard_map/ppermute | solution.py:21
  212.7 1.8 pad_maximum_fusion.9
  214.6 6.3 %collective-permute-done.24.refs_1_ = bf16[128,1024]{1,0:T(8,128)(2,1)} collective-permute-done((bf16[128,1024]{1,0:T(8,128)(2,1)}, bf16[128,1024]{1,0:T(8,128)(2,1)}, u32[]{:S(2)}, u32[]{:S(2)}) %collective-permute-start.24) | collective-permute-done | bytes 262176 | tf_op jit(solution)/shard_map/ppermute | solution.py:21
  222.0 1.7 shard_map.166
  223.8 1.8 shard_map.167
  226.9 12.5 %collective-permute-done.26.refs_1_ = bf16[128,1024]{1,0:T(8,128)(2,1)S(1)} collective-permute-done((bf16[128,1024]{1,0:T(8,128)(2,1)}, bf16[128,1024]{1,0:T(8,128)(2,1)S(1)}, u32[]{:S(2)}, u32[]{:S(2)}) %collective-permute-start.26) | collective-permute-done | bytes 262176 | tf_op jit(solution)/shard_map/ppermute | solution.py:21
  244.1 3.8 %all-to-all-start = ((bf16[8,2,7296]{2,1,0:T(2,128)(2,1)}), bf16[8,2,7296]{2,1,0:T(2,128)(2,1)S(1)}, u32[]{:S(2)}, u32[]{:S(2)}) async-start(bf16[8,2,7296]{2,1,0:T(2,128)(2,1)} %reshape.79), calls=%async_computation | async-start | bytes 466944 | tf_op jit(solution)/shard_map/all_to_all | solution.py:338
  249.0 2.1 collective-permute-start.34
  251.1 5.6 %all-to-all-done = bf16[8,2,7296]{2,1,0:T(2,128)(2,1)S(1)} async-done(((bf16[8,2,7296]{2,1,0:T(2,128)(2,1)}), bf16[8,2,7296]{2,1,0:T(2,128)(2,1)S(1)}, u32[]{:S(2)}, u32[]{:S(2)}) %all-to-all-start) | async-done | bytes 233504 | tf_op jit(solution)/shard_map/all_to_all | solution.py:338
  257.9 5.0 %collective-permute-done.27.refs_1_ = bf16[16,7296]{1,0:T(8,128)(2,1)S(1)} collective-permute-done((bf16[16,7296]{1,0:T(8,128)(2,1)S(1)}, bf16[16,7296]{1,0:T(8,128)(2,1)S(1)}, u32[]{:S(2)}, u32[]{:S(2)}) %collective-permute-start.27) | collective-permute-done | bytes 233504 | tf_op jit(solution)/shard_map/ppermute | solution.py:21
  264.4 3.1 copy-done.5
  267.5 3.1 copy-done.6
  270.6 4.8 %shard_map.170.refs_0_ = bf16[64,512]{1,0:T(8,128)(2,1)S(1)} custom-call(bf16[16,7296]{1,0:T(8,128)(2,1)S(1)} %reshape.80.refs_0_, bf16[16,7296]{1,0:T(8,128)(2,1)S(1)} %collective-permute-done.27.refs_1_, bf16[16,7296]{1,0:T(8,128)(2,1)S(1)} %collective-permute-done.28.refs_2_, bf16[16,7296]{1,0:T(8,128)(2,1)S(1)} %collective-permute-done.29.refs_3_, ...), custom_call_target="tpu_custom_call" | custom-call | flops 1 | bytes 1 | tf_op jit(solution)/shard_map/pallas_call | solution.py:44
  275.3 3.1 copy-done.7
  278.4 2.8 shard_map.171
  288.4 5.1 %collective-permute-done.31.refs_1_ = bf16[16,7168]{1,0:T(8,128)(2,1)S(1)} collective-permute-done((bf16[16,7168]{1,0:T(8,128)(2,1)S(1)}, bf16[16,7168]{1,0:T(8,128)(2,1)S(1)}, u32[]{:S(2)}, u32[]{:S(2)}) %collective-permute-start.31) | collective-permute-done | bytes 229408 | tf_op jit(solution)/shard_map/ppermute | solution.py:21
  294.5 4.4 %all-to-all-start.1 = ((bf16[8,2,7168]{2,1,0:T(2,128)(2,1)}), bf16[8,2,7168]{2,1,0:T(2,128)(2,1)S(1)}, u32[]{:S(2)}, u32[]{:S(2)}) async-start(bf16[8,2,7168]{2,1,0:T(2,128)(2,1)} %reshape.81), calls=%async_computation.1 | async-start | bytes 458752 | tf_op jit(solution)/shard_map/all_to_all | solution.py:444
  300.0 6.9 %all-to-all-done.1 = bf16[8,2,7168]{2,1,0:T(2,128)(2,1)S(1)} async-done(((bf16[8,2,7168]{2,1,0:T(2,128)(2,1)}), bf16[8,2,7168]{2,1,0:T(2,128)(2,1)S(1)}, u32[]{:S(2)}, u32[]{:S(2)}) %all-to-all-start.1) | async-done | bytes 229408 | tf_op jit(solution)/shard_map/all_to_all | solution.py:444
  306.9 1.9 fusion
  (175 shorter events, 56.1 us)
Async XLA Ops:
  0.6 123.6 %copy-start = (bf16[7168,32]{0,1:T(8,128)(2,1)S(1)}, bf16[7168,32]{0,1:T(8,128)(2,1)}, u32[]{:S(2)}) copy-start(bf16[7168,32]{0,1:T(8,128)(2,1)} %param.15) | copy-start | bytes 1376260
  9.9 15.0 %collective-permute-start = (bf16[512,512]{1,0:T(8,128)(2,1)S(1)}, bf16[512,512]{1,0:T(8,128)(2,1)S(1)}, u32[]{:S(2)}, u32[]{:S(2)}) collective-permute-start(bf16[512,512]{1,0:T(8,128)(2,1)S(1)} %get-tuple-element.72), channel_id=1, source_target_pairs={{0,4},{4,0},{8,12},{12,8},{16,20},{20,16},{24,28},{28,24},{1,5},{5... | collective-permute-start | bytes 1572872 | tf_op jit(solution)/shard_map/ppermute | solution.py:21
  12.9 13.4 %collective-permute-start.1 = (bf16[512,512]{1,0:T(8,128)(2,1)S(1)}, bf16[512,512]{1,0:T(8,128)(2,1)S(1)}, u32[]{:S(2)}, u32[]{:S(2)}) collective-permute-start(bf16[512,512]{1,0:T(8,128)(2,1)S(1)} %get-tuple-element.74), channel_id=1, source_target_pairs={{0,8},{4,12},{8,0},{12,4},{16,24},{20,28},{24,16},{28,20},{1,9},{5... | collective-permute-start | bytes 1572872 | tf_op jit(solution)/shard_map/ppermute | solution.py:21
  26.5 23.8 %collective-permute-start.4 = (bf16[512,1024]{1,0:T(8,128)(2,1)S(1)}, bf16[512,1024]{1,0:T(8,128)(2,1)S(1)}, u32[]{:S(2)}, u32[]{:S(2)}) collective-permute-start(bf16[512,1024]{1,0:T(8,128)(2,1)S(1)} %shard_map.141), channel_id=1, source_target_pairs={{0,4},{4,0},{8,12},{12,8},{16,20},{20,16},{24,28},{28,24},{1,5},{5... | collective-permute-start | bytes 3145736 | tf_op jit(solution)/shard_map/ppermute | solution.py:21
  27.2 1.2 collective-permute-start.5
  34.6 17.2 %copy-start.8 = (bf16[512,1024]{1,0:T(8,128)(2,1)}, bf16[512,1024]{1,0:T(8,128)(2,1)S(1)}, u32[]{:S(2)}) copy-start(bf16[512,1024]{1,0:T(8,128)(2,1)S(1)} %get-tuple-element.81.refs_2_.refs_0_) | copy-start | bytes 3145732
  51.8 30.2 %copy-start.4 = (bf16[512,1024]{1,0:T(8,128)(2,1)S(1)}, bf16[512,1024]{1,0:T(8,128)(2,1)}, u32[]{:S(2)}) copy-start(bf16[512,1024]{1,0:T(8,128)(2,1)} %get-tuple-element.153.refs_1_) | copy-start | bytes 3145732
  51.8 60.9 %collective-permute-start.7 = (bf16[512,1024]{1,0:T(8,128)(2,1)}, bf16[512,1024]{1,0:T(8,128)(2,1)}, u32[]{:S(2)}, u32[]{:S(2)}) collective-permute-start(bf16[512,1024]{1,0:T(8,128)(2,1)} %shard_map.146), channel_id=1, source_target_pairs={{0,4},{4,0},{8,12},{12,8},{16,20},{20,16},{24,28},{28,24},{1,5},{5... | collective-permute-start | bytes 3145736 | tf_op jit(solution)/shard_map/ppermute | solution.py:21
  52.5 9.2 %collective-permute-start.2 = (bf16[256,512]{1,0:T(8,128)(2,1)S(1)}, bf16[256,512]{1,0:T(8,128)(2,1)S(1)}, u32[]{:S(2)}, u32[]{:S(2)}) collective-permute-start(bf16[256,512]{1,0:T(8,128)(2,1)S(1)} %get-tuple-element.77.refs_1_.refs_5_), channel_id=1, source_target_pairs={{0,8},{4,12},{8,0},{12,4},{16,24},{20,28},{24,16},{28,20},{1,9},{5... | collective-permute-start | bytes 786440 | tf_op jit(solution)/shard_map/ppermute | solution.py:21
  54.0 26.4 %collective-permute-start.3 = (bf16[256,512]{1,0:T(8,128)(2,1)S(1)}, bf16[256,512]{1,0:T(8,128)(2,1)S(1)}, u32[]{:S(2)}, u32[]{:S(2)}) collective-permute-start(bf16[256,512]{1,0:T(8,128)(2,1)S(1)} %get-tuple-element.79), channel_id=1, source_target_pairs={{0,4},{4,0},{8,12},{12,8},{16,20},{20,16},{24,28},{28,24},{1,5},{5... | collective-permute-start | bytes 786440 | tf_op jit(solution)/shard_map/ppermute | solution.py:21
  55.4 44.4 %collective-permute-start.9 = (bf16[256,1024]{1,0:T(8,128)(2,1)S(1)}, bf16[256,1024]{1,0:T(8,128)(2,1)}, u32[]{:S(2)}, u32[]{:S(2)}) collective-permute-start(bf16[256,1024]{1,0:T(8,128)(2,1)S(1)} %get-tuple-element.82.refs_4_.refs_1_), channel_id=1, source_target_pairs={{0,8},{4,12},{8,0},{12,4},{16,24},{20,28},{24,16},{28,20},{1,9},{5... | collective-permute-start | bytes 1572872 | tf_op jit(solution)/shard_map/ppermute | solution.py:21
  92.9 48.6 %collective-permute-start.6 = (bf16[512,1280]{1,0:T(8,128)(2,1)}, bf16[512,1280]{1,0:T(8,128)(2,1)}, u32[]{:S(2)}, u32[]{:S(2)}) collective-permute-start(bf16[512,1280]{1,0:T(8,128)(2,1)} %get-tuple-element.85), channel_id=1, source_target_pairs={{0,4},{4,0},{8,12},{12,8},{16,20},{20,16},{24,28},{28,24},{1,5},{5... | collective-permute-start | bytes 3932168 | tf_op jit(solution)/shard_map/ppermute | solution.py:21
  93.9 17.0 %collective-permute-start.8 = (bf16[128,1024]{1,0:T(8,128)(2,1)}, bf16[128,1024]{1,0:T(8,128)(2,1)}, u32[]{:S(2)}, u32[]{:S(2)}) collective-permute-start(bf16[128,1024]{1,0:T(8,128)(2,1)} %get-tuple-element.83.refs_5_), channel_id=1, source_target_pairs={{0,16},{4,20},{8,24},{12,28},{16,0},{20,4},{24,8},{28,12},{1,17},{... | collective-permute-start | bytes 786440 | tf_op jit(solution)/shard_map/ppermute | solution.py:21
  96.2 3.6 %collective-permute-start.10 = (s32[256]{0:T(256)S(1)}, s32[256]{0:T(256)S(1)}, u32[]{:S(2)}, u32[]{:S(2)}) collective-permute-start(s32[256]{0:T(256)S(1)} %add.93.refs_3_), channel_id=1, source_target_pairs={{0,2},{1,3},{2,0},{3,1},{4,6},{5,7},{6,4},{7,5},{8,10},{9,11},{10,... | collective-permute-start | bytes 3080 | tf_op jit(solution)/shard_map/ppermute | solution.py:21
  102.2 8.8 %copy-start.21 = (f32[128,1024]{1,0:T(8,128)S(1)}, f32[128,1024]{1,0:T(8,128)}, u32[]{:S(2)}) copy-start(f32[128,1024]{1,0:T(8,128)} %copy-done.20) | copy-start | bytes 1572868
  103.5 20.7 %collective-permute-start.13 = (bf16[128,1024]{1,0:T(8,128)(2,1)S(1)}, bf16[128,1024]{1,0:T(8,128)(2,1)S(1)}, u32[]{:S(2)}, u32[]{:S(2)}) collective-permute-start(bf16[128,1024]{1,0:T(8,128)(2,1)S(1)} %get-tuple-element.90.refs_3_.refs_1_), channel_id=1, source_target_pairs={{0,16},{4,20},{8,24},{12,28},{16,0},{20,4},{24,8},{28,12},{1,17},{... | collective-permute-start | bytes 786440 | tf_op jit(solution)/shard_map/ppermute | solution.py:21
  104.2 27.1 %collective-permute-start.12 = (bf16[512,768]{1,0:T(8,128)(2,1)}, bf16[512,768]{1,0:T(8,128)(2,1)S(1)}, u32[]{:S(2)}, u32[]{:S(2)}) collective-permute-start(bf16[512,768]{1,0:T(8,128)(2,1)} %shard_map.150), channel_id=1, source_target_pairs={{0,8},{4,12},{8,0},{12,4},{16,24},{20,28},{24,16},{28,20},{1,9},{5... | collective-permute-start | bytes 2359304 | tf_op jit(solution)/shard_map/ppermute | solution.py:21
  114.2 25.3 %collective-permute-start.11 = (bf16[256,1024]{1,0:T(8,128)(2,1)S(1)}, bf16[256,1024]{1,0:T(8,128)(2,1)S(1)}, u32[]{:S(2)}, u32[]{:S(2)}) collective-permute-start(bf16[256,1024]{1,0:T(8,128)(2,1)S(1)} %get-tuple-element.93.refs_5_), channel_id=1, source_target_pairs={{0,8},{4,12},{8,0},{12,4},{16,24},{20,28},{24,16},{28,20},{1,9},{5... | collective-permute-start | bytes 1572872 | tf_op jit(solution)/shard_map/ppermute | solution.py:21
  122.9 46.3 %collective-permute-start.15 = (bf16[512,1024]{1,0:T(8,128)(2,1)}, bf16[512,1024]{1,0:T(8,128)(2,1)S(1)}, u32[]{:S(2)}, u32[]{:S(2)}) collective-permute-start(bf16[512,1024]{1,0:T(8,128)(2,1)} %get-tuple-element.104), channel_id=1, source_target_pairs={{0,4},{4,0},{8,12},{12,8},{16,20},{20,16},{24,28},{28,24},{1,5},{5... | collective-permute-start | bytes 3145736 | tf_op jit(solution)/shard_map/ppermute | solution.py:21
  125.1 16.5 %copy-start.13 = (bf16[512,1280]{1,0:T(8,128)(2,1)S(1)}, bf16[512,1280]{1,0:T(8,128)(2,1)}, u32[]{:S(2)}) copy-start(bf16[512,1280]{1,0:T(8,128)(2,1)} %get-tuple-element.84.refs_0_) | copy-start | bytes 3932164
  131.8 38.0 %collective-permute-start.21 = (bf16[256,768]{1,0:T(8,128)(2,1)S(1)}, bf16[256,768]{1,0:T(8,128)(2,1)S(1)}, u32[]{:S(2)}, u32[]{:S(2)}) collective-permute-start(bf16[256,768]{1,0:T(8,128)(2,1)S(1)} %get-tuple-element.99.refs_2_), channel_id=1, source_target_pairs={{0,4},{4,0},{8,12},{12,8},{16,20},{20,16},{24,28},{28,24},{1,5},{5... | collective-permute-start | bytes 1179656 | tf_op jit(solution)/shard_map/ppermute | solution.py:21
  139.8 13.3 %collective-permute-start.17 = (bf16[128,1024]{1,0:T(8,128)(2,1)S(1)}, bf16[128,1024]{1,0:T(8,128)(2,1)S(1)}, u32[]{:S(2)}, u32[]{:S(2)}) collective-permute-start(bf16[128,1024]{1,0:T(8,128)(2,1)S(1)} %get-tuple-element.100.refs_2_), channel_id=1, source_target_pairs={{0,16},{4,20},{8,24},{12,28},{16,0},{20,4},{24,8},{28,12},{1,17},{... | collective-permute-start | bytes 786440 | tf_op jit(solution)/shard_map/ppermute | solution.py:21
  143.2 25.5 %collective-permute-start.16 = (bf16[256,1280]{1,0:T(8,128)(2,1)S(1)}, bf16[256,1280]{1,0:T(8,128)(2,1)S(1)}, u32[]{:S(2)}, u32[]{:S(2)}) collective-permute-start(bf16[256,1280]{1,0:T(8,128)(2,1)S(1)} %get-tuple-element.101.refs_5_), channel_id=1, source_target_pairs={{0,8},{4,12},{8,0},{12,4},{16,24},{20,28},{24,16},{28,20},{1,9},{5... | collective-permute-start | bytes 1966088 | tf_op jit(solution)/shard_map/ppermute | solution.py:21
  152.0 44.8 %collective-permute-start.14 = (bf16[512,512]{1,0:T(8,128)(2,1)S(1)}, bf16[512,512]{1,0:T(8,128)(2,1)S(1)}, u32[]{:S(2)}, u32[]{:S(2)}) collective-permute-start(bf16[512,512]{1,0:T(8,128)(2,1)S(1)} %get-tuple-element.103), channel_id=1, source_target_pairs={{0,4},{4,0},{8,12},{12,8},{16,20},{20,16},{24,28},{28,24},{1,5},{5... | collective-permute-start | bytes 1572872 | tf_op jit(solution)/shard_map/ppermute | solution.py:21
  153.1 33.4 %collective-permute-start.19 = (bf16[512,512]{1,0:T(8,128)(2,1)}, bf16[512,512]{1,0:T(8,128)(2,1)S(1)}, u32[]{:S(2)}, u32[]{:S(2)}) collective-permute-start(bf16[512,512]{1,0:T(8,128)(2,1)} %get-tuple-element.113), channel_id=1, source_target_pairs={{0,8},{4,12},{8,0},{12,4},{16,24},{20,28},{24,16},{28,20},{1,9},{5... | collective-permute-start | bytes 1572872 | tf_op jit(solution)/shard_map/ppermute | solution.py:21
  169.1 11.5 %collective-permute-start.20 = (bf16[128,1280]{1,0:T(8,128)(2,1)S(1)}, bf16[128,1280]{1,0:T(8,128)(2,1)S(1)}, u32[]{:S(2)}, u32[]{:S(2)}) collective-permute-start(bf16[128,1280]{1,0:T(8,128)(2,1)S(1)} %get-tuple-element.110.refs_2_), channel_id=1, source_target_pairs={{0,16},{4,20},{8,24},{12,28},{16,0},{20,4},{24,8},{28,12},{1,17},{... | collective-permute-start | bytes 983048 | tf_op jit(solution)/shard_map/ppermute | solution.py:21
  169.7 26.0 %collective-permute-start.18 = (bf16[256,1024]{1,0:T(8,128)(2,1)S(1)}, bf16[256,1024]{1,0:T(8,128)(2,1)S(1)}, u32[]{:S(2)}, u32[]{:S(2)}) collective-permute-start(bf16[256,1024]{1,0:T(8,128)(2,1)S(1)} %get-tuple-element.112.refs_2_), channel_id=1, source_target_pairs={{0,8},{4,12},{8,0},{12,4},{16,24},{20,28},{24,16},{28,20},{1,9},{5... | collective-permute-start | bytes 1572872 | tf_op jit(solution)/shard_map/ppermute | solution.py:21
  170.1 26.8 %collective-permute-start.25 = (bf16[128,768]{1,0:T(8,128)(2,1)S(1)}, bf16[128,768]{1,0:T(8,128)(2,1)S(1)}, u32[]{:S(2)}, u32[]{:S(2)}) collective-permute-start(bf16[128,768]{1,0:T(8,128)(2,1)S(1)} %get-tuple-element.117.refs_4_), channel_id=1, source_target_pairs={{0,16},{4,20},{8,24},{12,28},{16,0},{20,4},{24,8},{28,12},{1,17},{... | collective-permute-start | bytes 589832 | tf_op jit(solution)/shard_map/ppermute | solution.py:21
  186.7 11.7 %copy-start.22 = (bf16[256,512]{1,0:T(8,128)(2,1)}, bf16[256,512]{1,0:T(8,128)(2,1)S(1)}, u32[]{:S(2)}) copy-start(bf16[256,512]{1,0:T(8,128)(2,1)S(1)} %get-tuple-element.119.refs_2_) | copy-start | bytes 786436
  198.4 14.3 %collective-permute-start.32 = (bf16[16,7168]{1,0:T(8,128)(2,1)S(1)}, bf16[16,7168]{1,0:T(8,128)(2,1)}, u32[]{:S(2)}, u32[]{:S(2)}) collective-permute-start(bf16[16,7168]{1,0:T(8,128)(2,1)S(1)} %shard_map.173), channel_id=1, source_target_pairs={{0,16},{4,20},{8,24},{12,28},{16,0},{20,4},{24,8},{28,12},{1,17},{... | collective-permute-start | bytes 688136 | tf_op jit(solution)/shard_map/ppermute | solution.py:21
  199.2 24.6 %collective-permute-start.23 = (bf16[256,512]{1,0:T(8,128)(2,1)}, bf16[256,512]{1,0:T(8,128)(2,1)}, u32[]{:S(2)}, u32[]{:S(2)}) collective-permute-start(bf16[256,512]{1,0:T(8,128)(2,1)} %copy-done.22), channel_id=1, source_target_pairs={{0,4},{4,0},{8,12},{12,8},{16,20},{20,16},{24,28},{28,24},{1,5},{5... | collective-permute-start | bytes 786440 | tf_op jit(solution)/shard_map/ppermute | solution.py:21
  200.2 23.6 %collective-permute-start.22 = (bf16[256,512]{1,0:T(8,128)(2,1)}, bf16[256,512]{1,0:T(8,128)(2,1)}, u32[]{:S(2)}, u32[]{:S(2)}) collective-permute-start(bf16[256,512]{1,0:T(8,128)(2,1)} %copy-done.23), channel_id=1, source_target_pairs={{0,8},{4,12},{8,0},{12,4},{16,24},{20,28},{24,16},{28,20},{1,9},{5... | collective-permute-start | bytes 786440 | tf_op jit(solution)/shard_map/ppermute | solution.py:21
  202.6 18.3 %collective-permute-start.24 = (bf16[128,1024]{1,0:T(8,128)(2,1)}, bf16[128,1024]{1,0:T(8,128)(2,1)}, u32[]{:S(2)}, u32[]{:S(2)}) collective-permute-start(bf16[128,1024]{1,0:T(8,128)(2,1)} %copy-done.24), channel_id=1, source_target_pairs={{0,16},{4,20},{8,24},{12,28},{16,0},{20,4},{24,8},{28,12},{1,17},{... | collective-permute-start | bytes 786440 | tf_op jit(solution)/shard_map/ppermute | solution.py:21
  214.4 33.4 %collective-permute-start.33 = (bf16[32,7168]{1,0:T(8,128)(2,1)}, bf16[32,7168]{1,0:T(8,128)(2,1)}, u32[]{:S(2)}, u32[]{:S(2)}) collective-permute-start(bf16[32,7168]{1,0:T(8,128)(2,1)} %pad_maximum_fusion.9), channel_id=1, source_target_pairs={{0,8},{4,12},{8,0},{12,4},{16,24},{20,28},{24,16},{28,20},{1,9},{5... | collective-permute-start | bytes 1376264 | tf_op jit(solution)/shard_map/ppermute | solution.py:21
  226.4 13.1 %collective-permute-start.26 = (bf16[128,1024]{1,0:T(8,128)(2,1)}, bf16[128,1024]{1,0:T(8,128)(2,1)S(1)}, u32[]{:S(2)}, u32[]{:S(2)}) collective-permute-start(bf16[128,1024]{1,0:T(8,128)(2,1)} %get-tuple-element.131.refs_4_), channel_id=1, source_target_pairs={{0,16},{4,20},{8,24},{12,28},{16,0},{20,4},{24,8},{28,12},{1,17},{... | collective-permute-start | bytes 786440 | tf_op jit(solution)/shard_map/ppermute | solution.py:21
  243.3 14.6 %copy-start.28 = (s32[8]{0:T(128)S(1)}, s32[8]{0:T(128)}, u32[]{:S(2)}) copy-start(s32[8]{0:T(128)} %constant.83.clone) | copy-start | bytes 100
  244.1 12.6 %all-to-all-start = ((bf16[8,2,7296]{2,1,0:T(2,128)(2,1)}), bf16[8,2,7296]{2,1,0:T(2,128)(2,1)S(1)}, u32[]{:S(2)}, u32[]{:S(2)}) async-start(bf16[8,2,7296]{2,1,0:T(2,128)(2,1)} %reshape.79), calls=%async_computation | async-start | bytes 466944 | tf_op jit(solution)/shard_map/all_to_all | solution.py:338
  249.0 32.4 %collective-permute-start.34 = (bf16[64,7168]{1,0:T(8,128)(2,1)S(1)}, bf16[64,7168]{1,0:T(8,128)(2,1)S(1)}, u32[]{:S(2)}, u32[]{:S(2)}) collective-permute-start(bf16[64,7168]{1,0:T(8,128)(2,1)S(1)} %pad_maximum_fusion.8), channel_id=1, source_target_pairs={{0,4},{4,0},{8,12},{12,8},{16,20},{20,16},{24,28},{28,24},{1,5},{5... | collective-permute-start | bytes 2752520 | tf_op jit(solution)/shard_map/ppermute | solution.py:21
  256.8 6.1 %collective-permute-start.27 = (bf16[16,7296]{1,0:T(8,128)(2,1)S(1)}, bf16[16,7296]{1,0:T(8,128)(2,1)S(1)}, u32[]{:S(2)}, u32[]{:S(2)}) collective-permute-start(bf16[16,7296]{1,0:T(8,128)(2,1)S(1)} %reshape.80.refs_0_), channel_id=1, source_target_pairs={{0,2},{1,3},{2,0},{3,1},{4,6},{5,7},{6,4},{7,5},{8,10},{9,11},{10,... | collective-permute-start | bytes 700424 | tf_op jit(solution)/shard_map/ppermute | solution.py:21
  257.9 5.2 %collective-permute-start.28 = (bf16[16,7296]{1,0:T(8,128)(2,1)S(1)}, bf16[16,7296]{1,0:T(8,128)(2,1)S(1)}, u32[]{:S(2)}, u32[]{:S(2)}) collective-permute-start(bf16[16,7296]{1,0:T(8,128)(2,1)S(1)} %reshape.80.refs_0_), channel_id=1, source_target_pairs={{0,1},{1,0},{2,3},{3,2},{4,5},{5,4},{6,7},{7,6},{8,9},{9,8},{10,11... | collective-permute-start | bytes 700424 | tf_op jit(solution)/shard_map/ppermute | solution.py:21
  262.9 1.5 collective-permute-start.29
  281.2 4.6 %collective-permute-start.30 = (bf16[32,7168]{1,0:T(8,128)(2,1)S(1)}, bf16[32,7168]{1,0:T(8,128)(2,1)S(1)}, u32[]{:S(2)}, u32[]{:S(2)}) collective-permute-start(bf16[32,7168]{1,0:T(8,128)(2,1)S(1)} %get-tuple-element.135), channel_id=1, source_target_pairs={{0,1},{1,0},{2,3},{3,2},{4,5},{5,4},{6,7},{7,6},{8,9},{9,8},{10,11... | collective-permute-start | bytes 1376264 | tf_op jit(solution)/shard_map/ppermute | solution.py:21
  283.5 15.4 %copy-start.27 = (f32[256]{0:T(256)S(1)}, f32[256]{0:T(256)}, u32[]{:S(2)}) copy-start(f32[256]{0:T(256)} %param.16) | copy-start | bytes 3076
  283.5 1.3 collective-permute-start.35
  284.8 3.7 %collective-permute-start.36 = (f32[16,128]{1,0:T(8,128)S(1)}, f32[16,128]{1,0:T(8,128)S(1)}, u32[]{:S(2)}, u32[]{:S(2)}) collective-permute-start(f32[16,128]{1,0:T(8,128)S(1)} %slice.36), channel_id=1, source_target_pairs={{0,2},{1,3},{2,0},{3,1},{4,6},{5,7},{6,4},{7,5},{8,10},{9,11},{10,... | collective-permute-start | bytes 24584 | tf_op jit(solution)/shard_map/ppermute | solution.py:21
  285.8 23.0 %copy-start.1 = (bf16[7168,32]{0,1:T(8,128)(2,1)S(1)}, bf16[7168,32]{0,1:T(8,128)(2,1)}, u32[]{:S(2)}) copy-start(bf16[7168,32]{0,1:T(8,128)(2,1)} %param.15) | copy-start | bytes 1376260
  285.9 7.6 %collective-permute-start.31 = (bf16[16,7168]{1,0:T(8,128)(2,1)S(1)}, bf16[16,7168]{1,0:T(8,128)(2,1)S(1)}, u32[]{:S(2)}, u32[]{:S(2)}) collective-permute-start(bf16[16,7168]{1,0:T(8,128)(2,1)S(1)} %get-tuple-element.137), channel_id=1, source_target_pairs={{0,2},{1,3},{2,0},{3,1},{4,6},{5,7},{6,4},{7,5},{8,10},{9,11},{10,... | collective-permute-start | bytes 688136 | tf_op jit(solution)/shard_map/ppermute | solution.py:21
  294.5 12.4 %all-to-all-start.1 = ((bf16[8,2,7168]{2,1,0:T(2,128)(2,1)}), bf16[8,2,7168]{2,1,0:T(2,128)(2,1)S(1)}, u32[]{:S(2)}, u32[]{:S(2)}) async-start(bf16[8,2,7168]{2,1,0:T(2,128)(2,1)} %reshape.81), calls=%async_computation.1 | async-start | bytes 458752 | tf_op jit(solution)/shard_map/all_to_all | solution.py:444
  (20 other events, 52.1 us)

commit v2 on v1

--- a/solution.py
+++ b/solution.py
@@ -35,7 +35,7 @@
 ANY = pl.BlockSpec(memory_space=pl.ANY)
 
 
-def run(body, grid, ins, outs, marks, aliases=None, scratch=(), mib=16):
+def run(body, grid, ins, outs, marks, aliases=None, scratch=(), mib=16, moved=1):
     count, skip = len(ins), len(marks)
 
     def inner(*refs):
@@ -50,7 +50,7 @@
         input_output_aliases=aliases or {},
         scratch_shapes=list(scratch),
         compiler_params=pltpu.CompilerParams(vmem_limit_bytes=mib * 1024 * 1024),
-        cost_estimate=pl.CostEstimate(flops=1, bytes_accessed=1, transcendentals=0),
+        cost_estimate=pl.CostEstimate(flops=1, bytes_accessed=moved, transcendentals=0),
     )(*[a for a, _ in ins], *marks)
 
 
@@ -152,7 +152,7 @@
         rel = rel + [j | bit for j in rel]
     per_device = routed // tp_count
     per_part = per_device // ep_count
-    part_rows = -(-(per_part + 2) // 16) * 16
+    digit_cols = -(-2 * routed // (per_part * 128)) * 128
     base_digit = 64
 
     def count_hop():
@@ -160,11 +160,14 @@
         counts = counts + swap(counts, "ep", count_hops.pop(0))
         return [counts]
 
-    def router_gather(marks):
+    def router_payload():
         part = lax.dynamic_slice_in_dim(router.T, ep_me * per_part, per_part, axis=0)
-        digits = jnp.stack([counts // base_digit, counts % base_digit]).astype(bf16)
-        digits = jnp.pad(digits, ((0, part_rows - per_part - 2), (0, width - routed)))
-        part = gated(jnp.concatenate([part, digits], axis=0), marks)
+        digits = jnp.concatenate([counts // base_digit, counts % base_digit]).astype(bf16)
+        digits = jnp.pad(digits, (0, per_part * digit_cols - 2 * routed)).reshape(per_part, digit_cols)
+        return jnp.concatenate([part, digits], axis=1)
+
+    def router_gather(part, marks):
+        part = gated(part, marks)
         for bit in tp_bits[::-1]:
             part = jnp.concatenate([part, swap(part, "tp", bit)], axis=0)
         return part
@@ -173,11 +176,14 @@
         lax.dynamic_slice_in_dim(attn_out, (me ^ j) * tok_rows, tok_rows, axis=0)
         for j in range(tp_count)
     ]
-    halves = []
-    for kind in ("y", "z"):
-        for part in (slice(0, tp_count // 2), slice(tp_count // 2, tp_count)):
-            halves.append(jnp.concatenate([blocks[j] for j in order[kind][part]], axis=0))
-    tiles = {"y0": 2, "z0": 2, "y1": 4, "y2": 4, "y3": 5, "z1": 3, "y4": 4, "y5": 2, "z2": 2}
+    halves = {
+        kind: [
+            jnp.concatenate([blocks[j] for j in order[kind][part]], axis=0)
+            for part in (slice(0, tp_count // 2), slice(tp_count // 2, tp_count))
+        ]
+        for kind in ("y", "z")
+    }
+    tiles = {"y0": 2, "z0": 4, "y1": 4, "y2": 6, "y3": 5, "y4": 4, "y5": 3}
     unit = width // sum(tiles.values())
     spans, lo = {}, 0
     for name, count in tiles.items():
@@ -196,21 +202,24 @@
             )
             outs += [(((half, tiles[name] * unit), bf16), spec)] * 2
 
+        kinds = sorted({name[0] for name in names})
+        rows_used = [rows for kind in kinds for rows in halves[kind]]
+
         def body(*refs):
             step = pl.program_id(0)
-            w, refs_out = refs[4], refs[5:]
+            w, refs_out = refs[len(rows_used)], refs[len(rows_used) + 1 :]
             for n, (name, low) in enumerate(zip(names, starts)):
 
                 @pl.when((step >= low) & (step < low + tiles[name]))
                 def _(n=n, name=name):
-                    at = 0 if name[0] == "y" else 2
+                    at = 2 * kinds.index(name[0])
                     refs_out[2 * n][...] = mm(refs[at][...], w[...]).astype(bf16)
                     refs_out[2 * n + 1][...] = mm(refs[at + 1][...], w[...]).astype(bf16)
 
         got = run(
             body,
             (sum(tiles[name] for name in names),),
-            [(rows, kept_block(rows.shape)) for rows in halves]
+            [(rows, kept_block(rows.shape)) for rows in rows_used]
             + [(w_out, pl.BlockSpec((w_out.shape[0], unit), lambda i: (0, base + i)))],
             outs,
             marks,
@@ -267,46 +276,6 @@
         hidden.append(out)
         return [mark]
 
-    marks = bulk(("y0", "z0"), [])
-    begin("y0")
-    begin("z0")
-    marks = bulk(("y1",), marks)
-    marks = second(("y0", "z0"), marks)
-    begin("y1", marks)
-    marks = bulk(("y2",), marks)
-    marks = second(("y1",), marks + count_hop())
-    begin("y2", marks)
-    marks = third(("y0", "z0"), marks)
-    marks = bulk(("y3", "z1"), marks)
-    begin("y3")
-    marks = third(("y1",), marks)
-    begin("z1", marks)
-    marks = finish(("y0", "z0"), marks + count_hop())
-    marks = second(("y2",), marks)
-    marks = bulk(("y4",), marks)
-    begin("y4")
-    marks = finish(("y1",), marks)
-    marks = second(("z1",), marks)
-    marks = third(("y2",), marks)
-    marks = second(("y3",), marks)
-    marks = bulk(("y5", "z2"), marks)
-    begin("y5")
-    begin("z2")
-    marks = finish(("y2",), marks)
-    marks = third(("y3",), marks)
-    marks = second(("y4",), marks)
-    marks = third(("z1",), marks)
-    marks = finish(("y3",), marks)
-    marks = second(("z2",), marks)
-    marks = third(("y4",), marks)
-    marks = second(("y5",), marks)
-    marks = finish(("z1",), marks)
-    router_all = router_gather(marks)
-    marks = finish(("y4",), marks)
-    marks = third(("y5", "z2"), marks)
-    finish(("y5", "z2"), marks)
-    (hidden_out,) = hidden
-
     window = onehot[:, :, :tp_count]
     member = jnp.any(window, axis=1).astype(jnp.int32)
     slot_rank = jnp.cumsum(member, axis=0) - member
@@ -316,6 +285,46 @@
 
     lanes = 128
     choice_cols = jnp.pad(choices.astype(bf16), ((0, 0), (0, lanes - top)))
+    gain = norm_gain[None]
+
+    marks = bulk(("y0",), [])
+    begin("y0")
+    marks = bulk(("z0",), marks)
+    begin("z0")
+    marks = bulk(("y1",), marks)
+    marks = second(("y0",), marks)
+    begin("y1", marks)
+    marks = second(("z0",), marks + [pick, choice_cols, gain])
+    marks = bulk(("y2",), marks + count_hop())
+    marks = second(("y1",), marks)
+    marks = third(("y0",), marks)
+    marks = third(("z0",), marks)
+    begin("y2", marks)
+    marks = bulk(("y3",), marks)
+    begin("y3")
+    marks = third(("y1",), marks)
+    marks = finish(("y0",), marks)
+    marks = finish(("z0",), marks)
+    marks = second(("y2",), marks + count_hop())
+    marks = bulk(("y4",), marks)
+    begin("y4")
+    marks = finish(("y1",), marks)
+    marks = third(("y2",), marks)
+    router_part = router_payload()
+    marks = second(("y3",), marks + [router_part])
+    marks = bulk(("y5",), marks)
+    begin("y5")
+    marks = finish(("y2",), marks)
+    marks = third(("y3",), marks)
+    marks = second(("y4",), marks)
+    marks = finish(("y3",), marks)
+    marks = third(("y4",), marks)
+    marks = second(("y5",), marks)
+    router_all = router_gather(router_part, marks)
+    marks = third(("y5",), marks)
+    marks = finish(("y4",), marks)
+    finish(("y5",), marks)
+    (hidden_out,) = hidden
 
     def norm_body(pick, rows, gain, choice, out):
         stream = mm(pick[...], rows[...])
@@ -329,7 +338,7 @@
         [
             (pick, whole(pick.shape)),
             (hidden_out, whole(hidden_out.shape)),
-            (norm_gain[None], whole((1, width))),
+            (gain, whole((1, width))),
             (choice_cols, whole(choice_cols.shape)),
         ],
         [(((first, width + lanes), bf16), whole((first, width + lanes)))],
@@ -346,8 +355,11 @@
     deep = block_of(slice(0, width), 1024)
     last_step = width // deep - 1
 
-    def up_body(*refs):
-        rows, (gate_w, up_w, out, gate_sum, up_sum) = refs[:ep_count], refs[ep_count:]
+    cut = rows_all // 2
+
+    def expert_body(*refs):
+        rows, refs = refs[:ep_count], refs[ep_count:]
+        gate_a, gate_b, up_a, up_b, down_a, down_b, out, kept, gate_sum, up_sum, active = refs
         step = pl.program_id(0)
 
         @pl.when(step == 0)
@@ -355,51 +367,57 @@
             gate_sum[...] = jnp.zeros_like(gate_sum)
             up_sum[...] = jnp.zeros_like(up_sum)
 
-        x = jnp.concatenate([r[...] for r in rows], axis=0)
-        gate_sum[...] += mm(x, gate_w[0])
-        up_sum[...] += mm(x, up_w[0])
+        @pl.when(step <= last_step)
+        def _():
+            x = jnp.concatenate([r[...] for r in rows], axis=0)
+            gate_sum[...] += mm(x[:, : deep // 2], gate_a[0]) + mm(x[:, deep // 2 :], gate_b[0])
+            up_sum[...] += mm(x[:, : deep // 2], up_a[0]) + mm(x[:, deep // 2 :], up_b[0])
 
         @pl.when(step == last_step)
         def _():
             gate = gate_sum[...]
-            out[...] = (gate / (1.0 + jnp.exp(-gate)) * up_sum[...]).astype(bf16)
-
-    deep_rows = pl.BlockSpec((first, deep), lambda i: (0, i))
-    deep_w = pl.BlockSpec((1, deep, hid), lambda i: (0, i, 0))
-    (active,) = run(
-        up_body,
-        (last_step + 1,),
-        [(rows, deep_rows) for rows in picked] + [(w_gate, deep_w), (w_up, deep_w)],
-        [(((rows_all, hid), bf16), whole((rows_all, hid)))],
-        [],
-        scratch=[pltpu.VMEM((rows_all, hid), f32)] * 2,
-    )
-    cut = rows_all // 2
-
-    def down_body(x, w, out, kept):
-        value = mm(x[...], w[0])
-        kept[...] = value[:cut]
-        out[...] = value[cut:].astype(bf16)
-
-    wide_half = pl.BlockSpec((cut, deep), lambda i: (0, i))
+            active[...] = (gate / (1.0 + jnp.exp(-gate)) * up_sum[...]).astype(bf16)
+
+        @pl.when(step > last_step)
+        def _():
+            x = active[...]
+            value = mm(x[:, : hid // 2], down_a[0]) + mm(x[:, hid // 2 :], down_b[0])
+            kept[...] = value[:cut]
+            out[...] = value[cut:].astype(bf16)
+
+    def early_step(i):
+        return jnp.minimum(i, last_step)
+
+    def late_step(i):
+        return jnp.maximum(i - last_step - 1, 0)
+
+    deep_rows = pl.BlockSpec((first, deep), lambda i: (0, early_step(i)))
+    deep_a = pl.BlockSpec((1, deep // 2, hid), lambda i: (0, 2 * early_step(i), 0))
+    deep_b = pl.BlockSpec((1, deep // 2, hid), lambda i: (0, 2 * early_step(i) + 1, 0))
+    down_a = pl.BlockSpec((1, hid // 2, deep), lambda i: (0, 0, late_step(i)))
+    down_b = pl.BlockSpec((1, hid // 2, deep), lambda i: (0, 1, late_step(i)))
+    wide_half = pl.BlockSpec((cut, deep), lambda i: (0, late_step(i)))
     out, kept = run(
-        down_body,
-        (last_step + 1,),
-        [(active, whole(active.shape)), (w_down, pl.BlockSpec((1, hid, deep), lambda i: (0, 0, i)))],
+        expert_body,
+        (2 * (last_step + 1),),
+        [(rows, deep_rows) for rows in picked]
+        + [(w_gate, deep_a), (w_gate, deep_b), (w_up, deep_a), (w_up, deep_b), (w_down, down_a), (w_down, down_b)],
         [(((cut, width), bf16), wide_half), (((cut, width), f32), wide_half)],
         [],
+        scratch=[pltpu.VMEM((rows_all, hid), f32)] * 2 + [pltpu.VMEM((rows_all, hid), bf16)],
+        mib=50,
     )
     got = swap(out, "ep", ep_bits[0])
 
-    row_of = jnp.arange(part_rows, dtype=jnp.int32)
+    row_of = jnp.arange(per_part, dtype=jnp.int32)
     column_ids = (jnp.array(rel, jnp.int32) ^ me)[:, None] * per_device + ep_me * per_part + row_of
-    column_ids = jnp.where(row_of < per_part, column_ids, -1).reshape(1, -1)
+    column_ids = column_ids.reshape(1, -1)
 
     def score_body(*refs):
         rows, (table, columns, expert, out) = refs[:ep_count], refs[ep_count:]
         x = jnp.concatenate([r[:, :width] for r in rows], axis=0)
         ids = jnp.concatenate([r[:, width:] for r in rows], axis=0).astype(f32).astype(jnp.int32)
-        scores = 1.0 / (1.0 + jnp.exp(-mm_t(x, table[...])))
+        scores = 1.0 / (1.0 + jnp.exp(-mm_t(x, table[:, :width])))
         here = columns[...]
         chosen = jnp.where(here == expert[...], scores, 0.0)
         total = jnp.zeros_like(scores)
@@ -446,8 +464,8 @@
     ).reshape(first, width)
     moe_out = mm_rows(pick, returned).astype(bf16)
 
-    digits = router_all.reshape(tp_count, part_rows, width)[:, per_part : per_part + 2, :routed]
-    digits = jnp.sum(digits.astype(jnp.int32), axis=0)
+    digits = router_all[:, width:].reshape(tp_count, per_part * digit_cols)[:, : 2 * routed]
+    digits = jnp.sum(digits.astype(jnp.int32), axis=0).reshape(2, routed)
     counts = digits[0] * base_digit + digits[1]
     all_slots = all_rows * ep_count * top
     load = counts.astype(f32) * routed / all_slots

time: 310 us -> 268 us (0.86)
  waiting for transfers between devices: 159 us -> 130 us
  local copies, waits for them, and re-layouts: 23.6 us -> 11.7 us
  Pallas kernels: 68.5 us -> 74.4 us
  other arithmetic: 7.88 us -> 3.17 us
  starting transfers between devices: 47.1 us -> 43.5 us
    ppermute x37 -> x33, waiting for transfers between devices: 146 us -> 115 us  [swap(): return lax.ppermute(value, axis, [(i, i ^ bit) for i in range(size)])]
    unnamed x58 -> x49, local copies, waits for them, and re-layouts: 19.5 us -> 7.8 us
    pallas_call x38 -> x36, Pallas kernels: 68.5 us -> 74.4 us  [run(): pl.pallas_call(inner, grid=grid, in_specs=[spec for _, spec in ins] + [AN...]
    concatenate x3, other arithmetic: 4.1 us -> 0.11 us  [router_gather(): part = jnp.concatenate([part, swap(part, 'tp', bit)], axis=0)]
    ppermute x37 -> x33, starting transfers between devices: 38.9 us -> 36.1 us  [swap(): return lax.ppermute(value, axis, [(i, i ^ bit) for i in range(size)])]
  transfers between devices with their start and end apart: 39 -> 35, of which waited for: 24 -> 22; matrix products, arithmetic and copies ran while one was open for 2% -> 1% of each run, Pallas kernels for 20% -> 26%
where the time goes in v2:
time: 268 us; the launch traced here: 266 us
  waiting for transfers between devices  130 us (49%)
  Pallas kernels  74.4 us (28%)
  starting transfers between devices  43.5 us (16%)
  local copies, waits for them, and re-layouts  11.7 us (4%)
  other arithmetic  3.17 us (1%)
    ppermute x33, waiting for transfers between devices, swap(): return lax.ppermute(value, axis, [(i, i ^ bit) for i in range(size)])  115 us
    pallas_call x36, Pallas kernels, run(): pl.pallas_call(inner, grid=grid, in_specs=[spec for _, spec in ins] + [AN...  74.4 us
    ppermute x33, starting transfers between devices, swap(): return lax.ppermute(value, axis, [(i, i ^ bit) for i in range(size)])  36.1 us
    unnamed x49, local copies, waits for them, and re-layouts  7.8 us
    all_to_all x1, waiting for transfers between devices, on_device(): lax.all_to_all(normed.reshape(tp_count, CAP, width + lanes), 'tp', split_...  7.52 us
    all_to_all x1, waiting for transfers between devices, on_device(): lax.all_to_all(summed.reshape(tp_count, CAP, width), 'tp', split_axis=0,...  7.36 us
  transfers between devices with their start and end apart: 35, of which 22 were waited for; matrix products, arithmetic and copies ran while one was open for 1% of the time, Pallas kernels for 26%

profile of v2, /device:TPU:0, one launch (start us, length us, event | category | flops | bytes accessed | tf_op | source)
XLA Modules:
  0.0 266.2 jit_solution(12255722997291860887)
XLA Ops:
  0.7 1.7 constant_dynamic-slice_fusion.3
  2.4 1.4 pad_maximum_fusion
  3.9 3.6 %shard_map.138 = (bf16[512,512]{1,0:T(8,128)(2,1)S(1)}, bf16[512,512]{1,0:T(8,128)(2,1)}) custom-call(bf16[512,1024]{1,0:T(8,128)(2,1)S(1)} %get-tuple-element.133.refs_0_, bf16[512,1024]{1,0:T(8,128)(2,1)S(1)} %get-tuple-element.135.refs_1_, bf16[1024,7168]{1,0:T(8,128)(2,1)} %refs_2_.23), custom_call_target="tpu_custom_call" | custom-call | flops 1 | bytes 1 | tf_op jit(solution)/shard_map/pallas_call | solution.py:44
  7.5 3.0 %collective-permute-start.1 = (bf16[512,512]{1,0:T(8,128)(2,1)}, bf16[512,512]{1,0:T(8,128)(2,1)}, u32[]{:S(2)}, u32[]{:S(2)}) collective-permute-start(bf16[512,512]{1,0:T(8,128)(2,1)} %get-tuple-element.66), channel_id=1, source_target_pairs={{0,4},{4,0},{8,12},{12,8},{16,20},{20,16},{24,28},{28,24},{1,5},{5... | collective-permute-start | bytes 1572872 | tf_op jit(solution)/shard_map/ppermute | solution.py:21
  10.5 5.6 %shard_map.139 = (bf16[512,1024]{1,0:T(8,128)(2,1)S(1)}, bf16[512,1024]{1,0:T(8,128)(2,1)}) custom-call(bf16[512,1024]{1,0:T(8,128)(2,1)S(1)} %get-tuple-element.134.refs_0_, bf16[512,1024]{1,0:T(8,128)(2,1)} %get-tuple-element.132.refs_1_, bf16[1024,7168]{1,0:T(8,128)(2,1)} %refs_2_.23, bf16[512,512]{1,0:T(8,128)(2,1)S(1)} %get-tuple-element.63.refs_3_.refs_0_), custom_call_target="tpu_custom_call" | custom-call | flops 1 | bytes 1 | tf_op jit(solution)/shard_map/pallas_call | solution.py:44
  17.0 1.6 collective-permute-start
  18.6 5.6 %shard_map.140 = (bf16[512,1024]{1,0:T(8,128)(2,1)S(1)}, bf16[512,1024]{1,0:T(8,128)(2,1)}) custom-call(bf16[512,1024]{1,0:T(8,128)(2,1)S(1)} %get-tuple-element.133.refs_0_, bf16[512,1024]{1,0:T(8,128)(2,1)} %copy-done.4, bf16[1024,7168]{1,0:T(8,128)(2,1)} %refs_2_.23, bf16[512,1024]{1,0:T(8,128)(2,1)} %copy-done.8), custom_call_target="tpu_custom_call" | custom-call | flops 1 | bytes 1 | tf_op jit(solution)/shard_map/pallas_call | solution.py:44
  28.0 14.0 %collective-permute-done.refs_1_ = bf16[512,1024]{1,0:T(8,128)(2,1)} collective-permute-done((bf16[512,1024]{1,0:T(8,128)(2,1)}, bf16[512,1024]{1,0:T(8,128)(2,1)}, u32[]{:S(2)}, u32[]{:S(2)}) %collective-permute-start) | collective-permute-done | bytes 1048608 | tf_op jit(solution)/shard_map/ppermute | solution.py:21
  45.0 1.7 collective-permute-start.3
  48.2 7.5 %shard_map.144 = (bf16[512,1536]{1,0:T(8,128)(2,1)}, bf16[512,1536]{1,0:T(8,128)(2,1)}) custom-call(bf16[512,1024]{1,0:T(8,128)(2,1)S(1)} %get-tuple-element.133.refs_0_, bf16[512,1024]{1,0:T(8,128)(2,1)S(1)} %copy-done.5, bf16[1024,7168]{1,0:T(8,128)(2,1)} %refs_2_.23, bf16[256,1024]{1,0:T(8,128)(2,1)S(1)} %get-tuple-element.70.refs_3_, s32[256]{0:T(256)S(1)} %add.94.refs_4_), custom_call_target="tpu_custom_call" | custom-call | flops 1 | bytes 1 | tf_op jit(solution)/shard_map/pallas_call | solution.py:44
  59.6 2.9 %collective-permute-done.2.refs_1_ = bf16[256,1024]{1,0:T(8,128)(2,1)S(1)} collective-permute-done((bf16[256,1024]{1,0:T(8,128)(2,1)S(1)}, bf16[256,1024]{1,0:T(8,128)(2,1)S(1)}, u32[]{:S(2)}, u32[]{:S(2)}) %collective-permute-start.2) | collective-permute-done | bytes 524320 | tf_op jit(solution)/shard_map/ppermute | solution.py:21
  64.1 1.5 collective-permute-start.11
  65.6 6.4 %shard_map.148 = (bf16[512,1280]{1,0:T(8,128)(2,1)S(1)}, bf16[512,1280]{1,0:T(8,128)(2,1)}) custom-call(bf16[512,1024]{1,0:T(8,128)(2,1)S(1)} %get-tuple-element.133.refs_0_, bf16[512,1024]{1,0:T(8,128)(2,1)S(1)} %copy-done.5, bf16[1024,7168]{1,0:T(8,128)(2,1)} %refs_2_.23, bf16[128,1024]{1,0:T(8,128)(2,1)S(1)} %get-tuple-element.76.refs_3_.refs_1_), custom_call_target="tpu_custom_call" | custom-call | flops 1 | bytes 1 | tf_op jit(solution)/shard_map/pallas_call | solution.py:44
  72.5 1.5 collective-permute-start.6
  74.0 2.7 collective-permute-start.8
  77.1 15.0 %collective-permute-done.10.refs_1_ = bf16[256,1024]{1,0:T(8,128)(2,1)S(1)} collective-permute-done((bf16[256,1024]{1,0:T(8,128)(2,1)S(1)}, bf16[256,1024]{1,0:T(8,128)(2,1)S(1)}, u32[]{:S(2)}, u32[]{:S(2)}) %collective-permute-start.10) | collective-permute-done | bytes 524320 | tf_op jit(solution)/shard_map/ppermute | solution.py:21
  94.1 7.1 %collective-permute-done.7.refs_1_ = bf16[512,1536]{1,0:T(8,128)(2,1)} collective-permute-done((bf16[512,1536]{1,0:T(8,128)(2,1)}, bf16[512,1536]{1,0:T(8,128)(2,1)}, u32[]{:S(2)}, u32[]{:S(2)}) %collective-permute-start.7) | collective-permute-done | bytes 1572896 | tf_op jit(solution)/shard_map/ppermute | solution.py:21
  101.2 2.5 shard_map.153
  104.3 5.6 %shard_map.154 = (bf16[512,1024]{1,0:T(8,128)(2,1)S(1)}, bf16[512,1024]{1,0:T(8,128)(2,1)}) custom-call(bf16[512,1024]{1,0:T(8,128)(2,1)S(1)} %get-tuple-element.133.refs_0_, bf16[512,1024]{1,0:T(8,128)(2,1)} %copy-done.4, bf16[1024,7168]{1,0:T(8,128)(2,1)} %refs_2_.23, bf16[256,1536]{1,0:T(8,128)(2,1)S(1)} %get-tuple-element.88.refs_3_), custom_call_target="tpu_custom_call" | custom-call | flops 1 | bytes 1 | tf_op jit(solution)/shard_map/pallas_call | solution.py:44
  111.3 11.0 %collective-permute-done.12.refs_1_ = bf16[256,1536]{1,0:T(8,128)(2,1)S(1)} collective-permute-done((bf16[256,1536]{1,0:T(8,128)(2,1)S(1)}, bf16[256,1536]{1,0:T(8,128)(2,1)S(1)}, u32[]{:S(2)}, u32[]{:S(2)}) %collective-permute-start.12) | collective-permute-done | bytes 786464 | tf_op jit(solution)/shard_map/ppermute | solution.py:21
  122.7 6.6 %collective-permute-done.6.refs_1_ = bf16[512,1280]{1,0:T(8,128)(2,1)S(1)} collective-permute-done((bf16[512,1280]{1,0:T(8,128)(2,1)}, bf16[512,1280]{1,0:T(8,128)(2,1)S(1)}, u32[]{:S(2)}, u32[]{:S(2)}) %collective-permute-start.6) | collective-permute-done | bytes 1310752 | tf_op jit(solution)/shard_map/ppermute | solution.py:21
  130.5 2.6 collective-permute-start.17
  133.0 4.0 %shard_map.158 = (bf16[512,768]{1,0:T(8,128)(2,1)S(1)}, bf16[512,768]{1,0:T(8,128)(2,1)S(1)}) custom-call(bf16[512,1024]{1,0:T(8,128)(2,1)S(1)} %get-tuple-element.133.refs_0_, bf16[512,1024]{1,0:T(8,128)(2,1)} %copy-done.4, bf16[1024,7168]{1,0:T(8,128)(2,1)} %refs_2_.23, bf16[256,1280]{1,0:T(8,128)(2,1)S(1)} %get-tuple-element.94.refs_3_), custom_call_target="tpu_custom_call" | custom-call | flops 1 | bytes 1 | tf_op jit(solution)/shard_map/pallas_call | solution.py:44
  137.6 10.1 %collective-permute-done.17.refs_1_ = bf16[128,1536]{1,0:T(8,128)(2,1)S(1)} collective-permute-done((bf16[128,1536]{1,0:T(8,128)(2,1)S(1)}, bf16[128,1536]{1,0:T(8,128)(2,1)S(1)}, u32[]{:S(2)}, u32[]{:S(2)}) %collective-permute-start.17) | collective-permute-done | bytes 393248 | tf_op jit(solution)/shard_map/ppermute | solution.py:21
  147.8 1.5 shard_map.159
  150.2 1.6 collective-permute-done.15.refs_1_
  153.2 2.6 collective-permute-start.18
  156.3 12.2 %collective-permute-done.19.refs_1_ = bf16[128,1280]{1,0:T(8,128)(2,1)S(1)} collective-permute-done((bf16[128,1280]{1,0:T(8,128)(2,1)S(1)}, bf16[128,1280]{1,0:T(8,128)(2,1)S(1)}, u32[]{:S(2)}, u32[]{:S(2)}) %collective-permute-start.19) | collective-permute-done | bytes 327712 | tf_op jit(solution)/shard_map/ppermute | solution.py:21
  168.5 2.1 shard_map.162
  171.5 3.1 %collective-permute-start.20 = (bf16[256,768]{1,0:T(8,128)(2,1)S(1)}, bf16[256,768]{1,0:T(8,128)(2,1)S(1)}, u32[]{:S(2)}, u32[]{:S(2)}) collective-permute-start(bf16[256,768]{1,0:T(8,128)(2,1)S(1)} %get-tuple-element.110.refs_2_.refs_1_), channel_id=1, source_target_pairs={{0,8},{4,12},{8,0},{12,4},{16,24},{20,28},{24,16},{28,20},{1,9},{5... | collective-permute-start | bytes 1179656 | tf_op jit(solution)/shard_map/ppermute | solution.py:21
  174.9 12.0 %collective-permute-done.20.refs_1_ = bf16[256,768]{1,0:T(8,128)(2,1)S(1)} collective-permute-done((bf16[256,768]{1,0:T(8,128)(2,1)S(1)}, bf16[256,768]{1,0:T(8,128)(2,1)S(1)}, u32[]{:S(2)}, u32[]{:S(2)}) %collective-permute-start.20) | collective-permute-done | bytes 393248 | tf_op jit(solution)/shard_map/ppermute | solution.py:21
  187.7 2.4 collective-permute-start.28
  190.2 1.5 shard_map.166
  191.6 8.8 %collective-permute-done.21.refs_1_ = bf16[128,768]{1,0:T(8,128)(2,1)S(1)} collective-permute-done((bf16[128,768]{1,0:T(8,128)(2,1)S(1)}, bf16[128,768]{1,0:T(8,128)(2,1)S(1)}, u32[]{:S(2)}, u32[]{:S(2)}) %collective-permute-start.21) | collective-permute-done | bytes 196640 | tf_op jit(solution)/shard_map/ppermute | solution.py:21
  201.9 1.5 copy-done.3
  204.7 3.6 %all-to-all-start = ((bf16[8,2,7296]{2,1,0:T(2,128)(2,1)}), bf16[8,2,7296]{2,1,0:T(2,128)(2,1)S(1)}, u32[]{:S(2)}, u32[]{:S(2)}) async-start(bf16[8,2,7296]{2,1,0:T(2,128)(2,1)} %reshape.64), calls=%async_computation | async-start | bytes 466944 | tf_op jit(solution)/shard_map/all_to_all | solution.py:347
  208.3 1.8 collective-permute-start.29
  210.1 7.5 %all-to-all-done = bf16[8,2,7296]{2,1,0:T(2,128)(2,1)S(1)} async-done(((bf16[8,2,7296]{2,1,0:T(2,128)(2,1)}), bf16[8,2,7296]{2,1,0:T(2,128)(2,1)S(1)}, u32[]{:S(2)}, u32[]{:S(2)}) %all-to-all-start) | async-done | bytes 233504 | tf_op jit(solution)/shard_map/all_to_all | solution.py:347
  217.7 1.6 collective-permute-start.23
  219.5 1.5 collective-permute-start.30
  221.0 2.8 %collective-permute-done.23.refs_1_ = bf16[16,7296]{1,0:T(8,128)(2,1)S(1)} collective-permute-done((bf16[16,7296]{1,0:T(8,128)(2,1)S(1)}, bf16[16,7296]{1,0:T(8,128)(2,1)S(1)}, u32[]{:S(2)}, u32[]{:S(2)}) %collective-permute-start.23) | collective-permute-done | bytes 233504 | tf_op jit(solution)/shard_map/ppermute | solution.py:21
  225.3 14.8 %shard_map.169 = (bf16[32,7168]{1,0:T(8,128)(2,1)S(1)}, f32[32,7168]{1,0:T(8,128)S(1)}) custom-call(bf16[16,7296]{1,0:T(8,128)(2,1)S(1)} %reshape.65.refs_0_, bf16[16,7296]{1,0:T(8,128)(2,1)S(1)} %collective-permute-done.23.refs_1_, bf16[16,7296]{1,0:T(8,128)(2,1)S(1)} %collective-permute-done.24.refs_2_, ...), custom_call_target="tpu_custom_call" | custom-call | flops 1 | bytes 1 | tf_op jit(solution)/shard_map/pallas_call | solution.py:44
  242.3 1.5 collective-permute-start.32
  244.4 1.5 collective-permute-done.32
  245.9 5.6 %collective-permute-done.27.refs_1_ = bf16[16,7168]{1,0:T(8,128)(2,1)S(1)} collective-permute-done((bf16[16,7168]{1,0:T(8,128)(2,1)S(1)}, bf16[16,7168]{1,0:T(8,128)(2,1)S(1)}, u32[]{:S(2)}, u32[]{:S(2)}) %collective-permute-start.27) | collective-permute-done | bytes 229408 | tf_op jit(solution)/shard_map/ppermute | solution.py:21
  252.4 3.8 %all-to-all-start.1 = ((bf16[8,2,7168]{2,1,0:T(2,128)(2,1)}), bf16[8,2,7168]{2,1,0:T(2,128)(2,1)S(1)}, u32[]{:S(2)}, u32[]{:S(2)}) async-start(bf16[8,2,7168]{2,1,0:T(2,128)(2,1)} %reshape.66), calls=%async_computation.1 | async-start | bytes 458752 | tf_op jit(solution)/shard_map/all_to_all | solution.py:462
  256.9 7.4 %all-to-all-done.1 = bf16[8,2,7168]{2,1,0:T(2,128)(2,1)S(1)} async-done(((bf16[8,2,7168]{2,1,0:T(2,128)(2,1)}), bf16[8,2,7168]{2,1,0:T(2,128)(2,1)S(1)}, u32[]{:S(2)}, u32[]{:S(2)}) %all-to-all-start.1) | async-done | bytes 229408 | tf_op jit(solution)/shard_map/all_to_all | solution.py:462
  264.3 1.9 fusion
  (152 shorter events, 35.3 us)
Async XLA Ops:
  0.6 65.0 %copy-start = (bf16[7168,32]{0,1:T(8,128)(2,1)S(1)}, bf16[7168,32]{0,1:T(8,128)(2,1)}, u32[]{:S(2)}) copy-start(bf16[7168,32]{0,1:T(8,128)(2,1)} %param.15) | copy-start | bytes 1376260
  7.5 17.2 %collective-permute-start.1 = (bf16[512,512]{1,0:T(8,128)(2,1)}, bf16[512,512]{1,0:T(8,128)(2,1)}, u32[]{:S(2)}, u32[]{:S(2)}) collective-permute-start(bf16[512,512]{1,0:T(8,128)(2,1)} %get-tuple-element.66), channel_id=1, source_target_pairs={{0,4},{4,0},{8,12},{12,8},{16,20},{20,16},{24,28},{28,24},{1,5},{5... | collective-permute-start | bytes 1572872 | tf_op jit(solution)/shard_map/ppermute | solution.py:21
  17.0 24.9 %collective-permute-start = (bf16[512,1024]{1,0:T(8,128)(2,1)}, bf16[512,1024]{1,0:T(8,128)(2,1)}, u32[]{:S(2)}, u32[]{:S(2)}) collective-permute-start(bf16[512,1024]{1,0:T(8,128)(2,1)} %get-tuple-element.65), channel_id=1, source_target_pairs={{0,8},{4,12},{8,0},{12,4},{16,24},{20,28},{24,16},{28,20},{1,9},{5... | collective-permute-start | bytes 3145736 | tf_op jit(solution)/shard_map/ppermute | solution.py:21
  18.6 5.6 %copy-start.20 = (s32[128,8]{0,1:T(8,128)S(1)}, s32[128,8]{0,1:T(8,128)}, u32[]{:S(2)}) copy-start(s32[128,8]{0,1:T(8,128)} %param.17) | copy-start | bytes 12292
  26.7 21.5 %copy-start.5 = (bf16[512,1024]{1,0:T(8,128)(2,1)S(1)}, bf16[512,1024]{1,0:T(8,128)(2,1)}, u32[]{:S(2)}) copy-start(bf16[512,1024]{1,0:T(8,128)(2,1)} %copy-done.4) | copy-start | bytes 3145732
  26.7 28.9 %collective-permute-start.4 = (bf16[512,1024]{1,0:T(8,128)(2,1)}, bf16[512,1024]{1,0:T(8,128)(2,1)}, u32[]{:S(2)}, u32[]{:S(2)}) collective-permute-start(bf16[512,1024]{1,0:T(8,128)(2,1)} %shard_map.143), channel_id=1, source_target_pairs={{0,4},{4,0},{8,12},{12,8},{16,20},{20,16},{24,28},{28,24},{1,5},{5... | collective-permute-start | bytes 3145736 | tf_op jit(solution)/shard_map/ppermute | solution.py:21
  44.6 17.9 %collective-permute-start.2 = (bf16[256,1024]{1,0:T(8,128)(2,1)S(1)}, bf16[256,1024]{1,0:T(8,128)(2,1)S(1)}, u32[]{:S(2)}, u32[]{:S(2)}) collective-permute-start(bf16[256,1024]{1,0:T(8,128)(2,1)S(1)} %get-tuple-element.70.refs_3_), channel_id=1, source_target_pairs={{0,4},{4,0},{8,12},{12,8},{16,20},{20,16},{24,28},{28,24},{1,5},{5... | collective-permute-start | bytes 1572872 | tf_op jit(solution)/shard_map/ppermute | solution.py:21
  45.0 14.5 %collective-permute-start.3 = (bf16[256,512]{1,0:T(8,128)(2,1)S(1)}, bf16[256,512]{1,0:T(8,128)(2,1)S(1)}, u32[]{:S(2)}, u32[]{:S(2)}) collective-permute-start(bf16[256,512]{1,0:T(8,128)(2,1)S(1)} %get-tuple-element.68.refs_2_.refs_1_), channel_id=1, source_target_pairs={{0,8},{4,12},{8,0},{12,4},{16,24},{20,28},{24,16},{28,20},{1,9},{5... | collective-permute-start | bytes 786440 | tf_op jit(solution)/shard_map/ppermute | solution.py:21
  47.0 1.2 collective-permute-start.5
  48.2 7.5 %copy-start.11 = (bf16[512,1024]{1,0:T(8,128)(2,1)S(1)}, bf16[512,1024]{1,0:T(8,128)(2,1)}, u32[]{:S(2)}) copy-start(bf16[512,1024]{1,0:T(8,128)(2,1)} %copy-done.10) | copy-start | bytes 3145732
  48.2 11.3 %copy-start.17 = (f32[256,512]{1,0:T(8,128)S(1)}, f32[256,512]{1,0:T(8,128)}, u32[]{:S(2)}) copy-start(f32[256,512]{1,0:T(8,128)} %copy-done.16) | copy-start | bytes 1572868
  59.5 4.1 %copy-start.18 = (bf16[256,1024]{1,0:T(8,128)(2,1)}, bf16[256,1024]{1,0:T(8,128)(2,1)S(1)}, u32[]{:S(2)}) copy-start(bf16[256,1024]{1,0:T(8,128)(2,1)S(1)} %get-tuple-element.74.refs_2_) | copy-start | bytes 1572868
  63.6 37.6 %collective-permute-start.7 = (bf16[512,1536]{1,0:T(8,128)(2,1)}, bf16[512,1536]{1,0:T(8,128)(2,1)}, u32[]{:S(2)}, u32[]{:S(2)}) collective-permute-start(bf16[512,1536]{1,0:T(8,128)(2,1)} %shard_map.149), channel_id=1, source_target_pairs={{0,4},{4,0},{8,12},{12,8},{16,20},{20,16},{24,28},{28,24},{1,5},{5... | collective-permute-start | bytes 4718600 | tf_op jit(solution)/shard_map/ppermute | solution.py:21
  64.1 9.9 %collective-permute-start.11 = (s32[256]{0:T(256)S(1)}, s32[256]{0:T(256)S(1)}, u32[]{:S(2)}, u32[]{:S(2)}) collective-permute-start(s32[256]{0:T(256)S(1)} %add.94.refs_4_), channel_id=1, source_target_pairs={{0,2},{1,3},{2,0},{3,1},{4,6},{5,7},{6,4},{7,5},{8,10},{9,11},{10,... | collective-permute-start | bytes 3080 | tf_op jit(solution)/shard_map/ppermute | solution.py:21
  65.6 6.5 %copy-start.19 = (bf16[256,1024]{1,0:T(8,128)(2,1)S(1)}, bf16[256,1024]{1,0:T(8,128)(2,1)}, u32[]{:S(2)}) copy-start(bf16[256,1024]{1,0:T(8,128)(2,1)} %copy-done.18) | copy-start | bytes 1572868
  65.6 26.5 %copy-start.13 = (f32[256,1024]{1,0:T(8,128)S(1)}, f32[256,1024]{1,0:T(8,128)}, u32[]{:S(2)}) copy-start(f32[256,1024]{1,0:T(8,128)} %copy-done.12) | copy-start | bytes 3145732
  72.1 20.4 %copy-start.2 = (bf16[128,7168]{1,0:T(8,128)(2,1)S(1)}, bf16[128,7168]{1,0:T(8,128)(2,1)}, u32[]{:S(2)}) copy-start(bf16[128,7168]{1,0:T(8,128)(2,1)} %refs_2_.27) | copy-start | bytes 5505028
  72.1 20.0 %collective-permute-start.10 = (bf16[256,1024]{1,0:T(8,128)(2,1)S(1)}, bf16[256,1024]{1,0:T(8,128)(2,1)S(1)}, u32[]{:S(2)}, u32[]{:S(2)}) collective-permute-start(bf16[256,1024]{1,0:T(8,128)(2,1)S(1)} %copy-done.19), channel_id=1, source_target_pairs={{0,8},{4,12},{8,0},{12,4},{16,24},{20,28},{24,16},{28,20},{1,9},{5... | collective-permute-start | bytes 1572872 | tf_op jit(solution)/shard_map/ppermute | solution.py:21
  72.5 56.7 %collective-permute-start.6 = (bf16[512,1280]{1,0:T(8,128)(2,1)}, bf16[512,1280]{1,0:T(8,128)(2,1)S(1)}, u32[]{:S(2)}, u32[]{:S(2)}) collective-permute-start(bf16[512,1280]{1,0:T(8,128)(2,1)} %get-tuple-element.78), channel_id=1, source_target_pairs={{0,4},{4,0},{8,12},{12,8},{16,20},{20,16},{24,28},{28,24},{1,5},{5... | collective-permute-start | bytes 3932168 | tf_op jit(solution)/shard_map/ppermute | solution.py:21
  74.0 19.2 %collective-permute-start.8 = (bf16[128,1024]{1,0:T(8,128)(2,1)S(1)}, bf16[128,1024]{1,0:T(8,128)(2,1)S(1)}, u32[]{:S(2)}, u32[]{:S(2)}) collective-permute-start(bf16[128,1024]{1,0:T(8,128)(2,1)S(1)} %get-tuple-element.76.refs_3_.refs_1_), channel_id=1, source_target_pairs={{0,16},{4,20},{8,24},{12,28},{16,0},{20,4},{24,8},{28,12},{1,17},{... | collective-permute-start | bytes 786440 | tf_op jit(solution)/shard_map/ppermute | solution.py:21
  76.7 15.8 %collective-permute-start.9 = (bf16[128,512]{1,0:T(8,128)(2,1)S(1)}, bf16[128,512]{1,0:T(8,128)(2,1)S(1)}, u32[]{:S(2)}, u32[]{:S(2)}) collective-permute-start(bf16[128,512]{1,0:T(8,128)(2,1)S(1)} %get-tuple-element.75.refs_2_), channel_id=1, source_target_pairs={{0,16},{4,20},{8,24},{12,28},{16,0},{20,4},{24,8},{28,12},{1,17},{... | collective-permute-start | bytes 393224 | tf_op jit(solution)/shard_map/ppermute | solution.py:21
  92.4 18.0 %collective-permute-start.13 = (bf16[128,1024]{1,0:T(8,128)(2,1)S(1)}, bf16[128,1024]{1,0:T(8,128)(2,1)S(1)}, u32[]{:S(2)}, u32[]{:S(2)}) collective-permute-start(bf16[128,1024]{1,0:T(8,128)(2,1)S(1)} %get-tuple-element.83.refs_3_), channel_id=1, source_target_pairs={{0,16},{4,20},{8,24},{12,28},{16,0},{20,4},{24,8},{28,12},{1,17},{... | collective-permute-start | bytes 786440 | tf_op jit(solution)/shard_map/ppermute | solution.py:21
  93.2 8.0 %copy-start.7 = (bf16[512,1536]{1,0:T(8,128)(2,1)S(1)}, bf16[512,1536]{1,0:T(8,128)(2,1)}, u32[]{:S(2)}) copy-start(bf16[512,1536]{1,0:T(8,128)(2,1)} %get-tuple-element.73.refs_2_.refs_0_) | copy-start | bytes 4718596
  103.8 18.5 %collective-permute-start.12 = (bf16[256,1536]{1,0:T(8,128)(2,1)S(1)}, bf16[256,1536]{1,0:T(8,128)(2,1)S(1)}, u32[]{:S(2)}, u32[]{:S(2)}) collective-permute-start(bf16[256,1536]{1,0:T(8,128)(2,1)S(1)} %get-tuple-element.88.refs_3_), channel_id=1, source_target_pairs={{0,8},{4,12},{8,0},{12,4},{16,24},{20,28},{24,16},{28,20},{1,9},{5... | collective-permute-start | bytes 2359304 | tf_op jit(solution)/shard_map/ppermute | solution.py:21
  109.8 42.0 %collective-permute-start.15 = (bf16[512,1024]{1,0:T(8,128)(2,1)}, bf16[512,1024]{1,0:T(8,128)(2,1)}, u32[]{:S(2)}, u32[]{:S(2)}) collective-permute-start(bf16[512,1024]{1,0:T(8,128)(2,1)} %get-tuple-element.97), channel_id=1, source_target_pairs={{0,4},{4,0},{8,12},{12,8},{16,20},{20,16},{24,28},{28,24},{1,5},{5... | collective-permute-start | bytes 3145736 | tf_op jit(solution)/shard_map/ppermute | solution.py:21
  129.9 19.9 %collective-permute-start.16 = (bf16[256,1280]{1,0:T(8,128)(2,1)S(1)}, bf16[256,1280]{1,0:T(8,128)(2,1)S(1)}, u32[]{:S(2)}, u32[]{:S(2)}) collective-permute-start(bf16[256,1280]{1,0:T(8,128)(2,1)S(1)} %get-tuple-element.94.refs_3_), channel_id=1, source_target_pairs={{0,8},{4,12},{8,0},{12,4},{16,24},{20,28},{24,16},{28,20},{1,9},{5... | collective-permute-start | bytes 1966088 | tf_op jit(solution)/shard_map/ppermute | solution.py:21
  130.5 17.3 %collective-permute-start.17 = (bf16[128,1536]{1,0:T(8,128)(2,1)S(1)}, bf16[128,1536]{1,0:T(8,128)(2,1)S(1)}, u32[]{:S(2)}, u32[]{:S(2)}) collective-permute-start(bf16[128,1536]{1,0:T(8,128)(2,1)S(1)} %get-tuple-element.93.refs_2_), channel_id=1, source_target_pairs={{0,16},{4,20},{8,24},{12,28},{16,0},{20,4},{24,8},{28,12},{1,17},{... | collective-permute-start | bytes 1179656 | tf_op jit(solution)/shard_map/ppermute | solution.py:21
  137.0 34.0 %collective-permute-start.14 = (bf16[512,768]{1,0:T(8,128)(2,1)S(1)}, bf16[512,768]{1,0:T(8,128)(2,1)S(1)}, u32[]{:S(2)}, u32[]{:S(2)}) collective-permute-start(bf16[512,768]{1,0:T(8,128)(2,1)S(1)} %get-tuple-element.96), channel_id=1, source_target_pairs={{0,4},{4,0},{8,12},{12,8},{16,20},{20,16},{24,28},{28,24},{1,5},{5... | collective-permute-start | bytes 2359304 | tf_op jit(solution)/shard_map/ppermute | solution.py:21
  153.2 17.5 %collective-permute-start.18 = (bf16[256,1024]{1,0:T(8,128)(2,1)S(1)}, bf16[256,1024]{1,0:T(8,128)(2,1)S(1)}, u32[]{:S(2)}, u32[]{:S(2)}) collective-permute-start(bf16[256,1024]{1,0:T(8,128)(2,1)S(1)} %get-tuple-element.104.refs_4_), channel_id=1, source_target_pairs={{0,8},{4,12},{8,0},{12,4},{16,24},{20,28},{24,16},{28,20},{1,9},{5... | collective-permute-start | bytes 1572872 | tf_op jit(solution)/shard_map/ppermute | solution.py:21
  155.8 12.7 %collective-permute-start.19 = (bf16[128,1280]{1,0:T(8,128)(2,1)S(1)}, bf16[128,1280]{1,0:T(8,128)(2,1)S(1)}, u32[]{:S(2)}, u32[]{:S(2)}) collective-permute-start(bf16[128,1280]{1,0:T(8,128)(2,1)S(1)} %get-tuple-element.102.refs_2_), channel_id=1, source_target_pairs={{0,16},{4,20},{8,24},{12,28},{16,0},{20,4},{24,8},{28,12},{1,17},{... | collective-permute-start | bytes 983048 | tf_op jit(solution)/shard_map/ppermute | solution.py:21
  171.5 15.4 %collective-permute-start.20 = (bf16[256,768]{1,0:T(8,128)(2,1)S(1)}, bf16[256,768]{1,0:T(8,128)(2,1)S(1)}, u32[]{:S(2)}, u32[]{:S(2)}) collective-permute-start(bf16[256,768]{1,0:T(8,128)(2,1)S(1)} %get-tuple-element.110.refs_2_.refs_1_), channel_id=1, source_target_pairs={{0,8},{4,12},{8,0},{12,4},{16,24},{20,28},{24,16},{28,20},{1,9},{5... | collective-permute-start | bytes 1179656 | tf_op jit(solution)/shard_map/ppermute | solution.py:21
  174.7 15.5 %collective-permute-start.22 = (bf16[128,1024]{1,0:T(8,128)(2,1)S(1)}, bf16[128,1024]{1,0:T(8,128)(2,1)S(1)}, u32[]{:S(2)}, u32[]{:S(2)}) collective-permute-start(bf16[128,1024]{1,0:T(8,128)(2,1)S(1)} %get-tuple-element.108.refs_2_), channel_id=1, source_target_pairs={{0,16},{4,20},{8,24},{12,28},{16,0},{20,4},{24,8},{28,12},{1,17},{... | collective-permute-start | bytes 786440 | tf_op jit(solution)/shard_map/ppermute | solution.py:21
  187.2 13.3 %collective-permute-start.21 = (bf16[128,768]{1,0:T(8,128)(2,1)S(1)}, bf16[128,768]{1,0:T(8,128)(2,1)S(1)}, u32[]{:S(2)}, u32[]{:S(2)}) collective-permute-start(bf16[128,768]{1,0:T(8,128)(2,1)S(1)} %get-tuple-element.112.refs_4_), channel_id=1, source_target_pairs={{0,16},{4,20},{8,24},{12,28},{16,0},{20,4},{24,8},{28,12},{1,17},{... | collective-permute-start | bytes 589832 | tf_op jit(solution)/shard_map/ppermute | solution.py:21
  187.7 20.5 %collective-permute-start.28 = (bf16[8,7296]{1,0:T(8,128)(2,1)S(1)}, bf16[8,7296]{1,0:T(8,128)(2,1)S(1)}, u32[]{:S(2)}, u32[]{:S(2)}) collective-permute-start(bf16[8,7296]{1,0:T(8,128)(2,1)S(1)} %shard_map.171), channel_id=1, source_target_pairs={{0,16},{4,20},{8,24},{12,28},{16,0},{20,4},{24,8},{28,12},{1,17},{... | collective-permute-start | bytes 350216 | tf_op jit(solution)/shard_map/ppermute | solution.py:21
  203.4 20.5 %copy-start.23 = (s32[8]{0:T(128)S(1)}, s32[8]{0:T(128)}, u32[]{:S(2)}) copy-start(s32[8]{0:T(128)} %constant.81.clone) | copy-start | bytes 100
  204.7 12.9 %all-to-all-start = ((bf16[8,2,7296]{2,1,0:T(2,128)(2,1)}), bf16[8,2,7296]{2,1,0:T(2,128)(2,1)S(1)}, u32[]{:S(2)}, u32[]{:S(2)}) async-start(bf16[8,2,7296]{2,1,0:T(2,128)(2,1)} %reshape.64), calls=%async_computation | async-start | bytes 466944 | tf_op jit(solution)/shard_map/all_to_all | solution.py:347
  208.3 11.2 %collective-permute-start.29 = (bf16[16,7296]{1,0:T(8,128)(2,1)S(1)}, bf16[16,7296]{1,0:T(8,128)(2,1)S(1)}, u32[]{:S(2)}, u32[]{:S(2)}) collective-permute-start(bf16[16,7296]{1,0:T(8,128)(2,1)S(1)} %pad_maximum_fusion.9), channel_id=1, source_target_pairs={{0,8},{4,12},{8,0},{12,4},{16,24},{20,28},{24,16},{28,20},{1,9},{5... | collective-permute-start | bytes 700424 | tf_op jit(solution)/shard_map/ppermute | solution.py:21
  217.7 6.1 %collective-permute-start.23 = (bf16[16,7296]{1,0:T(8,128)(2,1)S(1)}, bf16[16,7296]{1,0:T(8,128)(2,1)S(1)}, u32[]{:S(2)}, u32[]{:S(2)}) collective-permute-start(bf16[16,7296]{1,0:T(8,128)(2,1)S(1)} %reshape.65.refs_0_), channel_id=1, source_target_pairs={{0,2},{1,3},{2,0},{3,1},{4,6},{5,7},{6,4},{7,5},{8,10},{9,11},{10,... | collective-permute-start | bytes 700424 | tf_op jit(solution)/shard_map/ppermute | solution.py:21
  219.5 20.9 %collective-permute-start.30 = (bf16[32,7296]{1,0:T(8,128)(2,1)S(1)}, bf16[32,7296]{1,0:T(8,128)(2,1)S(1)}, u32[]{:S(2)}, u32[]{:S(2)}) collective-permute-start(bf16[32,7296]{1,0:T(8,128)(2,1)S(1)} %pad_maximum_fusion.8), channel_id=1, source_target_pairs={{0,4},{4,0},{8,12},{12,8},{16,20},{20,16},{24,28},{28,24},{1,5},{5... | collective-permute-start | bytes 1400840 | tf_op jit(solution)/shard_map/ppermute | solution.py:21
  221.0 3.0 %collective-permute-start.24 = (bf16[16,7296]{1,0:T(8,128)(2,1)S(1)}, bf16[16,7296]{1,0:T(8,128)(2,1)S(1)}, u32[]{:S(2)}, u32[]{:S(2)}) collective-permute-start(bf16[16,7296]{1,0:T(8,128)(2,1)S(1)} %reshape.65.refs_0_), channel_id=1, source_target_pairs={{0,1},{1,0},{2,3},{3,2},{4,5},{5,4},{6,7},{7,6},{8,9},{9,8},{10,11... | collective-permute-start | bytes 700424 | tf_op jit(solution)/shard_map/ppermute | solution.py:21
  223.8 1.5 collective-permute-start.25
  240.2 3.6 %collective-permute-start.26 = (bf16[32,7168]{1,0:T(8,128)(2,1)S(1)}, bf16[32,7168]{1,0:T(8,128)(2,1)S(1)}, u32[]{:S(2)}, u32[]{:S(2)}) collective-permute-start(bf16[32,7168]{1,0:T(8,128)(2,1)S(1)} %get-tuple-element.119), channel_id=1, source_target_pairs={{0,1},{1,0},{2,3},{3,2},{4,5},{5,4},{6,7},{7,6},{8,9},{9,8},{10,11... | collective-permute-start | bytes 1376264 | tf_op jit(solution)/shard_map/ppermute | solution.py:21
  240.9 15.4 %copy-start.22 = (f32[256]{0:T(256)S(1)}, f32[256]{0:T(256)}, u32[]{:S(2)}) copy-start(f32[256]{0:T(256)} %param.16) | copy-start | bytes 3076
  241.0 1.3 collective-permute-start.31
  242.3 3.7 %collective-permute-start.32 = (f32[16,128]{1,0:T(8,128)S(1)}, f32[16,128]{1,0:T(8,128)S(1)}, u32[]{:S(2)}, u32[]{:S(2)}) collective-permute-start(f32[16,128]{1,0:T(8,128)S(1)} %slice.42), channel_id=1, source_target_pairs={{0,2},{1,3},{2,0},{3,1},{4,6},{5,7},{6,4},{7,5},{8,10},{9,11},{10,... | collective-permute-start | bytes 24584 | tf_op jit(solution)/shard_map/ppermute | solution.py:21
  243.8 22.4 %copy-start.1 = (bf16[7168,32]{0,1:T(8,128)(2,1)S(1)}, bf16[7168,32]{0,1:T(8,128)(2,1)}, u32[]{:S(2)}) copy-start(bf16[7168,32]{0,1:T(8,128)(2,1)} %param.15) | copy-start | bytes 1376260
  243.8 7.6 %collective-permute-start.27 = (bf16[16,7168]{1,0:T(8,128)(2,1)S(1)}, bf16[16,7168]{1,0:T(8,128)(2,1)S(1)}, u32[]{:S(2)}, u32[]{:S(2)}) collective-permute-start(bf16[16,7168]{1,0:T(8,128)(2,1)S(1)} %get-tuple-element.121), channel_id=1, source_target_pairs={{0,2},{1,3},{2,0},{3,1},{4,6},{5,7},{6,4},{7,5},{8,10},{9,11},{10,... | collective-permute-start | bytes 688136 | tf_op jit(solution)/shard_map/ppermute | solution.py:21
  252.4 11.8 %all-to-all-start.1 = ((bf16[8,2,7168]{2,1,0:T(2,128)(2,1)}), bf16[8,2,7168]{2,1,0:T(2,128)(2,1)S(1)}, u32[]{:S(2)}, u32[]{:S(2)}) async-start(bf16[8,2,7168]{2,1,0:T(2,128)(2,1)} %reshape.66), calls=%async_computation.1 | async-start | bytes 458752 | tf_op jit(solution)/shard_map/all_to_all | solution.py:462
  (11 other events, 18.0 us)

commit v3 on v2

--- a/solution.py
+++ b/solution.py
@@ -317,11 +317,11 @@
     marks = finish(("y2",), marks)
     marks = third(("y3",), marks)
     marks = second(("y4",), marks)
+    marks = third(("y4",), marks)
     marks = finish(("y3",), marks)
-    marks = third(("y4",), marks)
     marks = second(("y5",), marks)
+    marks = third(("y5",), marks)
     router_all = router_gather(router_part, marks)
-    marks = third(("y5",), marks)
     marks = finish(("y4",), marks)
     finish(("y5",), marks)
     (hidden_out,) = hidden

time: 268 us -> 270 us (level)
  waiting for transfers between devices: 130 us -> 133 us
  transfers between devices with their start and end apart: 35 -> 35, of which waited for: 22 -> 21; matrix products, arithmetic and copies ran while one was open for 1% -> 1% of each run, Pallas kernels for 26% -> 26%
where the time goes in v3:
time: 270 us; the launch traced here: 268 us
  waiting for transfers between devices  133 us (49%)
  Pallas kernels  74.4 us (28%)
  starting transfers between devices  43 us (16%)
  local copies, waits for them, and re-layouts  11.7 us (4%)
  other arithmetic  3.17 us (1%)
    ppermute x33, waiting for transfers between devices, swap(): return lax.ppermute(value, axis, [(i, i ^ bit) for i in range(size)])  118 us
    pallas_call x36, Pallas kernels, run(): pl.pallas_call(inner, grid=grid, in_specs=[spec for _, spec in ins] + [AN...  74.4 us
    ppermute x33, starting transfers between devices, swap(): return lax.ppermute(value, axis, [(i, i ^ bit) for i in range(size)])  35.6 us
    unnamed x49, local copies, waits for them, and re-layouts  7.8 us
    all_to_all x1, waiting for transfers between devices, on_device(): lax.all_to_all(normed.reshape(tp_count, CAP, width + lanes), 'tp', split_...  7.52 us
    all_to_all x1, waiting for transfers between devices, on_device(): lax.all_to_all(summed.reshape(tp_count, CAP, width), 'tp', split_axis=0,...  7.36 us
  transfers between devices with their start and end apart: 35, of which 21 were waited for; matrix products, arithmetic and copies ran while one was open for 1% of the time, Pallas kernels for 26%

profile of v3, /device:TPU:0, one launch (start us, length us, event | category | flops | bytes accessed | tf_op | source)
XLA Modules:
  0.0 268.3 jit_solution(14736600457486465756)
XLA Ops:
  0.7 1.7 constant_dynamic-slice_fusion.3
  2.4 1.4 pad_maximum_fusion
  3.9 3.6 %shard_map.138 = (bf16[512,512]{1,0:T(8,128)(2,1)S(1)}, bf16[512,512]{1,0:T(8,128)(2,1)}) custom-call(bf16[512,1024]{1,0:T(8,128)(2,1)S(1)} %get-tuple-element.133.refs_0_, bf16[512,1024]{1,0:T(8,128)(2,1)S(1)} %get-tuple-element.135.refs_1_, bf16[1024,7168]{1,0:T(8,128)(2,1)} %refs_2_.23), custom_call_target="tpu_custom_call" | custom-call | flops 1 | bytes 1 | tf_op jit(solution)/shard_map/pallas_call | solution.py:44
  7.5 3.0 %collective-permute-start.1 = (bf16[512,512]{1,0:T(8,128)(2,1)}, bf16[512,512]{1,0:T(8,128)(2,1)}, u32[]{:S(2)}, u32[]{:S(2)}) collective-permute-start(bf16[512,512]{1,0:T(8,128)(2,1)} %get-tuple-element.66), channel_id=1, source_target_pairs={{0,4},{4,0},{8,12},{12,8},{16,20},{20,16},{24,28},{28,24},{1,5},{5... | collective-permute-start | bytes 1572872 | tf_op jit(solution)/shard_map/ppermute | solution.py:21
  10.5 5.6 %shard_map.139 = (bf16[512,1024]{1,0:T(8,128)(2,1)S(1)}, bf16[512,1024]{1,0:T(8,128)(2,1)}) custom-call(bf16[512,1024]{1,0:T(8,128)(2,1)S(1)} %get-tuple-element.134.refs_0_, bf16[512,1024]{1,0:T(8,128)(2,1)} %get-tuple-element.132.refs_1_, bf16[1024,7168]{1,0:T(8,128)(2,1)} %refs_2_.23, bf16[512,512]{1,0:T(8,128)(2,1)S(1)} %get-tuple-element.63.refs_3_.refs_0_), custom_call_target="tpu_custom_call" | custom-call | flops 1 | bytes 1 | tf_op jit(solution)/shard_map/pallas_call | solution.py:44
  17.0 1.6 collective-permute-start
  18.6 5.6 %shard_map.140 = (bf16[512,1024]{1,0:T(8,128)(2,1)S(1)}, bf16[512,1024]{1,0:T(8,128)(2,1)}) custom-call(bf16[512,1024]{1,0:T(8,128)(2,1)S(1)} %get-tuple-element.133.refs_0_, bf16[512,1024]{1,0:T(8,128)(2,1)} %copy-done.4, bf16[1024,7168]{1,0:T(8,128)(2,1)} %refs_2_.23, bf16[512,1024]{1,0:T(8,128)(2,1)} %copy-done.8), custom_call_target="tpu_custom_call" | custom-call | flops 1 | bytes 1 | tf_op jit(solution)/shard_map/pallas_call | solution.py:44
  28.0 14.0 %collective-permute-done.refs_1_ = bf16[512,1024]{1,0:T(8,128)(2,1)} collective-permute-done((bf16[512,1024]{1,0:T(8,128)(2,1)}, bf16[512,1024]{1,0:T(8,128)(2,1)}, u32[]{:S(2)}, u32[]{:S(2)}) %collective-permute-start) | collective-permute-done | bytes 1048608 | tf_op jit(solution)/shard_map/ppermute | solution.py:21
  45.0 1.7 collective-permute-start.3
  48.2 7.5 %shard_map.144 = (bf16[512,1536]{1,0:T(8,128)(2,1)}, bf16[512,1536]{1,0:T(8,128)(2,1)}) custom-call(bf16[512,1024]{1,0:T(8,128)(2,1)S(1)} %get-tuple-element.133.refs_0_, bf16[512,1024]{1,0:T(8,128)(2,1)S(1)} %copy-done.5, bf16[1024,7168]{1,0:T(8,128)(2,1)} %refs_2_.23, bf16[256,1024]{1,0:T(8,128)(2,1)S(1)} %get-tuple-element.70.refs_3_, s32[256]{0:T(256)S(1)} %add.94.refs_4_), custom_call_target="tpu_custom_call" | custom-call | flops 1 | bytes 1 | tf_op jit(solution)/shard_map/pallas_call | solution.py:44
  59.6 2.9 %collective-permute-done.2.refs_1_ = bf16[256,1024]{1,0:T(8,128)(2,1)S(1)} collective-permute-done((bf16[256,1024]{1,0:T(8,128)(2,1)S(1)}, bf16[256,1024]{1,0:T(8,128)(2,1)S(1)}, u32[]{:S(2)}, u32[]{:S(2)}) %collective-permute-start.2) | collective-permute-done | bytes 524320 | tf_op jit(solution)/shard_map/ppermute | solution.py:21
  64.1 1.5 collective-permute-start.11
  65.6 6.4 %shard_map.148 = (bf16[512,1280]{1,0:T(8,128)(2,1)S(1)}, bf16[512,1280]{1,0:T(8,128)(2,1)}) custom-call(bf16[512,1024]{1,0:T(8,128)(2,1)S(1)} %get-tuple-element.133.refs_0_, bf16[512,1024]{1,0:T(8,128)(2,1)S(1)} %copy-done.5, bf16[1024,7168]{1,0:T(8,128)(2,1)} %refs_2_.23, bf16[128,1024]{1,0:T(8,128)(2,1)S(1)} %get-tuple-element.76.refs_3_.refs_1_), custom_call_target="tpu_custom_call" | custom-call | flops 1 | bytes 1 | tf_op jit(solution)/shard_map/pallas_call | solution.py:44
  72.5 1.5 collective-permute-start.6
  74.0 2.7 collective-permute-start.8
  77.1 15.0 %collective-permute-done.10.refs_1_ = bf16[256,1024]{1,0:T(8,128)(2,1)S(1)} collective-permute-done((bf16[256,1024]{1,0:T(8,128)(2,1)S(1)}, bf16[256,1024]{1,0:T(8,128)(2,1)S(1)}, u32[]{:S(2)}, u32[]{:S(2)}) %collective-permute-start.10) | collective-permute-done | bytes 524320 | tf_op jit(solution)/shard_map/ppermute | solution.py:21
  94.1 7.1 %collective-permute-done.7.refs_1_ = bf16[512,1536]{1,0:T(8,128)(2,1)} collective-permute-done((bf16[512,1536]{1,0:T(8,128)(2,1)}, bf16[512,1536]{1,0:T(8,128)(2,1)}, u32[]{:S(2)}, u32[]{:S(2)}) %collective-permute-start.7) | collective-permute-done | bytes 1572896 | tf_op jit(solution)/shard_map/ppermute | solution.py:21
  101.2 2.5 shard_map.153
  104.3 5.6 %shard_map.154 = (bf16[512,1024]{1,0:T(8,128)(2,1)S(1)}, bf16[512,1024]{1,0:T(8,128)(2,1)}) custom-call(bf16[512,1024]{1,0:T(8,128)(2,1)S(1)} %get-tuple-element.133.refs_0_, bf16[512,1024]{1,0:T(8,128)(2,1)} %copy-done.4, bf16[1024,7168]{1,0:T(8,128)(2,1)} %refs_2_.23, bf16[256,1536]{1,0:T(8,128)(2,1)S(1)} %get-tuple-element.88.refs_3_), custom_call_target="tpu_custom_call" | custom-call | flops 1 | bytes 1 | tf_op jit(solution)/shard_map/pallas_call | solution.py:44
  111.3 11.0 %collective-permute-done.12.refs_1_ = bf16[256,1536]{1,0:T(8,128)(2,1)S(1)} collective-permute-done((bf16[256,1536]{1,0:T(8,128)(2,1)S(1)}, bf16[256,1536]{1,0:T(8,128)(2,1)S(1)}, u32[]{:S(2)}, u32[]{:S(2)}) %collective-permute-start.12) | collective-permute-done | bytes 786464 | tf_op jit(solution)/shard_map/ppermute | solution.py:21
  122.7 6.6 %collective-permute-done.6.refs_1_ = bf16[512,1280]{1,0:T(8,128)(2,1)S(1)} collective-permute-done((bf16[512,1280]{1,0:T(8,128)(2,1)}, bf16[512,1280]{1,0:T(8,128)(2,1)S(1)}, u32[]{:S(2)}, u32[]{:S(2)}) %collective-permute-start.6) | collective-permute-done | bytes 1310752 | tf_op jit(solution)/shard_map/ppermute | solution.py:21
  130.5 2.6 collective-permute-start.16
  133.0 4.0 %shard_map.158 = (bf16[512,768]{1,0:T(8,128)(2,1)S(1)}, bf16[512,768]{1,0:T(8,128)(2,1)S(1)}) custom-call(bf16[512,1024]{1,0:T(8,128)(2,1)S(1)} %get-tuple-element.133.refs_0_, bf16[512,1024]{1,0:T(8,128)(2,1)} %copy-done.4, bf16[1024,7168]{1,0:T(8,128)(2,1)} %refs_2_.23, bf16[256,1280]{1,0:T(8,128)(2,1)S(1)} %get-tuple-element.94.refs_3_), custom_call_target="tpu_custom_call" | custom-call | flops 1 | bytes 1 | tf_op jit(solution)/shard_map/pallas_call | solution.py:44
  137.6 10.1 %collective-permute-done.16.refs_1_ = bf16[128,1536]{1,0:T(8,128)(2,1)S(1)} collective-permute-done((bf16[128,1536]{1,0:T(8,128)(2,1)S(1)}, bf16[128,1536]{1,0:T(8,128)(2,1)S(1)}, u32[]{:S(2)}, u32[]{:S(2)}) %collective-permute-start.16) | collective-permute-done | bytes 393248 | tf_op jit(solution)/shard_map/ppermute | solution.py:21
  147.8 1.5 shard_map.159
  150.2 1.6 collective-permute-done.18.refs_1_
  153.2 2.6 collective-permute-start.19
  156.3 14.4 %collective-permute-done.19.refs_1_ = bf16[256,1024]{1,0:T(8,128)(2,1)S(1)} collective-permute-done((bf16[256,1024]{1,0:T(8,128)(2,1)S(1)}, bf16[256,1024]{1,0:T(8,128)(2,1)S(1)}, u32[]{:S(2)}, u32[]{:S(2)}) %collective-permute-start.19) | collective-permute-done | bytes 524320 | tf_op jit(solution)/shard_map/ppermute | solution.py:21
  171.0 2.1 shard_map.163
  174.4 2.1 collective-permute-start.22
  176.4 12.5 %collective-permute-done.20.refs_1_ = bf16[256,768]{1,0:T(8,128)(2,1)S(1)} collective-permute-done((bf16[256,768]{1,0:T(8,128)(2,1)S(1)}, bf16[256,768]{1,0:T(8,128)(2,1)S(1)}, u32[]{:S(2)}, u32[]{:S(2)}) %collective-permute-start.20) | collective-permute-done | bytes 393248 | tf_op jit(solution)/shard_map/ppermute | solution.py:21
  189.8 2.4 collective-permute-start.28
  192.2 1.5 shard_map.166
  193.7 8.8 %collective-permute-done.21.refs_1_ = bf16[128,768]{1,0:T(8,128)(2,1)S(1)} collective-permute-done((bf16[128,768]{1,0:T(8,128)(2,1)S(1)}, bf16[128,768]{1,0:T(8,128)(2,1)S(1)}, u32[]{:S(2)}, u32[]{:S(2)}) %collective-permute-start.21) | collective-permute-done | bytes 196640 | tf_op jit(solution)/shard_map/ppermute | solution.py:21
  203.9 1.5 copy-done.3
  206.7 3.6 %all-to-all-start = ((bf16[8,2,7296]{2,1,0:T(2,128)(2,1)}), bf16[8,2,7296]{2,1,0:T(2,128)(2,1)S(1)}, u32[]{:S(2)}, u32[]{:S(2)}) async-start(bf16[8,2,7296]{2,1,0:T(2,128)(2,1)} %reshape.64), calls=%async_computation | async-start | bytes 466944 | tf_op jit(solution)/shard_map/all_to_all | solution.py:347
  210.4 1.8 collective-permute-start.29
  212.2 7.5 %all-to-all-done = bf16[8,2,7296]{2,1,0:T(2,128)(2,1)S(1)} async-done(((bf16[8,2,7296]{2,1,0:T(2,128)(2,1)}), bf16[8,2,7296]{2,1,0:T(2,128)(2,1)S(1)}, u32[]{:S(2)}, u32[]{:S(2)}) %all-to-all-start) | async-done | bytes 233504 | tf_op jit(solution)/shard_map/all_to_all | solution.py:347
  219.8 1.6 collective-permute-start.23
  221.6 1.5 collective-permute-start.30
  223.1 2.8 %collective-permute-done.23.refs_1_ = bf16[16,7296]{1,0:T(8,128)(2,1)S(1)} collective-permute-done((bf16[16,7296]{1,0:T(8,128)(2,1)S(1)}, bf16[16,7296]{1,0:T(8,128)(2,1)S(1)}, u32[]{:S(2)}, u32[]{:S(2)}) %collective-permute-start.23) | collective-permute-done | bytes 233504 | tf_op jit(solution)/shard_map/ppermute | solution.py:21
  227.4 14.8 %shard_map.169 = (bf16[32,7168]{1,0:T(8,128)(2,1)S(1)}, f32[32,7168]{1,0:T(8,128)S(1)}) custom-call(bf16[16,7296]{1,0:T(8,128)(2,1)S(1)} %reshape.65.refs_0_, bf16[16,7296]{1,0:T(8,128)(2,1)S(1)} %collective-permute-done.23.refs_1_, bf16[16,7296]{1,0:T(8,128)(2,1)S(1)} %collective-permute-done.24.refs_2_, ...), custom_call_target="tpu_custom_call" | custom-call | flops 1 | bytes 1 | tf_op jit(solution)/shard_map/pallas_call | solution.py:44
  244.3 1.5 collective-permute-start.32
  246.5 1.5 collective-permute-done.32
  248.0 5.6 %collective-permute-done.27.refs_1_ = bf16[16,7168]{1,0:T(8,128)(2,1)S(1)} collective-permute-done((bf16[16,7168]{1,0:T(8,128)(2,1)S(1)}, bf16[16,7168]{1,0:T(8,128)(2,1)S(1)}, u32[]{:S(2)}, u32[]{:S(2)}) %collective-permute-start.27) | collective-permute-done | bytes 229408 | tf_op jit(solution)/shard_map/ppermute | solution.py:21
  254.5 3.8 %all-to-all-start.1 = ((bf16[8,2,7168]{2,1,0:T(2,128)(2,1)}), bf16[8,2,7168]{2,1,0:T(2,128)(2,1)S(1)}, u32[]{:S(2)}, u32[]{:S(2)}) async-start(bf16[8,2,7168]{2,1,0:T(2,128)(2,1)} %reshape.66), calls=%async_computation.1 | async-start | bytes 458752 | tf_op jit(solution)/shard_map/all_to_all | solution.py:462
  259.0 7.4 %all-to-all-done.1 = bf16[8,2,7168]{2,1,0:T(2,128)(2,1)S(1)} async-done(((bf16[8,2,7168]{2,1,0:T(2,128)(2,1)}), bf16[8,2,7168]{2,1,0:T(2,128)(2,1)S(1)}, u32[]{:S(2)}, u32[]{:S(2)}) %all-to-all-start.1) | async-done | bytes 229408 | tf_op jit(solution)/shard_map/all_to_all | solution.py:462
  266.3 1.9 fusion
  (152 shorter events, 35.6 us)
Async XLA Ops:
  0.6 65.0 %copy-start = (bf16[7168,32]{0,1:T(8,128)(2,1)S(1)}, bf16[7168,32]{0,1:T(8,128)(2,1)}, u32[]{:S(2)}) copy-start(bf16[7168,32]{0,1:T(8,128)(2,1)} %param.15) | copy-start | bytes 1376260
  7.5 17.2 %collective-permute-start.1 = (bf16[512,512]{1,0:T(8,128)(2,1)}, bf16[512,512]{1,0:T(8,128)(2,1)}, u32[]{:S(2)}, u32[]{:S(2)}) collective-permute-start(bf16[512,512]{1,0:T(8,128)(2,1)} %get-tuple-element.66), channel_id=1, source_target_pairs={{0,4},{4,0},{8,12},{12,8},{16,20},{20,16},{24,28},{28,24},{1,5},{5... | collective-permute-start | bytes 1572872 | tf_op jit(solution)/shard_map/ppermute | solution.py:21
  17.0 24.9 %collective-permute-start = (bf16[512,1024]{1,0:T(8,128)(2,1)}, bf16[512,1024]{1,0:T(8,128)(2,1)}, u32[]{:S(2)}, u32[]{:S(2)}) collective-permute-start(bf16[512,1024]{1,0:T(8,128)(2,1)} %get-tuple-element.65), channel_id=1, source_target_pairs={{0,8},{4,12},{8,0},{12,4},{16,24},{20,28},{24,16},{28,20},{1,9},{5... | collective-permute-start | bytes 3145736 | tf_op jit(solution)/shard_map/ppermute | solution.py:21
  18.6 5.6 %copy-start.20 = (s32[128,8]{0,1:T(8,128)S(1)}, s32[128,8]{0,1:T(8,128)}, u32[]{:S(2)}) copy-start(s32[128,8]{0,1:T(8,128)} %param.17) | copy-start | bytes 12292
  26.7 21.5 %copy-start.5 = (bf16[512,1024]{1,0:T(8,128)(2,1)S(1)}, bf16[512,1024]{1,0:T(8,128)(2,1)}, u32[]{:S(2)}) copy-start(bf16[512,1024]{1,0:T(8,128)(2,1)} %copy-done.4) | copy-start | bytes 3145732
  26.7 28.9 %collective-permute-start.4 = (bf16[512,1024]{1,0:T(8,128)(2,1)}, bf16[512,1024]{1,0:T(8,128)(2,1)}, u32[]{:S(2)}, u32[]{:S(2)}) collective-permute-start(bf16[512,1024]{1,0:T(8,128)(2,1)} %shard_map.143), channel_id=1, source_target_pairs={{0,4},{4,0},{8,12},{12,8},{16,20},{20,16},{24,28},{28,24},{1,5},{5... | collective-permute-start | bytes 3145736 | tf_op jit(solution)/shard_map/ppermute | solution.py:21
  44.6 17.9 %collective-permute-start.2 = (bf16[256,1024]{1,0:T(8,128)(2,1)S(1)}, bf16[256,1024]{1,0:T(8,128)(2,1)S(1)}, u32[]{:S(2)}, u32[]{:S(2)}) collective-permute-start(bf16[256,1024]{1,0:T(8,128)(2,1)S(1)} %get-tuple-element.70.refs_3_), channel_id=1, source_target_pairs={{0,4},{4,0},{8,12},{12,8},{16,20},{20,16},{24,28},{28,24},{1,5},{5... | collective-permute-start | bytes 1572872 | tf_op jit(solution)/shard_map/ppermute | solution.py:21
  45.0 14.5 %collective-permute-start.3 = (bf16[256,512]{1,0:T(8,128)(2,1)S(1)}, bf16[256,512]{1,0:T(8,128)(2,1)S(1)}, u32[]{:S(2)}, u32[]{:S(2)}) collective-permute-start(bf16[256,512]{1,0:T(8,128)(2,1)S(1)} %get-tuple-element.68.refs_2_.refs_1_), channel_id=1, source_target_pairs={{0,8},{4,12},{8,0},{12,4},{16,24},{20,28},{24,16},{28,20},{1,9},{5... | collective-permute-start | bytes 786440 | tf_op jit(solution)/shard_map/ppermute | solution.py:21
  47.0 1.2 collective-permute-start.5
  48.2 7.5 %copy-start.11 = (bf16[512,1024]{1,0:T(8,128)(2,1)S(1)}, bf16[512,1024]{1,0:T(8,128)(2,1)}, u32[]{:S(2)}) copy-start(bf16[512,1024]{1,0:T(8,128)(2,1)} %copy-done.10) | copy-start | bytes 3145732
  48.2 11.3 %copy-start.17 = (f32[256,512]{1,0:T(8,128)S(1)}, f32[256,512]{1,0:T(8,128)}, u32[]{:S(2)}) copy-start(f32[256,512]{1,0:T(8,128)} %copy-done.16) | copy-start | bytes 1572868
  59.5 4.1 %copy-start.18 = (bf16[256,1024]{1,0:T(8,128)(2,1)}, bf16[256,1024]{1,0:T(8,128)(2,1)S(1)}, u32[]{:S(2)}) copy-start(bf16[256,1024]{1,0:T(8,128)(2,1)S(1)} %get-tuple-element.74.refs_2_) | copy-start | bytes 1572868
  63.6 37.6 %collective-permute-start.7 = (bf16[512,1536]{1,0:T(8,128)(2,1)}, bf16[512,1536]{1,0:T(8,128)(2,1)}, u32[]{:S(2)}, u32[]{:S(2)}) collective-permute-start(bf16[512,1536]{1,0:T(8,128)(2,1)} %shard_map.149), channel_id=1, source_target_pairs={{0,4},{4,0},{8,12},{12,8},{16,20},{20,16},{24,28},{28,24},{1,5},{5... | collective-permute-start | bytes 4718600 | tf_op jit(solution)/shard_map/ppermute | solution.py:21
  64.1 9.9 %collective-permute-start.11 = (s32[256]{0:T(256)S(1)}, s32[256]{0:T(256)S(1)}, u32[]{:S(2)}, u32[]{:S(2)}) collective-permute-start(s32[256]{0:T(256)S(1)} %add.94.refs_4_), channel_id=1, source_target_pairs={{0,2},{1,3},{2,0},{3,1},{4,6},{5,7},{6,4},{7,5},{8,10},{9,11},{10,... | collective-permute-start | bytes 3080 | tf_op jit(solution)/shard_map/ppermute | solution.py:21
  65.6 6.5 %copy-start.19 = (bf16[256,1024]{1,0:T(8,128)(2,1)S(1)}, bf16[256,1024]{1,0:T(8,128)(2,1)}, u32[]{:S(2)}) copy-start(bf16[256,1024]{1,0:T(8,128)(2,1)} %copy-done.18) | copy-start | bytes 1572868
  65.6 26.5 %copy-start.13 = (f32[256,1024]{1,0:T(8,128)S(1)}, f32[256,1024]{1,0:T(8,128)}, u32[]{:S(2)}) copy-start(f32[256,1024]{1,0:T(8,128)} %copy-done.12) | copy-start | bytes 3145732
  72.1 20.4 %copy-start.2 = (bf16[128,7168]{1,0:T(8,128)(2,1)S(1)}, bf16[128,7168]{1,0:T(8,128)(2,1)}, u32[]{:S(2)}) copy-start(bf16[128,7168]{1,0:T(8,128)(2,1)} %refs_2_.27) | copy-start | bytes 5505028
  72.1 20.0 %collective-permute-start.10 = (bf16[256,1024]{1,0:T(8,128)(2,1)S(1)}, bf16[256,1024]{1,0:T(8,128)(2,1)S(1)}, u32[]{:S(2)}, u32[]{:S(2)}) collective-permute-start(bf16[256,1024]{1,0:T(8,128)(2,1)S(1)} %copy-done.19), channel_id=1, source_target_pairs={{0,8},{4,12},{8,0},{12,4},{16,24},{20,28},{24,16},{28,20},{1,9},{5... | collective-permute-start | bytes 1572872 | tf_op jit(solution)/shard_map/ppermute | solution.py:21
  72.5 56.7 %collective-permute-start.6 = (bf16[512,1280]{1,0:T(8,128)(2,1)}, bf16[512,1280]{1,0:T(8,128)(2,1)S(1)}, u32[]{:S(2)}, u32[]{:S(2)}) collective-permute-start(bf16[512,1280]{1,0:T(8,128)(2,1)} %get-tuple-element.78), channel_id=1, source_target_pairs={{0,4},{4,0},{8,12},{12,8},{16,20},{20,16},{24,28},{28,24},{1,5},{5... | collective-permute-start | bytes 3932168 | tf_op jit(solution)/shard_map/ppermute | solution.py:21
  74.0 19.2 %collective-permute-start.8 = (bf16[128,1024]{1,0:T(8,128)(2,1)S(1)}, bf16[128,1024]{1,0:T(8,128)(2,1)S(1)}, u32[]{:S(2)}, u32[]{:S(2)}) collective-permute-start(bf16[128,1024]{1,0:T(8,128)(2,1)S(1)} %get-tuple-element.76.refs_3_.refs_1_), channel_id=1, source_target_pairs={{0,16},{4,20},{8,24},{12,28},{16,0},{20,4},{24,8},{28,12},{1,17},{... | collective-permute-start | bytes 786440 | tf_op jit(solution)/shard_map/ppermute | solution.py:21
  76.7 15.8 %collective-permute-start.9 = (bf16[128,512]{1,0:T(8,128)(2,1)S(1)}, bf16[128,512]{1,0:T(8,128)(2,1)S(1)}, u32[]{:S(2)}, u32[]{:S(2)}) collective-permute-start(bf16[128,512]{1,0:T(8,128)(2,1)S(1)} %get-tuple-element.75.refs_2_), channel_id=1, source_target_pairs={{0,16},{4,20},{8,24},{12,28},{16,0},{20,4},{24,8},{28,12},{1,17},{... | collective-permute-start | bytes 393224 | tf_op jit(solution)/shard_map/ppermute | solution.py:21
  92.4 18.0 %collective-permute-start.13 = (bf16[128,1024]{1,0:T(8,128)(2,1)S(1)}, bf16[128,1024]{1,0:T(8,128)(2,1)S(1)}, u32[]{:S(2)}, u32[]{:S(2)}) collective-permute-start(bf16[128,1024]{1,0:T(8,128)(2,1)S(1)} %get-tuple-element.83.refs_3_), channel_id=1, source_target_pairs={{0,16},{4,20},{8,24},{12,28},{16,0},{20,4},{24,8},{28,12},{1,17},{... | collective-permute-start | bytes 786440 | tf_op jit(solution)/shard_map/ppermute | solution.py:21
  93.2 8.0 %copy-start.7 = (bf16[512,1536]{1,0:T(8,128)(2,1)S(1)}, bf16[512,1536]{1,0:T(8,128)(2,1)}, u32[]{:S(2)}) copy-start(bf16[512,1536]{1,0:T(8,128)(2,1)} %get-tuple-element.73.refs_2_.refs_0_) | copy-start | bytes 4718596
  103.8 18.5 %collective-permute-start.12 = (bf16[256,1536]{1,0:T(8,128)(2,1)S(1)}, bf16[256,1536]{1,0:T(8,128)(2,1)S(1)}, u32[]{:S(2)}, u32[]{:S(2)}) collective-permute-start(bf16[256,1536]{1,0:T(8,128)(2,1)S(1)} %get-tuple-element.88.refs_3_), channel_id=1, source_target_pairs={{0,8},{4,12},{8,0},{12,4},{16,24},{20,28},{24,16},{28,20},{1,9},{5... | collective-permute-start | bytes 2359304 | tf_op jit(solution)/shard_map/ppermute | solution.py:21
  109.8 42.0 %collective-permute-start.18 = (bf16[512,1024]{1,0:T(8,128)(2,1)}, bf16[512,1024]{1,0:T(8,128)(2,1)}, u32[]{:S(2)}, u32[]{:S(2)}) collective-permute-start(bf16[512,1024]{1,0:T(8,128)(2,1)} %get-tuple-element.104), channel_id=1, source_target_pairs={{0,4},{4,0},{8,12},{12,8},{16,20},{20,16},{24,28},{28,24},{1,5},{5... | collective-permute-start | bytes 3145736 | tf_op jit(solution)/shard_map/ppermute | solution.py:21
  129.9 19.9 %collective-permute-start.15 = (bf16[256,1280]{1,0:T(8,128)(2,1)S(1)}, bf16[256,1280]{1,0:T(8,128)(2,1)S(1)}, u32[]{:S(2)}, u32[]{:S(2)}) collective-permute-start(bf16[256,1280]{1,0:T(8,128)(2,1)S(1)} %get-tuple-element.94.refs_3_), channel_id=1, source_target_pairs={{0,8},{4,12},{8,0},{12,4},{16,24},{20,28},{24,16},{28,20},{1,9},{5... | collective-permute-start | bytes 1966088 | tf_op jit(solution)/shard_map/ppermute | solution.py:21
  130.5 17.3 %collective-permute-start.16 = (bf16[128,1536]{1,0:T(8,128)(2,1)S(1)}, bf16[128,1536]{1,0:T(8,128)(2,1)S(1)}, u32[]{:S(2)}, u32[]{:S(2)}) collective-permute-start(bf16[128,1536]{1,0:T(8,128)(2,1)S(1)} %get-tuple-element.93.refs_2_), channel_id=1, source_target_pairs={{0,16},{4,20},{8,24},{12,28},{16,0},{20,4},{24,8},{28,12},{1,17},{... | collective-permute-start | bytes 1179656 | tf_op jit(solution)/shard_map/ppermute | solution.py:21
  137.0 36.1 %collective-permute-start.14 = (bf16[512,768]{1,0:T(8,128)(2,1)S(1)}, bf16[512,768]{1,0:T(8,128)(2,1)S(1)}, u32[]{:S(2)}, u32[]{:S(2)}) collective-permute-start(bf16[512,768]{1,0:T(8,128)(2,1)S(1)} %get-tuple-element.96), channel_id=1, source_target_pairs={{0,4},{4,0},{8,12},{12,8},{16,20},{20,16},{24,28},{28,24},{1,5},{5... | collective-permute-start | bytes 2359304 | tf_op jit(solution)/shard_map/ppermute | solution.py:21
  153.2 17.5 %collective-permute-start.19 = (bf16[256,1024]{1,0:T(8,128)(2,1)S(1)}, bf16[256,1024]{1,0:T(8,128)(2,1)S(1)}, u32[]{:S(2)}, u32[]{:S(2)}) collective-permute-start(bf16[256,1024]{1,0:T(8,128)(2,1)S(1)} %get-tuple-element.106.refs_2_), channel_id=1, source_target_pairs={{0,8},{4,12},{8,0},{12,4},{16,24},{20,28},{24,16},{28,20},{1,9},{5... | collective-permute-start | bytes 1572872 | tf_op jit(solution)/shard_map/ppermute | solution.py:21
  155.8 15.2 %collective-permute-start.17 = (bf16[128,1280]{1,0:T(8,128)(2,1)S(1)}, bf16[128,1280]{1,0:T(8,128)(2,1)S(1)}, u32[]{:S(2)}, u32[]{:S(2)}) collective-permute-start(bf16[128,1280]{1,0:T(8,128)(2,1)S(1)} %get-tuple-element.102.refs_2_), channel_id=1, source_target_pairs={{0,16},{4,20},{8,24},{12,28},{16,0},{20,4},{24,8},{28,12},{1,17},{... | collective-permute-start | bytes 983048 | tf_op jit(solution)/shard_map/ppermute | solution.py:21
  173.6 15.4 %collective-permute-start.20 = (bf16[256,768]{1,0:T(8,128)(2,1)S(1)}, bf16[256,768]{1,0:T(8,128)(2,1)S(1)}, u32[]{:S(2)}, u32[]{:S(2)}) collective-permute-start(bf16[256,768]{1,0:T(8,128)(2,1)S(1)} %get-tuple-element.110.refs_2_), channel_id=1, source_target_pairs={{0,8},{4,12},{8,0},{12,4},{16,24},{20,28},{24,16},{28,20},{1,9},{5... | collective-permute-start | bytes 1179656 | tf_op jit(solution)/shard_map/ppermute | solution.py:21
  174.4 17.9 %collective-permute-start.22 = (bf16[128,1024]{1,0:T(8,128)(2,1)S(1)}, bf16[128,1024]{1,0:T(8,128)(2,1)S(1)}, u32[]{:S(2)}, u32[]{:S(2)}) collective-permute-start(bf16[128,1024]{1,0:T(8,128)(2,1)S(1)} %get-tuple-element.107.refs_4_), channel_id=1, source_target_pairs={{0,16},{4,20},{8,24},{12,28},{16,0},{20,4},{24,8},{28,12},{1,17},{... | collective-permute-start | bytes 786440 | tf_op jit(solution)/shard_map/ppermute | solution.py:21
  189.2 13.3 %collective-permute-start.21 = (bf16[128,768]{1,0:T(8,128)(2,1)S(1)}, bf16[128,768]{1,0:T(8,128)(2,1)S(1)}, u32[]{:S(2)}, u32[]{:S(2)}) collective-permute-start(bf16[128,768]{1,0:T(8,128)(2,1)S(1)} %get-tuple-element.112.refs_4_.refs_1_), channel_id=1, source_target_pairs={{0,16},{4,20},{8,24},{12,28},{16,0},{20,4},{24,8},{28,12},{1,17},{... | collective-permute-start | bytes 589832 | tf_op jit(solution)/shard_map/ppermute | solution.py:21
  189.8 20.5 %collective-permute-start.28 = (bf16[8,7296]{1,0:T(8,128)(2,1)S(1)}, bf16[8,7296]{1,0:T(8,128)(2,1)S(1)}, u32[]{:S(2)}, u32[]{:S(2)}) collective-permute-start(bf16[8,7296]{1,0:T(8,128)(2,1)S(1)} %shard_map.171), channel_id=1, source_target_pairs={{0,16},{4,20},{8,24},{12,28},{16,0},{20,4},{24,8},{28,12},{1,17},{... | collective-permute-start | bytes 350216 | tf_op jit(solution)/shard_map/ppermute | solution.py:21
  205.4 20.5 %copy-start.23 = (s32[8]{0:T(128)S(1)}, s32[8]{0:T(128)}, u32[]{:S(2)}) copy-start(s32[8]{0:T(128)} %constant.81.clone) | copy-start | bytes 100
  206.7 12.9 %all-to-all-start = ((bf16[8,2,7296]{2,1,0:T(2,128)(2,1)}), bf16[8,2,7296]{2,1,0:T(2,128)(2,1)S(1)}, u32[]{:S(2)}, u32[]{:S(2)}) async-start(bf16[8,2,7296]{2,1,0:T(2,128)(2,1)} %reshape.64), calls=%async_computation | async-start | bytes 466944 | tf_op jit(solution)/shard_map/all_to_all | solution.py:347
  210.4 11.2 %collective-permute-start.29 = (bf16[16,7296]{1,0:T(8,128)(2,1)S(1)}, bf16[16,7296]{1,0:T(8,128)(2,1)S(1)}, u32[]{:S(2)}, u32[]{:S(2)}) collective-permute-start(bf16[16,7296]{1,0:T(8,128)(2,1)S(1)} %pad_maximum_fusion.9), channel_id=1, source_target_pairs={{0,8},{4,12},{8,0},{12,4},{16,24},{20,28},{24,16},{28,20},{1,9},{5... | collective-permute-start | bytes 700424 | tf_op jit(solution)/shard_map/ppermute | solution.py:21
  219.8 6.1 %collective-permute-start.23 = (bf16[16,7296]{1,0:T(8,128)(2,1)S(1)}, bf16[16,7296]{1,0:T(8,128)(2,1)S(1)}, u32[]{:S(2)}, u32[]{:S(2)}) collective-permute-start(bf16[16,7296]{1,0:T(8,128)(2,1)S(1)} %reshape.65.refs_0_), channel_id=1, source_target_pairs={{0,2},{1,3},{2,0},{3,1},{4,6},{5,7},{6,4},{7,5},{8,10},{9,11},{10,... | collective-permute-start | bytes 700424 | tf_op jit(solution)/shard_map/ppermute | solution.py:21
  221.6 20.9 %collective-permute-start.30 = (bf16[32,7296]{1,0:T(8,128)(2,1)S(1)}, bf16[32,7296]{1,0:T(8,128)(2,1)S(1)}, u32[]{:S(2)}, u32[]{:S(2)}) collective-permute-start(bf16[32,7296]{1,0:T(8,128)(2,1)S(1)} %pad_maximum_fusion.8), channel_id=1, source_target_pairs={{0,4},{4,0},{8,12},{12,8},{16,20},{20,16},{24,28},{28,24},{1,5},{5... | collective-permute-start | bytes 1400840 | tf_op jit(solution)/shard_map/ppermute | solution.py:21
  223.1 3.0 %collective-permute-start.24 = (bf16[16,7296]{1,0:T(8,128)(2,1)S(1)}, bf16[16,7296]{1,0:T(8,128)(2,1)S(1)}, u32[]{:S(2)}, u32[]{:S(2)}) collective-permute-start(bf16[16,7296]{1,0:T(8,128)(2,1)S(1)} %reshape.65.refs_0_), channel_id=1, source_target_pairs={{0,1},{1,0},{2,3},{3,2},{4,5},{5,4},{6,7},{7,6},{8,9},{9,8},{10,11... | collective-permute-start | bytes 700424 | tf_op jit(solution)/shard_map/ppermute | solution.py:21
  225.9 1.5 collective-permute-start.25
  242.2 3.6 %collective-permute-start.26 = (bf16[32,7168]{1,0:T(8,128)(2,1)S(1)}, bf16[32,7168]{1,0:T(8,128)(2,1)S(1)}, u32[]{:S(2)}, u32[]{:S(2)}) collective-permute-start(bf16[32,7168]{1,0:T(8,128)(2,1)S(1)} %get-tuple-element.119), channel_id=1, source_target_pairs={{0,1},{1,0},{2,3},{3,2},{4,5},{5,4},{6,7},{7,6},{8,9},{9,8},{10,11... | collective-permute-start | bytes 1376264 | tf_op jit(solution)/shard_map/ppermute | solution.py:21
  243.0 15.4 %copy-start.22 = (f32[256]{0:T(256)S(1)}, f32[256]{0:T(256)}, u32[]{:S(2)}) copy-start(f32[256]{0:T(256)} %param.16) | copy-start | bytes 3076
  243.0 1.3 collective-permute-start.31
  244.3 3.7 %collective-permute-start.32 = (f32[16,128]{1,0:T(8,128)S(1)}, f32[16,128]{1,0:T(8,128)S(1)}, u32[]{:S(2)}, u32[]{:S(2)}) collective-permute-start(f32[16,128]{1,0:T(8,128)S(1)} %slice.42), channel_id=1, source_target_pairs={{0,2},{1,3},{2,0},{3,1},{4,6},{5,7},{6,4},{7,5},{8,10},{9,11},{10,... | collective-permute-start | bytes 24584 | tf_op jit(solution)/shard_map/ppermute | solution.py:21
  245.8 22.4 %copy-start.1 = (bf16[7168,32]{0,1:T(8,128)(2,1)S(1)}, bf16[7168,32]{0,1:T(8,128)(2,1)}, u32[]{:S(2)}) copy-start(bf16[7168,32]{0,1:T(8,128)(2,1)} %param.15) | copy-start | bytes 1376260
  245.9 7.6 %collective-permute-start.27 = (bf16[16,7168]{1,0:T(8,128)(2,1)S(1)}, bf16[16,7168]{1,0:T(8,128)(2,1)S(1)}, u32[]{:S(2)}, u32[]{:S(2)}) collective-permute-start(bf16[16,7168]{1,0:T(8,128)(2,1)S(1)} %get-tuple-element.121), channel_id=1, source_target_pairs={{0,2},{1,3},{2,0},{3,1},{4,6},{5,7},{6,4},{7,5},{8,10},{9,11},{10,... | collective-permute-start | bytes 688136 | tf_op jit(solution)/shard_map/ppermute | solution.py:21
  254.5 11.8 %all-to-all-start.1 = ((bf16[8,2,7168]{2,1,0:T(2,128)(2,1)}), bf16[8,2,7168]{2,1,0:T(2,128)(2,1)S(1)}, u32[]{:S(2)}, u32[]{:S(2)}) async-start(bf16[8,2,7168]{2,1,0:T(2,128)(2,1)} %reshape.66), calls=%async_computation.1 | async-start | bytes 458752 | tf_op jit(solution)/shard_map/all_to_all | solution.py:462
  (11 other events, 18.0 us)

commit v4 on v2

--- a/solution.py
+++ b/solution.py
@@ -183,7 +183,7 @@
         ]
         for kind in ("y", "z")
     }
-    tiles = {"y0": 2, "z0": 4, "y1": 4, "y2": 6, "y3": 5, "y4": 4, "y5": 3}
+    tiles = {"y0": 3, "z0": 4, "y1": 4, "y2": 6, "y3": 5, "y4": 4, "y5": 2}
     unit = width // sum(tiles.values())
     spans, lo = {}, 0
     for name, count in tiles.items():

time: 268 us -> 265 us (0.989)
  waiting for transfers between devices: 130 us -> 119 us
  starting transfers between devices: 43.5 us -> 51.9 us
    ppermute x33, waiting for transfers between devices: 115 us -> 105 us  [swap(): return lax.ppermute(value, axis, [(i, i ^ bit) for i in range(size)])]
    ppermute x33, starting transfers between devices: 36.1 us -> 44.6 us  [swap(): return lax.ppermute(value, axis, [(i, i ^ bit) for i in range(size)])]
    unnamed x49 -> x59, local copies, waits for them, and re-layouts: 7.8 us -> 8.83 us
where the time goes in v4:
time: 265 us; the launch traced here: 264 us
  waiting for transfers between devices  119 us (45%)
  Pallas kernels  74.3 us (28%)
  starting transfers between devices  51.9 us (20%)
  local copies, waits for them, and re-layouts  12.7 us (5%)
  other arithmetic  3.19 us (1%)
    ppermute x33, waiting for transfers between devices, swap(): return lax.ppermute(value, axis, [(i, i ^ bit) for i in range(size)])  105 us
    pallas_call x36, Pallas kernels, run(): pl.pallas_call(inner, grid=grid, in_specs=[spec for _, spec in ins] + [AN...  74.3 us
    ppermute x33, starting transfers between devices, swap(): return lax.ppermute(value, axis, [(i, i ^ bit) for i in range(size)])  44.6 us
    unnamed x59, local copies, waits for them, and re-layouts  8.83 us
    all_to_all x1, waiting for transfers between devices, on_device(): lax.all_to_all(summed.reshape(tp_count, CAP, width), 'tp', split_axis=0,...  7.38 us
    all_to_all x1, waiting for transfers between devices, on_device(): lax.all_to_all(normed.reshape(tp_count, CAP, width + lanes), 'tp', split_...  6.83 us
  transfers between devices with their start and end apart: 35, of which 22 were waited for; matrix products, arithmetic and copies ran while one was open for 1% of the time, Pallas kernels for 26%

profile of v4, /device:TPU:0, one launch (start us, length us, event | category | flops | bytes accessed | tf_op | source)
XLA Modules:
  0.0 264.0 jit_solution(251411658928619688)
XLA Ops:
  0.7 1.7 constant_dynamic-slice_fusion.3
  3.9 4.8 %shard_map.138 = (bf16[512,768]{1,0:T(8,128)(2,1)S(1)}, bf16[512,768]{1,0:T(8,128)(2,1)}) custom-call(bf16[512,1024]{1,0:T(8,128)(2,1)S(1)} %get-tuple-element.133.refs_0_, bf16[512,1024]{1,0:T(8,128)(2,1)S(1)} %get-tuple-element.135.refs_1_, bf16[1024,7168]{1,0:T(8,128)(2,1)} %refs_2_.23), custom_call_target="tpu_custom_call" | custom-call | flops 1 | bytes 1 | tf_op jit(solution)/shard_map/pallas_call | solution.py:44
  8.7 3.0 %collective-permute-start.1 = (bf16[512,768]{1,0:T(8,128)(2,1)}, bf16[512,768]{1,0:T(8,128)(2,1)}, u32[]{:S(2)}, u32[]{:S(2)}) collective-permute-start(bf16[512,768]{1,0:T(8,128)(2,1)} %get-tuple-element.66), channel_id=1, source_target_pairs={{0,4},{4,0},{8,12},{12,8},{16,20},{20,16},{24,28},{28,24},{1,5},{5... | collective-permute-start | bytes 2359304 | tf_op jit(solution)/shard_map/ppermute | solution.py:21
  11.6 5.6 %shard_map.139 = (bf16[512,1024]{1,0:T(8,128)(2,1)S(1)}, bf16[512,1024]{1,0:T(8,128)(2,1)}) custom-call(bf16[512,1024]{1,0:T(8,128)(2,1)S(1)} %get-tuple-element.134.refs_0_, bf16[512,1024]{1,0:T(8,128)(2,1)} %get-tuple-element.132.refs_1_, bf16[1024,7168]{1,0:T(8,128)(2,1)} %refs_2_.23, bf16[512,768]{1,0:T(8,128)(2,1)S(1)} %get-tuple-element.63.refs_3_.refs_0_), custom_call_target="tpu_custom_call" | custom-call | flops 1 | bytes 1 | tf_op jit(solution)/shard_map/pallas_call | solution.py:44
  18.2 1.6 collective-permute-start
  19.8 5.6 %shard_map.140 = (bf16[512,1024]{1,0:T(8,128)(2,1)S(1)}, bf16[512,1024]{1,0:T(8,128)(2,1)}) custom-call(bf16[512,1024]{1,0:T(8,128)(2,1)S(1)} %get-tuple-element.133.refs_0_, bf16[512,1024]{1,0:T(8,128)(2,1)} %copy-done.4, bf16[1024,7168]{1,0:T(8,128)(2,1)} %refs_2_.23, bf16[512,1024]{1,0:T(8,128)(2,1)} %copy-done.11), custom_call_target="tpu_custom_call" | custom-call | flops 1 | bytes 1 | tf_op jit(solution)/shard_map/pallas_call | solution.py:44
  25.9 3.6 %collective-permute-done.1.refs_1_ = bf16[512,768]{1,0:T(8,128)(2,1)} collective-permute-done((bf16[512,768]{1,0:T(8,128)(2,1)}, bf16[512,768]{1,0:T(8,128)(2,1)}, u32[]{:S(2)}, u32[]{:S(2)}) %collective-permute-start.1) | collective-permute-done | bytes 786464 | tf_op jit(solution)/shard_map/ppermute | solution.py:21
  29.5 1.9 shard_map.141
  32.3 1.8 collective-permute-start.4
  34.9 8.2 %collective-permute-done.refs_1_ = bf16[512,1024]{1,0:T(8,128)(2,1)} collective-permute-done((bf16[512,1024]{1,0:T(8,128)(2,1)}, bf16[512,1024]{1,0:T(8,128)(2,1)}, u32[]{:S(2)}, u32[]{:S(2)}) %collective-permute-start) | collective-permute-done | bytes 1048608 | tf_op jit(solution)/shard_map/ppermute | solution.py:21
  46.2 1.7 collective-permute-start.3
  49.4 7.4 %shard_map.144 = (bf16[512,1536]{1,0:T(8,128)(2,1)}, bf16[512,1536]{1,0:T(8,128)(2,1)}) custom-call(bf16[512,1024]{1,0:T(8,128)(2,1)S(1)} %get-tuple-element.133.refs_0_, bf16[512,1024]{1,0:T(8,128)(2,1)S(1)} %copy-done.5, bf16[1024,7168]{1,0:T(8,128)(2,1)} %refs_2_.23, bf16[256,1024]{1,0:T(8,128)(2,1)S(1)} %get-tuple-element.70.refs_3_, s32[256]{0:T(256)S(1)} %add.94.refs_4_), custom_call_target="tpu_custom_call" | custom-call | flops 1 | bytes 1 | tf_op jit(solution)/shard_map/pallas_call | solution.py:44
  56.8 2.0 collective-permute-done.4.refs_1_
  62.9 5.2 %collective-permute-done.2.refs_1_ = bf16[256,1024]{1,0:T(8,128)(2,1)S(1)} collective-permute-done((bf16[256,1024]{1,0:T(8,128)(2,1)S(1)}, bf16[256,1024]{1,0:T(8,128)(2,1)S(1)}, u32[]{:S(2)}, u32[]{:S(2)}) %collective-permute-start.2) | collective-permute-done | bytes 524320 | tf_op jit(solution)/shard_map/ppermute | solution.py:21
  72.2 6.4 %shard_map.148 = (bf16[512,1280]{1,0:T(8,128)(2,1)S(1)}, bf16[512,1280]{1,0:T(8,128)(2,1)}) custom-call(bf16[512,1024]{1,0:T(8,128)(2,1)S(1)} %get-tuple-element.133.refs_0_, bf16[512,1024]{1,0:T(8,128)(2,1)S(1)} %copy-done.5, bf16[1024,7168]{1,0:T(8,128)(2,1)} %refs_2_.23, bf16[128,1024]{1,0:T(8,128)(2,1)S(1)} %get-tuple-element.76.refs_3_.refs_1_), custom_call_target="tpu_custom_call" | custom-call | flops 1 | bytes 1 | tf_op jit(solution)/shard_map/pallas_call | solution.py:44
  78.7 1.6 collective-permute-start.10
  80.8 2.7 %collective-permute-start.8 = (bf16[128,1024]{1,0:T(8,128)(2,1)S(1)}, bf16[128,1024]{1,0:T(8,128)(2,1)S(1)}, u32[]{:S(2)}, u32[]{:S(2)}) collective-permute-start(bf16[128,1024]{1,0:T(8,128)(2,1)S(1)} %get-tuple-element.76.refs_3_.refs_1_), channel_id=1, source_target_pairs={{0,16},{4,20},{8,24},{12,28},{16,0},{20,4},{24,8},{28,12},{1,17},{... | collective-permute-start | bytes 786440 | tf_op jit(solution)/shard_map/ppermute | solution.py:21
  83.8 16.0 %collective-permute-done.10.refs_1_ = bf16[256,1024]{1,0:T(8,128)(2,1)S(1)} collective-permute-done((bf16[256,1024]{1,0:T(8,128)(2,1)S(1)}, bf16[256,1024]{1,0:T(8,128)(2,1)S(1)}, u32[]{:S(2)}, u32[]{:S(2)}) %collective-permute-start.10) | collective-permute-done | bytes 524320 | tf_op jit(solution)/shard_map/ppermute | solution.py:21
  100.1 1.6 collective-permute-start.13
  104.0 2.9 %collective-permute-done.7.refs_1_ = bf16[512,1536]{1,0:T(8,128)(2,1)} collective-permute-done((bf16[512,1536]{1,0:T(8,128)(2,1)}, bf16[512,1536]{1,0:T(8,128)(2,1)}, u32[]{:S(2)}, u32[]{:S(2)}) %collective-permute-start.7) | collective-permute-done | bytes 1572896 | tf_op jit(solution)/shard_map/ppermute | solution.py:21
  106.9 2.5 shard_map.153
  109.4 1.5 collective-permute-start.12
  111.0 5.6 %shard_map.154 = (bf16[512,1024]{1,0:T(8,128)(2,1)S(1)}, bf16[512,1024]{1,0:T(8,128)(2,1)}) custom-call(bf16[512,1024]{1,0:T(8,128)(2,1)S(1)} %get-tuple-element.133.refs_0_, bf16[512,1024]{1,0:T(8,128)(2,1)} %copy-done.4, bf16[1024,7168]{1,0:T(8,128)(2,1)} %refs_2_.23, bf16[256,1536]{1,0:T(8,128)(2,1)S(1)} %get-tuple-element.88.refs_3_), custom_call_target="tpu_custom_call" | custom-call | flops 1 | bytes 1 | tf_op jit(solution)/shard_map/pallas_call | solution.py:44
  116.5 2.7 %collective-permute-start.15 = (bf16[512,1024]{1,0:T(8,128)(2,1)}, bf16[512,1024]{1,0:T(8,128)(2,1)S(1)}, u32[]{:S(2)}, u32[]{:S(2)}) collective-permute-start(bf16[512,1024]{1,0:T(8,128)(2,1)} %get-tuple-element.97), channel_id=1, source_target_pairs={{0,4},{4,0},{8,12},{12,8},{16,20},{20,16},{24,28},{28,24},{1,5},{5... | collective-permute-start | bytes 3145736 | tf_op jit(solution)/shard_map/ppermute | solution.py:21
  120.7 8.6 %collective-permute-done.12.refs_1_ = bf16[256,1536]{1,0:T(8,128)(2,1)S(1)} collective-permute-done((bf16[256,1536]{1,0:T(8,128)(2,1)S(1)}, bf16[256,1536]{1,0:T(8,128)(2,1)S(1)}, u32[]{:S(2)}, u32[]{:S(2)}) %collective-permute-start.12) | collective-permute-done | bytes 786464 | tf_op jit(solution)/shard_map/ppermute | solution.py:21
  130.6 4.2 %collective-permute-done.6.refs_1_ = bf16[512,1280]{1,0:T(8,128)(2,1)S(1)} collective-permute-done((bf16[512,1280]{1,0:T(8,128)(2,1)}, bf16[512,1280]{1,0:T(8,128)(2,1)S(1)}, u32[]{:S(2)}, u32[]{:S(2)}) %collective-permute-start.6) | collective-permute-done | bytes 1310752 | tf_op jit(solution)/shard_map/ppermute | solution.py:21
  137.2 2.6 collective-permute-start.17
  139.7 2.6 shard_map.158
  142.4 11.5 %collective-permute-done.17.refs_1_ = bf16[128,1536]{1,0:T(8,128)(2,1)S(1)} collective-permute-done((bf16[128,1536]{1,0:T(8,128)(2,1)S(1)}, bf16[128,1536]{1,0:T(8,128)(2,1)S(1)}, u32[]{:S(2)}, u32[]{:S(2)}) %collective-permute-start.17) | collective-permute-done | bytes 393248 | tf_op jit(solution)/shard_map/ppermute | solution.py:21
  153.9 2.1 shard_map.159
  156.9 3.5 %collective-permute-start.18 = (bf16[256,1024]{1,0:T(8,128)(2,1)S(1)}, bf16[256,1024]{1,0:T(8,128)(2,1)S(1)}, u32[]{:S(2)}, u32[]{:S(2)}) collective-permute-start(bf16[256,1024]{1,0:T(8,128)(2,1)S(1)} %get-tuple-element.104.refs_4_), channel_id=1, source_target_pairs={{0,8},{4,12},{8,0},{12,4},{16,24},{20,28},{24,16},{28,20},{1,9},{5... | collective-permute-start | bytes 1572872 | tf_op jit(solution)/shard_map/ppermute | solution.py:21
  162.1 11.7 %collective-permute-done.19.refs_1_ = bf16[128,1280]{1,0:T(8,128)(2,1)S(1)} collective-permute-done((bf16[128,1280]{1,0:T(8,128)(2,1)S(1)}, bf16[128,1280]{1,0:T(8,128)(2,1)S(1)}, u32[]{:S(2)}, u32[]{:S(2)}) %collective-permute-start.19) | collective-permute-done | bytes 327712 | tf_op jit(solution)/shard_map/ppermute | solution.py:21
  173.9 2.1 shard_map.162
  176.5 2.5 collective-permute-start.20
  179.9 7.6 %collective-permute-done.20.refs_1_ = bf16[256,512]{1,0:T(8,128)(2,1)S(1)} collective-permute-done((bf16[256,512]{1,0:T(8,128)(2,1)S(1)}, bf16[256,512]{1,0:T(8,128)(2,1)S(1)}, u32[]{:S(2)}, u32[]{:S(2)}) %collective-permute-start.20) | collective-permute-done | bytes 262176 | tf_op jit(solution)/shard_map/ppermute | solution.py:21
  187.6 2.9 %collective-permute-start.28 = (bf16[8,7296]{1,0:T(8,128)(2,1)S(1)}, bf16[8,7296]{1,0:T(8,128)(2,1)S(1)}, u32[]{:S(2)}, u32[]{:S(2)}) collective-permute-start(bf16[8,7296]{1,0:T(8,128)(2,1)S(1)} %shard_map.171), channel_id=1, source_target_pairs={{0,16},{4,20},{8,24},{12,28},{16,0},{20,4},{24,8},{28,12},{1,17},{... | collective-permute-start | bytes 350216 | tf_op jit(solution)/shard_map/ppermute | solution.py:21
  190.5 6.3 %collective-permute-done.22.refs_1_ = bf16[128,1024]{1,0:T(8,128)(2,1)S(1)} collective-permute-done((bf16[128,1024]{1,0:T(8,128)(2,1)S(1)}, bf16[128,1024]{1,0:T(8,128)(2,1)S(1)}, u32[]{:S(2)}, u32[]{:S(2)}) %collective-permute-start.22) | collective-permute-done | bytes 262176 | tf_op jit(solution)/shard_map/ppermute | solution.py:21
  197.7 1.7 collective-permute-done.21.refs_1_
  202.9 3.9 %all-to-all-start = ((bf16[8,2,7296]{2,1,0:T(2,128)(2,1)}), bf16[8,2,7296]{2,1,0:T(2,128)(2,1)S(1)}, u32[]{:S(2)}, u32[]{:S(2)}) async-start(bf16[8,2,7296]{2,1,0:T(2,128)(2,1)} %reshape.64), calls=%async_computation | async-start | bytes 466944 | tf_op jit(solution)/shard_map/all_to_all | solution.py:347
  206.9 2.1 collective-permute-start.29
  209.0 6.8 %all-to-all-done = bf16[8,2,7296]{2,1,0:T(2,128)(2,1)S(1)} async-done(((bf16[8,2,7296]{2,1,0:T(2,128)(2,1)}), bf16[8,2,7296]{2,1,0:T(2,128)(2,1)S(1)}, u32[]{:S(2)}, u32[]{:S(2)}) %all-to-all-start) | async-done | bytes 233504 | tf_op jit(solution)/shard_map/all_to_all | solution.py:347
  215.9 1.6 collective-permute-start.23
  217.7 4.3 %collective-permute-done.23.refs_1_ = bf16[16,7296]{1,0:T(8,128)(2,1)S(1)} collective-permute-done((bf16[16,7296]{1,0:T(8,128)(2,1)S(1)}, bf16[16,7296]{1,0:T(8,128)(2,1)S(1)}, u32[]{:S(2)}, u32[]{:S(2)}) %collective-permute-start.23) | collective-permute-done | bytes 233504 | tf_op jit(solution)/shard_map/ppermute | solution.py:21
  223.5 14.8 %shard_map.169 = (bf16[32,7168]{1,0:T(8,128)(2,1)S(1)}, f32[32,7168]{1,0:T(8,128)S(1)}) custom-call(bf16[16,7296]{1,0:T(8,128)(2,1)S(1)} %reshape.65.refs_0_, bf16[16,7296]{1,0:T(8,128)(2,1)S(1)} %collective-permute-done.23.refs_1_, bf16[16,7296]{1,0:T(8,128)(2,1)S(1)} %collective-permute-done.24.refs_2_, ...), custom_call_target="tpu_custom_call" | custom-call | flops 1 | bytes 1 | tf_op jit(solution)/shard_map/pallas_call | solution.py:44
  244.1 5.6 %collective-permute-done.27.refs_1_ = bf16[16,7168]{1,0:T(8,128)(2,1)S(1)} collective-permute-done((bf16[16,7168]{1,0:T(8,128)(2,1)S(1)}, bf16[16,7168]{1,0:T(8,128)(2,1)S(1)}, u32[]{:S(2)}, u32[]{:S(2)}) %collective-permute-start.27) | collective-permute-done | bytes 229408 | tf_op jit(solution)/shard_map/ppermute | solution.py:21
  250.7 3.4 %all-to-all-start.1 = ((bf16[8,2,7168]{2,1,0:T(2,128)(2,1)}), bf16[8,2,7168]{2,1,0:T(2,128)(2,1)S(1)}, u32[]{:S(2)}, u32[]{:S(2)}) async-start(bf16[8,2,7168]{2,1,0:T(2,128)(2,1)} %reshape.66), calls=%async_computation.1 | async-start | bytes 458752 | tf_op jit(solution)/shard_map/all_to_all | solution.py:462
  254.7 7.4 %all-to-all-done.1 = bf16[8,2,7168]{2,1,0:T(2,128)(2,1)S(1)} async-done(((bf16[8,2,7168]{2,1,0:T(2,128)(2,1)}), bf16[8,2,7168]{2,1,0:T(2,128)(2,1)S(1)}, u32[]{:S(2)}, u32[]{:S(2)}) %all-to-all-start.1) | async-done | bytes 229408 | tf_op jit(solution)/shard_map/all_to_all | solution.py:462
  262.1 1.9 fusion
  (162 shorter events, 43.2 us)
Async XLA Ops:
  0.6 71.5 %copy-start = (bf16[7168,32]{0,1:T(8,128)(2,1)S(1)}, bf16[7168,32]{0,1:T(8,128)(2,1)}, u32[]{:S(2)}) copy-start(bf16[7168,32]{0,1:T(8,128)(2,1)} %param.15) | copy-start | bytes 1376260
  8.7 20.8 %collective-permute-start.1 = (bf16[512,768]{1,0:T(8,128)(2,1)}, bf16[512,768]{1,0:T(8,128)(2,1)}, u32[]{:S(2)}, u32[]{:S(2)}) collective-permute-start(bf16[512,768]{1,0:T(8,128)(2,1)} %get-tuple-element.66), channel_id=1, source_target_pairs={{0,4},{4,0},{8,12},{12,8},{16,20},{20,16},{24,28},{28,24},{1,5},{5... | collective-permute-start | bytes 2359304 | tf_op jit(solution)/shard_map/ppermute | solution.py:21
  18.2 24.9 %collective-permute-start = (bf16[512,1024]{1,0:T(8,128)(2,1)}, bf16[512,1024]{1,0:T(8,128)(2,1)}, u32[]{:S(2)}, u32[]{:S(2)}) collective-permute-start(bf16[512,1024]{1,0:T(8,128)(2,1)} %get-tuple-element.65), channel_id=1, source_target_pairs={{0,8},{4,12},{8,0},{12,4},{16,24},{20,28},{24,16},{28,20},{1,9},{5... | collective-permute-start | bytes 3145736 | tf_op jit(solution)/shard_map/ppermute | solution.py:21
  25.4 6.9 %copy-start.9 = (bf16[512,1024]{1,0:T(8,128)(2,1)}, bf16[512,1024]{1,0:T(8,128)(2,1)S(1)}, u32[]{:S(2)}) copy-start(bf16[512,1024]{1,0:T(8,128)(2,1)S(1)} %get-tuple-element.67.refs_2_.refs_0_) | copy-start | bytes 3145732
  32.3 17.0 %copy-start.5 = (bf16[512,1024]{1,0:T(8,128)(2,1)S(1)}, bf16[512,1024]{1,0:T(8,128)(2,1)}, u32[]{:S(2)}) copy-start(bf16[512,1024]{1,0:T(8,128)(2,1)} %copy-done.4) | copy-start | bytes 3145732
  32.3 26.5 %collective-permute-start.4 = (bf16[512,1024]{1,0:T(8,128)(2,1)}, bf16[512,1024]{1,0:T(8,128)(2,1)}, u32[]{:S(2)}, u32[]{:S(2)}) collective-permute-start(bf16[512,1024]{1,0:T(8,128)(2,1)} %shard_map.143), channel_id=1, source_target_pairs={{0,4},{4,0},{8,12},{12,8},{16,20},{20,16},{24,28},{28,24},{1,5},{5... | collective-permute-start | bytes 3145736 | tf_op jit(solution)/shard_map/ppermute | solution.py:21
  45.8 22.4 %collective-permute-start.2 = (bf16[256,1024]{1,0:T(8,128)(2,1)S(1)}, bf16[256,1024]{1,0:T(8,128)(2,1)S(1)}, u32[]{:S(2)}, u32[]{:S(2)}) collective-permute-start(bf16[256,1024]{1,0:T(8,128)(2,1)S(1)} %get-tuple-element.70.refs_3_), channel_id=1, source_target_pairs={{0,4},{4,0},{8,12},{12,8},{16,20},{20,16},{24,28},{28,24},{1,5},{5... | collective-permute-start | bytes 1572872 | tf_op jit(solution)/shard_map/ppermute | solution.py:21
  46.2 16.4 %collective-permute-start.3 = (bf16[256,768]{1,0:T(8,128)(2,1)}, bf16[256,768]{1,0:T(8,128)(2,1)S(1)}, u32[]{:S(2)}, u32[]{:S(2)}) collective-permute-start(bf16[256,768]{1,0:T(8,128)(2,1)} %get-tuple-element.68.refs_2_.refs_1_), channel_id=1, source_target_pairs={{0,8},{4,12},{8,0},{12,4},{16,24},{20,28},{24,16},{28,20},{1,9},{5... | collective-permute-start | bytes 1179656 | tf_op jit(solution)/shard_map/ppermute | solution.py:21
  48.1 1.2 collective-permute-start.5
  49.3 9.4 %copy-start.10 = (bf16[512,1024]{1,0:T(8,128)(2,1)S(1)}, bf16[512,1024]{1,0:T(8,128)(2,1)}, u32[]{:S(2)}) copy-start(bf16[512,1024]{1,0:T(8,128)(2,1)} %copy-done.9) | copy-start | bytes 3145732
  49.4 13.3 %copy-start.16 = (f32[256,768]{1,0:T(8,128)S(1)}, f32[256,768]{1,0:T(8,128)}, u32[]{:S(2)}) copy-start(f32[256,768]{1,0:T(8,128)} %copy-done.15) | copy-start | bytes 2359300
  69.3 37.6 %collective-permute-start.7 = (bf16[512,1536]{1,0:T(8,128)(2,1)}, bf16[512,1536]{1,0:T(8,128)(2,1)}, u32[]{:S(2)}, u32[]{:S(2)}) collective-permute-start(bf16[512,1536]{1,0:T(8,128)(2,1)} %shard_map.149), channel_id=1, source_target_pairs={{0,4},{4,0},{8,12},{12,8},{16,20},{20,16},{24,28},{28,24},{1,5},{5... | collective-permute-start | bytes 4718600 | tf_op jit(solution)/shard_map/ppermute | solution.py:21
  70.7 10.1 %collective-permute-start.11 = (s32[256]{0:T(256)S(1)}, s32[256]{0:T(256)S(1)}, u32[]{:S(2)}, u32[]{:S(2)}) collective-permute-start(s32[256]{0:T(256)S(1)} %add.94.refs_4_), channel_id=1, source_target_pairs={{0,2},{1,3},{2,0},{3,1},{4,6},{5,7},{6,4},{7,5},{8,10},{9,11},{10,... | collective-permute-start | bytes 3080 | tf_op jit(solution)/shard_map/ppermute | solution.py:21
  72.2 11.2 %copy-start.24 = (bf16[128,768]{1,0:T(8,128)(2,1)S(1)}, bf16[128,768]{1,0:T(8,128)(2,1)}, u32[]{:S(2)}) copy-start(bf16[128,768]{1,0:T(8,128)(2,1)} %copy-done.23) | copy-start | bytes 589828
  72.2 27.6 %copy-start.14 = (f32[256,1024]{1,0:T(8,128)S(1)}, f32[256,1024]{1,0:T(8,128)}, u32[]{:S(2)}) copy-start(f32[256,1024]{1,0:T(8,128)} %copy-done.13) | copy-start | bytes 3145732
  78.7 23.1 %copy-start.2 = (bf16[128,7168]{1,0:T(8,128)(2,1)S(1)}, bf16[128,7168]{1,0:T(8,128)(2,1)}, u32[]{:S(2)}) copy-start(bf16[128,7168]{1,0:T(8,128)(2,1)} %refs_2_.27) | copy-start | bytes 5505028
  78.7 21.1 %collective-permute-start.10 = (bf16[256,1024]{1,0:T(8,128)(2,1)S(1)}, bf16[256,1024]{1,0:T(8,128)(2,1)S(1)}, u32[]{:S(2)}, u32[]{:S(2)}) collective-permute-start(bf16[256,1024]{1,0:T(8,128)(2,1)S(1)} %copy-done.22), channel_id=1, source_target_pairs={{0,8},{4,12},{8,0},{12,4},{16,24},{20,28},{24,16},{28,20},{1,9},{5... | collective-permute-start | bytes 1572872 | tf_op jit(solution)/shard_map/ppermute | solution.py:21
  80.2 54.6 %collective-permute-start.6 = (bf16[512,1280]{1,0:T(8,128)(2,1)}, bf16[512,1280]{1,0:T(8,128)(2,1)S(1)}, u32[]{:S(2)}, u32[]{:S(2)}) collective-permute-start(bf16[512,1280]{1,0:T(8,128)(2,1)} %get-tuple-element.78), channel_id=1, source_target_pairs={{0,4},{4,0},{8,12},{12,8},{16,20},{20,16},{24,28},{28,24},{1,5},{5... | collective-permute-start | bytes 3932168 | tf_op jit(solution)/shard_map/ppermute | solution.py:21
  80.8 21.7 %collective-permute-start.8 = (bf16[128,1024]{1,0:T(8,128)(2,1)S(1)}, bf16[128,1024]{1,0:T(8,128)(2,1)S(1)}, u32[]{:S(2)}, u32[]{:S(2)}) collective-permute-start(bf16[128,1024]{1,0:T(8,128)(2,1)S(1)} %get-tuple-element.76.refs_3_.refs_1_), channel_id=1, source_target_pairs={{0,16},{4,20},{8,24},{12,28},{16,0},{20,4},{24,8},{28,12},{1,17},{... | collective-permute-start | bytes 786440 | tf_op jit(solution)/shard_map/ppermute | solution.py:21
  83.4 18.3 %collective-permute-start.9 = (bf16[128,768]{1,0:T(8,128)(2,1)S(1)}, bf16[128,768]{1,0:T(8,128)(2,1)S(1)}, u32[]{:S(2)}, u32[]{:S(2)}) collective-permute-start(bf16[128,768]{1,0:T(8,128)(2,1)S(1)} %copy-done.24), channel_id=1, source_target_pairs={{0,16},{4,20},{8,24},{12,28},{16,0},{20,4},{24,8},{28,12},{1,17},{... | collective-permute-start | bytes 589832 | tf_op jit(solution)/shard_map/ppermute | solution.py:21
  100.1 19.1 %collective-permute-start.13 = (bf16[128,1024]{1,0:T(8,128)(2,1)S(1)}, bf16[128,1024]{1,0:T(8,128)(2,1)S(1)}, u32[]{:S(2)}, u32[]{:S(2)}) collective-permute-start(bf16[128,1024]{1,0:T(8,128)(2,1)S(1)} %get-tuple-element.83.refs_3_), channel_id=1, source_target_pairs={{0,16},{4,20},{8,24},{12,28},{16,0},{20,4},{24,8},{28,12},{1,17},{... | collective-permute-start | bytes 786440 | tf_op jit(solution)/shard_map/ppermute | solution.py:21
  109.4 19.9 %collective-permute-start.12 = (bf16[256,1536]{1,0:T(8,128)(2,1)S(1)}, bf16[256,1536]{1,0:T(8,128)(2,1)S(1)}, u32[]{:S(2)}, u32[]{:S(2)}) collective-permute-start(bf16[256,1536]{1,0:T(8,128)(2,1)S(1)} %get-tuple-element.88.refs_3_), channel_id=1, source_target_pairs={{0,8},{4,12},{8,0},{12,4},{16,24},{20,28},{24,16},{28,20},{1,9},{5... | collective-permute-start | bytes 2359304 | tf_op jit(solution)/shard_map/ppermute | solution.py:21
  116.5 39.9 %collective-permute-start.15 = (bf16[512,1024]{1,0:T(8,128)(2,1)}, bf16[512,1024]{1,0:T(8,128)(2,1)S(1)}, u32[]{:S(2)}, u32[]{:S(2)}) collective-permute-start(bf16[512,1024]{1,0:T(8,128)(2,1)} %get-tuple-element.97), channel_id=1, source_target_pairs={{0,4},{4,0},{8,12},{12,8},{16,20},{20,16},{24,28},{28,24},{1,5},{5... | collective-permute-start | bytes 3145736 | tf_op jit(solution)/shard_map/ppermute | solution.py:21
  130.6 9.1 %copy-start.6 = (bf16[512,1024]{1,0:T(8,128)(2,1)S(1)}, bf16[512,1024]{1,0:T(8,128)(2,1)}, u32[]{:S(2)}) copy-start(bf16[512,1024]{1,0:T(8,128)(2,1)} %copy-done.4) | copy-start | bytes 3145732
  135.6 18.3 %copy-start.18 = (f32[128,1536]{1,0:T(8,128)S(1)}, f32[128,1536]{1,0:T(8,128)}, u32[]{:S(2)}) copy-start(f32[128,1536]{1,0:T(8,128)} %copy-done.17) | copy-start | bytes 2359300
  135.6 20.4 %collective-permute-start.16 = (bf16[256,1280]{1,0:T(8,128)(2,1)S(1)}, bf16[256,1280]{1,0:T(8,128)(2,1)S(1)}, u32[]{:S(2)}, u32[]{:S(2)}) collective-permute-start(bf16[256,1280]{1,0:T(8,128)(2,1)S(1)} %get-tuple-element.94.refs_3_), channel_id=1, source_target_pairs={{0,8},{4,12},{8,0},{12,4},{16,24},{20,28},{24,16},{28,20},{1,9},{5... | collective-permute-start | bytes 1966088 | tf_op jit(solution)/shard_map/ppermute | solution.py:21
  137.2 16.7 %collective-permute-start.17 = (bf16[128,1536]{1,0:T(8,128)(2,1)S(1)}, bf16[128,1536]{1,0:T(8,128)(2,1)S(1)}, u32[]{:S(2)}, u32[]{:S(2)}) collective-permute-start(bf16[128,1536]{1,0:T(8,128)(2,1)S(1)} %get-tuple-element.93.refs_2_), channel_id=1, source_target_pairs={{0,16},{4,20},{8,24},{12,28},{16,0},{20,4},{24,8},{28,12},{1,17},{... | collective-permute-start | bytes 1179656 | tf_op jit(solution)/shard_map/ppermute | solution.py:21
  156.9 19.1 %collective-permute-start.18 = (bf16[256,1024]{1,0:T(8,128)(2,1)S(1)}, bf16[256,1024]{1,0:T(8,128)(2,1)S(1)}, u32[]{:S(2)}, u32[]{:S(2)}) collective-permute-start(bf16[256,1024]{1,0:T(8,128)(2,1)S(1)} %get-tuple-element.104.refs_4_), channel_id=1, source_target_pairs={{0,8},{4,12},{8,0},{12,4},{16,24},{20,28},{24,16},{28,20},{1,9},{5... | collective-permute-start | bytes 1572872 | tf_op jit(solution)/shard_map/ppermute | solution.py:21
  160.5 15.9 %collective-permute-start.14 = (bf16[512,512]{1,0:T(8,128)(2,1)S(1)}, bf16[512,512]{1,0:T(8,128)(2,1)S(1)}, u32[]{:S(2)}, u32[]{:S(2)}) collective-permute-start(bf16[512,512]{1,0:T(8,128)(2,1)S(1)} %get-tuple-element.96), channel_id=1, source_target_pairs={{0,4},{4,0},{8,12},{12,8},{16,20},{20,16},{24,28},{28,24},{1,5},{5... | collective-permute-start | bytes 1572872 | tf_op jit(solution)/shard_map/ppermute | solution.py:21
  162.0 11.8 %collective-permute-start.19 = (bf16[128,1280]{1,0:T(8,128)(2,1)S(1)}, bf16[128,1280]{1,0:T(8,128)(2,1)S(1)}, u32[]{:S(2)}, u32[]{:S(2)}) collective-permute-start(bf16[128,1280]{1,0:T(8,128)(2,1)S(1)} %get-tuple-element.102.refs_2_), channel_id=1, source_target_pairs={{0,16},{4,20},{8,24},{12,28},{16,0},{20,4},{24,8},{28,12},{1,17},{... | collective-permute-start | bytes 983048 | tf_op jit(solution)/shard_map/ppermute | solution.py:21
  176.5 11.0 %collective-permute-start.20 = (bf16[256,512]{1,0:T(8,128)(2,1)S(1)}, bf16[256,512]{1,0:T(8,128)(2,1)S(1)}, u32[]{:S(2)}, u32[]{:S(2)}) collective-permute-start(bf16[256,512]{1,0:T(8,128)(2,1)S(1)} %get-tuple-element.110.refs_2_.refs_1_), channel_id=1, source_target_pairs={{0,8},{4,12},{8,0},{12,4},{16,24},{20,28},{24,16},{28,20},{1,9},{5... | collective-permute-start | bytes 786440 | tf_op jit(solution)/shard_map/ppermute | solution.py:21
  179.0 17.8 %collective-permute-start.22 = (bf16[128,1024]{1,0:T(8,128)(2,1)S(1)}, bf16[128,1024]{1,0:T(8,128)(2,1)S(1)}, u32[]{:S(2)}, u32[]{:S(2)}) collective-permute-start(bf16[128,1024]{1,0:T(8,128)(2,1)S(1)} %get-tuple-element.108.refs_2_), channel_id=1, source_target_pairs={{0,16},{4,20},{8,24},{12,28},{16,0},{20,4},{24,8},{28,12},{1,17},{... | collective-permute-start | bytes 786440 | tf_op jit(solution)/shard_map/ppermute | solution.py:21
  187.5 11.9 %collective-permute-start.21 = (bf16[128,512]{1,0:T(8,128)(2,1)S(1)}, bf16[128,512]{1,0:T(8,128)(2,1)S(1)}, u32[]{:S(2)}, u32[]{:S(2)}) collective-permute-start(bf16[128,512]{1,0:T(8,128)(2,1)S(1)} %get-tuple-element.112.refs_4_), channel_id=1, source_target_pairs={{0,16},{4,20},{8,24},{12,28},{16,0},{20,4},{24,8},{28,12},{1,17},{... | collective-permute-start | bytes 393224 | tf_op jit(solution)/shard_map/ppermute | solution.py:21
  187.6 19.3 %collective-permute-start.28 = (bf16[8,7296]{1,0:T(8,128)(2,1)S(1)}, bf16[8,7296]{1,0:T(8,128)(2,1)S(1)}, u32[]{:S(2)}, u32[]{:S(2)}) collective-permute-start(bf16[8,7296]{1,0:T(8,128)(2,1)S(1)} %shard_map.171), channel_id=1, source_target_pairs={{0,16},{4,20},{8,24},{12,28},{16,0},{20,4},{24,8},{28,12},{1,17},{... | collective-permute-start | bytes 350216 | tf_op jit(solution)/shard_map/ppermute | solution.py:21
  201.6 20.4 %copy-start.28 = (s32[8]{0:T(128)S(1)}, s32[8]{0:T(128)}, u32[]{:S(2)}) copy-start(s32[8]{0:T(128)} %constant.81.clone) | copy-start | bytes 100
  202.9 12.9 %all-to-all-start = ((bf16[8,2,7296]{2,1,0:T(2,128)(2,1)}), bf16[8,2,7296]{2,1,0:T(2,128)(2,1)S(1)}, u32[]{:S(2)}, u32[]{:S(2)}) async-start(bf16[8,2,7296]{2,1,0:T(2,128)(2,1)} %reshape.64), calls=%async_computation | async-start | bytes 466944 | tf_op jit(solution)/shard_map/all_to_all | solution.py:347
  206.9 10.6 %collective-permute-start.29 = (bf16[16,7296]{1,0:T(8,128)(2,1)S(1)}, bf16[16,7296]{1,0:T(8,128)(2,1)S(1)}, u32[]{:S(2)}, u32[]{:S(2)}) collective-permute-start(bf16[16,7296]{1,0:T(8,128)(2,1)S(1)} %pad_maximum_fusion.9), channel_id=1, source_target_pairs={{0,8},{4,12},{8,0},{12,4},{16,24},{20,28},{24,16},{28,20},{1,9},{5... | collective-permute-start | bytes 700424 | tf_op jit(solution)/shard_map/ppermute | solution.py:21
  215.9 6.1 %collective-permute-start.23 = (bf16[16,7296]{1,0:T(8,128)(2,1)S(1)}, bf16[16,7296]{1,0:T(8,128)(2,1)S(1)}, u32[]{:S(2)}, u32[]{:S(2)}) collective-permute-start(bf16[16,7296]{1,0:T(8,128)(2,1)S(1)} %reshape.65.refs_0_), channel_id=1, source_target_pairs={{0,2},{1,3},{2,0},{3,1},{4,6},{5,7},{6,4},{7,5},{8,10},{9,11},{10,... | collective-permute-start | bytes 700424 | tf_op jit(solution)/shard_map/ppermute | solution.py:21
  217.5 21.0 %collective-permute-start.30 = (bf16[32,7296]{1,0:T(8,128)(2,1)S(1)}, bf16[32,7296]{1,0:T(8,128)(2,1)S(1)}, u32[]{:S(2)}, u32[]{:S(2)}) collective-permute-start(bf16[32,7296]{1,0:T(8,128)(2,1)S(1)} %pad_maximum_fusion.8), channel_id=1, source_target_pairs={{0,4},{4,0},{8,12},{12,8},{16,20},{20,16},{24,28},{28,24},{1,5},{5... | collective-permute-start | bytes 1400840 | tf_op jit(solution)/shard_map/ppermute | solution.py:21
  217.6 4.6 %collective-permute-start.24 = (bf16[16,7296]{1,0:T(8,128)(2,1)S(1)}, bf16[16,7296]{1,0:T(8,128)(2,1)S(1)}, u32[]{:S(2)}, u32[]{:S(2)}) collective-permute-start(bf16[16,7296]{1,0:T(8,128)(2,1)S(1)} %reshape.65.refs_0_), channel_id=1, source_target_pairs={{0,1},{1,0},{2,3},{3,2},{4,5},{5,4},{6,7},{7,6},{8,9},{9,8},{10,11... | collective-permute-start | bytes 700424 | tf_op jit(solution)/shard_map/ppermute | solution.py:21
  222.0 1.5 collective-permute-start.25
  238.4 3.6 %collective-permute-start.26 = (bf16[32,7168]{1,0:T(8,128)(2,1)S(1)}, bf16[32,7168]{1,0:T(8,128)(2,1)S(1)}, u32[]{:S(2)}, u32[]{:S(2)}) collective-permute-start(bf16[32,7168]{1,0:T(8,128)(2,1)S(1)} %get-tuple-element.119), channel_id=1, source_target_pairs={{0,1},{1,0},{2,3},{3,2},{4,5},{5,4},{6,7},{7,6},{8,9},{9,8},{10,11... | collective-permute-start | bytes 1376264 | tf_op jit(solution)/shard_map/ppermute | solution.py:21
  239.2 15.0 %copy-start.27 = (f32[256]{0:T(256)S(1)}, f32[256]{0:T(256)}, u32[]{:S(2)}) copy-start(f32[256]{0:T(256)} %param.16) | copy-start | bytes 3076
  239.2 1.3 collective-permute-start.31
  240.5 3.7 %collective-permute-start.32 = (f32[16,128]{1,0:T(8,128)S(1)}, f32[16,128]{1,0:T(8,128)S(1)}, u32[]{:S(2)}, u32[]{:S(2)}) collective-permute-start(f32[16,128]{1,0:T(8,128)S(1)} %slice.42), channel_id=1, source_target_pairs={{0,2},{1,3},{2,0},{3,1},{4,6},{5,7},{6,4},{7,5},{8,10},{9,11},{10,... | collective-permute-start | bytes 24584 | tf_op jit(solution)/shard_map/ppermute | solution.py:21
  242.0 22.1 %copy-start.1 = (bf16[7168,32]{0,1:T(8,128)(2,1)S(1)}, bf16[7168,32]{0,1:T(8,128)(2,1)}, u32[]{:S(2)}) copy-start(bf16[7168,32]{0,1:T(8,128)(2,1)} %param.15) | copy-start | bytes 1376260
  242.1 7.6 %collective-permute-start.27 = (bf16[16,7168]{1,0:T(8,128)(2,1)S(1)}, bf16[16,7168]{1,0:T(8,128)(2,1)S(1)}, u32[]{:S(2)}, u32[]{:S(2)}) collective-permute-start(bf16[16,7168]{1,0:T(8,128)(2,1)S(1)} %get-tuple-element.121), channel_id=1, source_target_pairs={{0,2},{1,3},{2,0},{3,1},{4,6},{5,7},{6,4},{7,5},{8,10},{9,11},{10,... | collective-permute-start | bytes 688136 | tf_op jit(solution)/shard_map/ppermute | solution.py:21
  250.7 11.4 %all-to-all-start.1 = ((bf16[8,2,7168]{2,1,0:T(2,128)(2,1)}), bf16[8,2,7168]{2,1,0:T(2,128)(2,1)S(1)}, u32[]{:S(2)}, u32[]{:S(2)}) async-start(bf16[8,2,7168]{2,1,0:T(2,128)(2,1)} %reshape.66), calls=%async_computation.1 | async-start | bytes 458752 | tf_op jit(solution)/shard_map/all_to_all | solution.py:462
  (16 other events, 48.1 us)
